TPU v7x, 32 devices: a whole 2x2x4 slice. The times are simulated.
32 devices in a mesh: seq: 8 (over z, y), head: 4 (over x, core).
Axes of the slice: x: 2, y: 2, z: 4, core: 2. Of those that a mesh axis runs over, the one named last changes fastest.
Arguments:
- features: bfloat16 [1024, 1024], P('seq'), may hold values from -6 to 6
- w_in: bfloat16 [1024, 1024], P(None, 'head'), may hold values from -0.1875 to 0.1875
- b_ahead: bfloat16 [1024, 128], P('seq'), may hold values from -6 to 6
- c_ahead: bfloat16 [1024, 128], P('seq'), may hold values from -0.015625 to 0.015625
- b_behind: bfloat16 [1024, 128], P('seq'), may hold values from -6 to 6
- c_behind: bfloat16 [1024, 128], P('seq'), may hold values from -0.015625 to 0.015625
- decay_ahead: float32 [16, 1024], P('head', 'seq'), may hold values from -2 to 0, as said below
- decay_behind: float32 [16, 1024], P('head', 'seq'), may hold values from -2 to 0, as said below
- skip_gain: float32 [16], P('head'), may hold values from 0.5 to 1.5
- grad_y: bfloat16 [1024, 1024], P('seq', 'head'), may hold values from -6 to 6
Outputs:
- grad_features: bfloat16 [1024, 1024], P('seq', 'head')
- grad_w_in: float32 [1024, 1024], P('seq', 'head')
- grad_b_ahead: float32 [1024, 128], P('seq')
- grad_c_ahead: float32 [1024, 128], P('seq')
- grad_b_behind: float32 [1024, 128], P('seq')
- grad_c_behind: float32 [1024, 128], P('seq')
- grad_decay_ahead: float32 [16, 1024], P('head', 'seq')
- grad_decay_behind: float32 [16, 1024], P('head', 'seq')
Inputs may be any that keep to these rules, and one draw needn't show every extreme that they name: `decay_ahead`: every log-decay is negative. `decay_behind`: every log-decay is negative.
All inputs are finite; a program needn't handle non-finite values.
Results may differ from a plain program's by a relative error of at most 0.039.
Values may be sent and summed in bfloat16 or wider, within the bound.
No kernel may reach another device: no remote copies, remote signals or barrier semaphores. Data moves between devices by JAX's collectives and lax.ppermute only.
A program may use at most 128 MiB of HBM per device.

v0:
```python
import math

import jax
import jax.numpy as jnp
from jax import lax
from jax.sharding import PartitionSpec as P

SPAN = 128


HIGH = lax.Precision.HIGHEST


def prefix(x, axis, combine, identity, reverse):
    peers, index = (lax.axis_size(axis), lax.axis_index(axis))
    everything = jax.tree.map(
        lambda part, kind: lax.all_gather(part.astype(kind), axis), x, (jnp.bfloat16, jnp.bfloat16)
    )
    start = jax.tree.map(
        lambda part, zero: jnp.broadcast_to(jnp.asarray(zero, part.dtype), part.shape), x, identity
    )

    def hop(k, before):
        at = peers - 1 - k if reverse else k
        reached = at > index if reverse else at < index
        new = combine(
            before, jax.tree.map(lambda part, own: part[at].astype(own.dtype), everything, x)
        )
        return jax.tree.map(lambda a, b: jnp.where(reached, a, b), new, before)

    return lax.fori_loop(0, peers, hop, start)


def block_step(states, inputs):
    signal, b_proj, c_proj, log_decay = inputs
    length = log_decay.shape[1]
    signal_low = signal.astype(jnp.bfloat16)
    b_low = b_proj.astype(jnp.bfloat16)
    c_low = c_proj.astype(jnp.bfloat16)
    cumulative = jnp.cumsum(log_decay, axis=1)
    row_index = lax.broadcasted_iota(jnp.int32, (length, length), 0)
    col_index = lax.broadcasted_iota(jnp.int32, (length, length), 1)
    causal = (col_index <= row_index)[None]
    spread = cumulative[:, :, None] - cumulative[:, None, :]
    decays = jnp.where(causal, jnp.exp(jnp.where(causal, spread, 0.0)), 0.0)
    affinity = jnp.dot(c_low, b_low.T, preferred_element_type=jnp.float32)
    scores = (decays * affinity[None]).astype(jnp.bfloat16)
    within = jnp.einsum("hts,shp->thp", scores, signal_low, preferred_element_type=jnp.float32)
    carried = jnp.exp(cumulative).T[:, :, None] * jnp.einsum(
        "tn,hpn->thp", c_proj, states, precision=HIGH
    )
    final_log = cumulative[:, -1:]
    weighted = (signal * jnp.exp(final_log - cumulative).T[:, :, None]).astype(jnp.bfloat16)
    fresh = jnp.einsum("shp,sn->hpn", weighted, b_low, preferred_element_type=jnp.float32)
    return (jnp.exp(final_log)[:, :, None] * states + fresh, within + carried)


def local_pass(signal, b_proj, c_proj, log_decay):
    length = SPAN
    blocks = signal.shape[0] // length
    heads = signal.shape[1]
    signal_blocks = signal.reshape(blocks, length, heads, signal.shape[2])
    b_blocks = b_proj.reshape(blocks, length, b_proj.shape[1])
    c_blocks = c_proj.reshape(blocks, length, c_proj.shape[1])
    decay_blocks = log_decay.reshape(heads, blocks, length).transpose(1, 0, 2)
    init = jnp.zeros((heads, signal.shape[2], b_proj.shape[1]), jnp.float32)
    summary, outputs = lax.scan(block_step, init, (signal_blocks, b_blocks, c_blocks, decay_blocks))
    return (outputs.reshape(signal.shape), summary)


def carry_pass(c_proj, log_decay, state_in):
    growth = jnp.exp(jnp.cumsum(log_decay, axis=1))
    output = growth.T[:, :, None] * jnp.einsum("tn,hpn->thp", c_proj, state_in, precision=HIGH)
    return (output, growth[:, -1][:, None, None] * state_in)


def prepare(signal, b_proj, c_proj, log_decay, cotangent):
    (_, summary), pull_local = jax.vjp(local_pass, signal, b_proj, c_proj, log_decay)
    growth = jnp.exp(jnp.cumsum(log_decay, axis=1))
    state_grad = jnp.einsum("thp,tn->hpn", cotangent * growth.T[:, :, None], c_proj, precision=HIGH)
    log_gain = jnp.sum(log_decay, axis=1)
    return (pull_local, log_gain, summary, state_grad)


def finish(pull_local, c_proj, log_decay, cotangent, state_in, grad_out):
    grad_sig, grad_b, grad_c, grad_d = pull_local((cotangent, grad_out))

    def carry_only(c_value, d_value):
        return carry_pass(c_value, d_value, state_in)

    _, pull_carry = jax.vjp(carry_only, c_proj, log_decay)
    extra_c, extra_d = pull_carry((cotangent, grad_out))
    return (grad_sig, grad_b, grad_c + extra_c, grad_d + extra_d)


def combine(earlier, later):
    return (earlier[0] + later[0], jnp.exp(later[0])[:, None, None] * earlier[1] + later[1])


def local(
    features,
    w_in,
    b_ahead,
    c_ahead,
    b_behind,
    c_behind,
    decay_ahead,
    decay_behind,
    skip_gain,
    grad_y,
):
    frames_dev = features.shape[0]
    heads_dev = decay_ahead.shape[0]
    head_size = w_in.shape[1] // heads_dev
    x_proj = jnp.dot(features, w_in, preferred_element_type=jnp.float32).astype(jnp.bfloat16)
    signal = x_proj.astype(jnp.float32).reshape(frames_dev, heads_dev, head_size)
    cotangent = grad_y.astype(jnp.float32).reshape(frames_dev, heads_dev, head_size)
    b_fore = b_ahead.astype(jnp.float32)
    c_fore = c_ahead.astype(jnp.float32)
    b_back = jnp.flip(b_behind.astype(jnp.float32), 0)
    c_back = jnp.flip(c_behind.astype(jnp.float32), 0)
    d_back = jnp.flip(decay_behind, 1)
    signal_back = jnp.flip(signal, 0)
    cotan_back = jnp.flip(cotangent, 0)
    pull_fore, gain_fore, summ_fore, sgrad_fore = prepare(
        signal, b_fore, c_fore, decay_ahead, cotangent
    )
    pull_back, gain_back, summ_back, sgrad_back = prepare(
        signal_back, b_back, c_back, d_back, cotan_back
    )
    zero_gain = jnp.zeros_like(gain_fore)
    zero_state = jnp.zeros_like(summ_fore)
    identity = (zero_gain, zero_state)
    state_fore = prefix((gain_fore, summ_fore), "seq", combine, identity, False)[1]
    grad_fore = prefix((gain_fore, sgrad_fore), "seq", combine, identity, True)[1]
    state_back = prefix((gain_back, summ_back), "seq", combine, identity, True)[1]
    grad_back = prefix((gain_back, sgrad_back), "seq", combine, identity, False)[1]
    gx_fore, gb_fore, gc_fore, gd_fore = finish(
        pull_fore, c_fore, decay_ahead, cotangent, state_fore, grad_fore
    )
    gx_back, gb_back, gc_back, gd_back = finish(
        pull_back, c_back, d_back, cotan_back, state_back, grad_back
    )
    grad_x = gx_fore + jnp.flip(gx_back, 0) + skip_gain[None, :, None] * cotangent
    grad_x = grad_x.astype(jnp.bfloat16).reshape(frames_dev, heads_dev * head_size)
    summed = (
        lax.psum(gb_fore.astype(jnp.bfloat16), "head").astype(jnp.float32),
        lax.psum(gc_fore.astype(jnp.bfloat16), "head").astype(jnp.float32),
        lax.psum(jnp.flip(gb_back, 0).astype(jnp.bfloat16), "head").astype(jnp.float32),
        lax.psum(jnp.flip(gc_back, 0).astype(jnp.bfloat16), "head").astype(jnp.float32),
    )
    partial_terms = lax.dot_general(
        grad_x, w_in, (((1,), (1,)), ((), ())), preferred_element_type=jnp.float32
    )
    grad_features = lax.psum_scatter(
        partial_terms.astype(jnp.bfloat16), "head", scatter_dimension=1, tiled=True
    )
    frames_all = frames_dev * lax.axis_size("seq")
    weight_sum = lax.psum_scatter(
        lax.dot_general(
            features, grad_x, (((0,), (0,)), ((), ())), preferred_element_type=jnp.float32
        ),
        "seq",
        scatter_dimension=0,
        tiled=True,
    )
    grad_w_in = weight_sum * (1.0 / math.sqrt(frames_all))
    return (
        grad_features,
        grad_w_in,
        summed[0],
        summed[1],
        summed[2],
        summed[3],
        gd_fore,
        jnp.flip(gd_back, 1),
    )


def solution(mesh):
    in_specs = (
        P("seq", None),
        P(None, "head"),
        P("seq", None),
        P("seq", None),
        P("seq", None),
        P("seq", None),
        P("head", "seq"),
        P("head", "seq"),
        P("head"),
        P("seq", "head"),
    )
    out_specs = (
        P("seq", "head"),
        P("seq", "head"),
        P("seq", None),
        P("seq", None),
        P("seq", None),
        P("seq", None),
        P("head", "seq"),
        P("head", "seq"),
    )
    return jax.shard_map(local, mesh=mesh, in_specs=in_specs, out_specs=out_specs, check_vma=False)
```

profile of v0, /device:TPU:0, one launch (start us, length us, event | category | flops | bytes accessed | tf_op | source)
XLA Modules:
  0.0 273.8 jit_solution(11693340548982521189)
XLA Ops:
  9.5 0.8 reduce_sum.292
  10.3 1.0 reduce_window_sum.65
  12.7 33.0 %all-gather.3 = bf16[32,64,128]{2,1,0:T(8,128)(2,1)S(1)} all-gather(bf16[4,64,128]{2,1,0:T(8,128)(2,1)S(1)} %convolution_convert_fusion.6), channel_id=5, replica_groups=mesh['seq'=8,'head'=4] {'seq'}, dimensions={0}, use_global_device_ids=true | all-gather | bytes 589824 | tf_op jit(solution)/shard_map/all_gather | solution.py:17
  48.1 21.6 %all-reduce.6 = (bf16[32]{0:T(256)(128)(2,1)S(1)}, bf16[32]{0:T(256)(128)(2,1)S(1)}) all-reduce(bf16[32]{0:T(256)(128)(2,1)S(1)} %dynamic-update-slice.1, bf16[32]{0:T(256)(128)(2,1)S(1)} %dynamic-update-slice), channel_id=4, replica_groups=mesh['seq'=8,'head'=4] {'seq'}, use_global_device_ids=true, to_apply=%add.5 | all-reduce | flops 64 | bytes 256
  69.7 1.0 while.49
  72.8 31.7 %all-gather.5 = bf16[32,64,128]{2,1,0:T(8,128)(2,1)S(1)} all-gather(bf16[4,64,128]{2,1,0:T(8,128)(2,1)S(1)} %fusion.14), channel_id=7, replica_groups=mesh['seq'=8,'head'=4] {'seq'}, dimensions={0}, use_global_device_ids=true | all-gather | bytes 589824 | tf_op jit(solution)/shard_map/all_gather | solution.py:17
  104.5 1.1 while.51
  106.7 31.4 %all-gather.1 = bf16[32,64,128]{2,1,0:T(8,128)(2,1)S(1)} all-gather(bf16[4,64,128]{2,1,0:T(8,128)(2,1)S(1)} %convolution_convert_fusion.9), channel_id=3, replica_groups=mesh['seq'=8,'head'=4] {'seq'}, dimensions={0}, use_global_device_ids=true | all-gather | bytes 589824 | tf_op jit(solution)/shard_map/all_gather | solution.py:17
  138.2 1.1 while.48
  140.3 31.2 %all-gather.4 = bf16[32,64,128]{2,1,0:T(8,128)(2,1)S(1)} all-gather(bf16[4,64,128]{2,1,0:T(8,128)(2,1)S(1)} %fusion.13), channel_id=6, replica_groups=mesh['seq'=8,'head'=4] {'seq'}, dimensions={0}, use_global_device_ids=true | all-gather | bytes 589824 | tf_op jit(solution)/shard_map/all_gather | solution.py:17
  171.5 1.0 while.50
  178.2 1.0 fusion.38
  179.3 1.3 convolution_bitcast_fusion
  180.8 1.0 convolution_convert_fusion
  183.4 1.3 reduce_window_sum.69
  184.7 1.3 reduce_window_sum.70
  187.3 1.3 reduce_window_sum.67
  188.6 1.3 reduce_window_sum.68
  190.4 17.7 %all-reduce.10.cloned.1.call-done = (bf16[128,128]{1,0:T(8,128)(2,1)}, bf16[128,128]{1,0:T(8,128)(2,1)}, bf16[128,128]{1,0:T(8,128)(2,1)}, bf16[128,128]{1,0:T(8,128)(2,1)}) async-done(((bf16[128,128]{1,0:T(8,128)(2,1)}, bf16[128,128]{1,0:T(8,128)(2,1)}, bf16[128,128]{1,0:T(8,128)(2,1)}, bf16[128,128]{1,0:T(8,128)(2,1)}), (bf16[128,128]{1,0:T(8,128)(2,1)}, bf16[128,128]{1,0:T(8,128)(2,1)}, ...) | async-done | bytes 131088 | tf_op jit(solution)/shard_map/psum | solution.py:147
  208.1 1.4 convert_element_type.583
  211.7 32.6 %reduce-scatter.5.cloned.1.call-done = f32[128,256]{0,1:T(8,128)} async-done(((f32[1024,256]{0,1:T(8,128)}), f32[128,256]{0,1:T(8,128)}) %reduce-scatter.5.cloned.1.call-update) | async-done | bytes 131088 | tf_op jit(solution)/shard_map/reduce_scatter | solution.py:159
  244.3 0.9 broadcast_multiply_fusion
  245.2 0.8 copy.68
  246.0 20.4 %reduce-scatter.3.cloned.1.call-done = bf16[128,256]{1,0:T(8,128)(2,1)} async-done(((bf16[128,1024]{1,0:T(8,128)(2,1)}), bf16[128,256]{1,0:T(8,128)(2,1)}) %reduce-scatter.3.cloned.1.call-update) | async-done | bytes 65552 | tf_op jit(solution)/shard_map/reduce_scatter | solution.py:155
  (177 shorter events, 23.4 us)
Async XLA Ops:
  8.0 62.7 %copy-start = (bf16[1024,256]{1,0:T(8,128)(2,1)S(1)}, bf16[1024,256]{1,0:T(8,128)(2,1)}, u32[]{:S(2)}) copy-start(bf16[1024,256]{1,0:T(8,128)(2,1)} %param.19) | copy-start | bytes 1572868
  8.0 0.7 copy-start.10
  8.0 3.5 %copy-start.4 = (bf16[128,256]{1,0:T(8,128)(2,1)S(1)}, bf16[128,256]{1,0:T(8,128)(2,1)}, u32[]{:S(2)}) copy-start(bf16[128,256]{1,0:T(8,128)(2,1)} %param.27) | copy-start | bytes 196612
  8.0 200.1 %all-reduce.10.cloned.1.call-start = ((), (), s32[]{:S(2)}) async-start(), calls=%async_computation.4 | async-start | bytes 262144 | tf_op jit(solution)/shard_map/psum | solution.py:147
  11.6 0.8 copy-start.5
  45.7 0.7 copy-start.12
  69.7 1.0 copy-start.1
  71.1 0.8 copy-start.9
  105.6 0.8 copy-start.2
  105.6 0.8 copy-start.3
  172.8 0.7 copy-start.11
  179.2 65.1 %reduce-scatter.5.cloned.1.call-start = ((), (), s32[]{:S(2)}) async-start(), calls=%async_computation.3 | async-start | bytes 1179648 | tf_op jit(solution)/shard_map/reduce_scatter | solution.py:159
  180.6 85.8 %reduce-scatter.3.cloned.1.call-start = ((), (), s32[]{:S(2)}) async-start(), calls=%async_computation.2 | async-start | bytes 327680 | tf_op jit(solution)/shard_map/reduce_scatter | solution.py:155
  208.1 1.4 copy-start.8
  209.5 0.8 copy-start.7
  210.3 0.8 copy-start.6
Sparse Core Ops, SparseCore 0:
  179.4 28.7 all-reduce.9
Sparse Core Ops, SparseCore 1:
  183.1 61.1 reduce-scatter.4
  247.3 19.0 reduce-scatter.2
where the time goes:
time: 275 us; the launch traced here: 274 us
  blocking collectives  149 us (54%)
  waiting for transfers between devices  70.8 us (26%)
  other arithmetic  16.7 us (6%)
  between operations  16.5 us (6%)
  matrix products  10.2 us (4%)
  local copies, waits for them, and re-layouts  9.47 us (3%)
    all_gather x4, blocking collectives, prefix(): lax.all_gather(part.astype(kind), axis)  127 us
    reduce_scatter x1, waiting for transfers between devices, local(): lax.psum_scatter(lax.dot_general(features, grad_x, (((0,), (0,)), ((), ()...  32.6 us
    unnamed x1, blocking collectives  21.6 us
    reduce_scatter x1, waiting for transfers between devices, local(): lax.psum_scatter(partial_terms.astype(jnp.bfloat16), 'head', scatter_dime...  20.4 us
    psum x1, waiting for transfers between devices, local(): lax.psum(gb_fore.astype(jnp.bfloat16), 'head').astype(jnp.float32)  17.7 us
    unnamed x33, local copies, waits for them, and re-layouts  5.91 us
  transfers between devices with their start and end apart: 3, of which 3 were waited for; matrix products, arithmetic and copies ran while one was open for 6% of the time, Pallas kernels for 0%

commit v1 on v0

v1 whole, which is shorter than its diff:
```python
import functools
import math

import jax
import jax.numpy as jnp
from jax import lax
from jax.experimental import pallas as pl
from jax.experimental.pallas import tpu as pltpu
from jax.sharding import PartitionSpec as P

F32 = jnp.float32
BF16 = jnp.bfloat16
HIGH = lax.Precision.HIGHEST
GAIN_ROWS = 16
DIRECT_PEERS = 8


def nn(a, b, **kw):
    return lax.dot_general(a, b, (((1,), (0,)), ((), ())), preferred_element_type=F32, **kw)


def nt(a, b, **kw):
    return lax.dot_general(a, b, (((1,), (1,)), ((), ())), preferred_element_type=F32, **kw)


def iotas(rows, cols):
    return (
        lax.broadcasted_iota(jnp.int32, (rows, cols), 0),
        lax.broadcasted_iota(jnp.int32, (rows, cols), 1),
    )


def spread_rows(values, width):
    heads, length = values.shape
    return jnp.concatenate(
        [jnp.broadcast_to(values[h : h + 1], (width, length)) for h in range(heads)], axis=0
    )


def split3(value):
    high = value.astype(BF16)
    rest = value - high.astype(F32)
    middle = rest.astype(BF16)
    low = (rest - middle.astype(F32)).astype(BF16)
    return high, middle, low


def masked_sums(masks, values):
    masks = masks.astype(BF16)
    return sum(nt(masks, part) for part in split3(values))


def decay_factors(d_ahead, d_behind, width):
    length = d_ahead.shape[1]
    row, col = iotas(length, length)
    upto = (col <= row).astype(F32)
    since = (col >= row).astype(F32)
    ahead = masked_sums(
        jnp.concatenate([upto, 1.0 - upto], axis=0), spread_rows(d_ahead, width)
    )
    behind = masked_sums(
        jnp.concatenate([since, 1.0 - since], axis=0), spread_rows(d_behind, width)
    )
    ahead, behind = jnp.exp(ahead), jnp.exp(behind)
    return ahead[:length], ahead[length:], behind[:length], behind[length:]


def radices(peers):
    bits = peers.bit_length() - 1
    return ([2] if bits % 2 else []) + [4] * (bits // 2)


def digit(index, stride, radix):
    return lax.rem(lax.div(index, stride), radix)


def read_gains(block):
    rows = block.astype(F32)
    return (
        rows[0:1] + rows[1:2] + rows[2:3],
        rows[3:4] + rows[4:5] + rows[5:6],
    )


def gain_block(gains):
    width = gains[0].shape[1]
    parts = [p for g in gains for p in split3(g)]
    rows = [p.astype(F32) for p in parts]
    pad = jnp.zeros((GAIN_ROWS - len(rows), width), F32)
    return jnp.concatenate(rows + [pad], axis=0).astype(BF16)


def product_where(conditions, gains):
    result = jnp.ones_like(gains[0])
    for condition, gain in zip(conditions, gains):
        result = jnp.where(condition, result * gain, result)
    return result


def merge_coefficients(me, members, gains):
    below, above = [], []
    zero = jnp.zeros_like(gains[0])
    others = range(1, len(members))
    for j in others:
        q = members[j]
        low = product_where(
            [jnp.logical_and(members[i] > q, members[i] < me) for i in others], [gains[i] for i in others]
        )
        high = product_where(
            [jnp.logical_and(members[i] < q, members[i] > me) for i in others], [gains[i] for i in others]
        )
        below.append(jnp.where(q < me, low, zero))
        above.append(jnp.where(q > me, high, zero))
    return below, above


def write_payloads(out_refs, totals, gains, me, last):
    n = totals[0].shape[0]
    block = gain_block(gains)
    rounded = [t.astype(BF16) for t in totals]
    if not last:
        for k in range(4):
            out_refs[0][k * n : (k + 1) * n] = rounded[k]
        out_refs[0][4 * n :] = block
        return
    for j, ref in enumerate(out_refs, start=1):
        up = (me ^ j) > me
        ref[0:n] = jnp.where(up, rounded[0], rounded[2])
        ref[n : 2 * n] = jnp.where(up, rounded[1], rounded[3])
        ref[2 * n :] = block


def front_kernel(me, last, peers_out, features, w_in, gy, ba, ca, bb, cb, da, db, x_out, own_out, *sends):
    width = w_in.shape[1] // da.shape[0]
    x = nn(features[...], w_in[...]).astype(BF16)
    x_out[...] = x
    grow_a, left_a, grow_b, left_b = decay_factors(da[...], db[...], width)
    xf, gyf = x.astype(F32), gy[...].astype(F32)
    length = x.shape[0]
    up0 = nn(ba[...].T, (xf * left_a).astype(BF16))
    up1 = nn(cb[...].T, (gyf * grow_b).astype(BF16))
    down0 = nn(ca[...].T, (gyf * grow_a).astype(BF16))
    down1 = nn(bb[...].T, (xf * left_b).astype(BF16))
    gains = (grow_a[length - 1 : length], grow_b[0:1])
    totals = (up0, up1, down0, down1)
    write_payloads([own_out], totals, gains, None, False)
    if last:
        write_payloads(sends, totals, gains, me(), True)


def load_member(ref, n):
    return [ref[k * n : (k + 1) * n].astype(F32) for k in range(4)], read_gains(ref[4 * n :])


def step_kernel(index, stride, radix, first, next_last, next_radix, *refs):
    refs = list(refs)
    own = refs.pop(0)
    received = [refs.pop(0) for _ in range(radix - 1)]
    before = None if first else refs.pop(0)
    pre_out, own_out = refs.pop(0), refs.pop(0)
    n = (own.shape[0] - GAIN_ROWS) // 4
    seq = index()
    me = digit(seq, stride, radix)
    members = [me ^ j for j in range(radix)]
    loaded = [load_member(ref, n) for ref in [own] + received]
    gains = [[l[1][d] for l in loaded] for d in range(2)]
    coefficients = [merge_coefficients(me, members, gains[d]) for d in range(2)]
    width = own.shape[1]
    one = jnp.ones((1, width), F32)
    grow = [one] * 4 if first else [before[4 * n + k : 4 * n + k + 1] for k in range(4)]
    new_grow = []
    totals = []
    for k in range(4):
        d, down = k % 2, k // 2
        total = sum(coefficients[d][down][j - 1] * loaded[j][0][k] for j in range(1, radix))
        if not first:
            total = grow[k] * total + before[k * n : (k + 1) * n]
        pre_out[k * n : (k + 1) * n] = total
        inside = [(members[j] > me) if down else (members[j] < me) for j in range(1, radix)]
        new_grow.append(product_where(inside, gains[d][1:]) * grow[k])
        group = 0.0
        for j in range(radix):
            outer = [
                (members[i] < members[j]) if down else (members[i] > members[j])
                for i in range(radix)
                if i != j
            ]
            others = [gains[d][i] for i in range(radix) if i != j]
            group = group + product_where(outer, others) * loaded[j][0][k]
        totals.append(group)
    pre_out[4 * n :] = jnp.concatenate(new_grow + [jnp.zeros((4, width), F32)], axis=0)
    new_gains = tuple(functools.reduce(lambda a, b: a * b, gains[d]) for d in range(2))
    write_payloads([own_out], totals, new_gains, None, False)
    if next_last:
        write_payloads(refs, totals, new_gains, digit(seq, stride * radix, next_radix), True)


def local_kernel(
    skip, x, gy, features, ba, ca, bb, cb, da, db, gx_out, maps_out, decay_out, factors_out, turned_out
):
    heads, length = da.shape
    width = x.shape[1] // heads
    n = ba.shape[1]
    factors = decay_factors(da[...], db[...], width)
    for k in range(4):
        factors_out[k] = factors[k]
    row, col = iotas(length, length)
    upto = (col <= row).astype(F32)
    since = (col >= row).astype(F32)
    pad = jnp.zeros((8 - heads, length), F32)
    d_ahead = jnp.concatenate([da[...], pad], axis=0)
    d_behind = jnp.concatenate([db[...], pad], axis=0)
    columns_a = masked_sums(upto, d_ahead)
    columns_b = masked_sums(since, d_behind)
    rows_a = columns_a.T
    rows_b = columns_b.T
    later, same = col > row, col == row
    raw_a = nt(ba[...], ca[...])
    raw_b = nt(bb[...], cb[...])
    affinity = jnp.where(same, raw_a + raw_b, jnp.where(later, raw_a, raw_b))
    weight_sum = jnp.zeros((length, length), F32)
    counts = jnp.concatenate([since.T, upto.T], axis=1).astype(BF16)
    cross = jnp.concatenate([row < col, row > col], axis=1).astype(F32)
    totals = []
    for h in range(heads):
        part = slice(h * width, (h + 1) * width)
        gap = jnp.where(
            later,
            rows_a[h : h + 1] - columns_a[:, h : h + 1],
            rows_b[h : h + 1] - columns_b[:, h : h + 1],
        )
        decay = jnp.exp(jnp.where(same, 0.0, gap))
        score_grad = nt(x[:, part], gy[:, part])
        weighted = score_grad * decay
        weight_sum = weight_sum + weighted
        gx_out[:, part] = nn((decay * affinity).astype(BF16), gy[:, part]) + skip[h] * gy[:, part].astype(F32)
        pieces = nn((weighted * affinity).astype(BF16), counts)
        totals.append(jnp.sum(pieces * cross, axis=0, keepdims=True))
    for h in range(heads):
        decay_out[h : h + 1] = totals[h]
    ahead = jnp.where(col >= row, weight_sum, 0.0).astype(BF16)
    behind = jnp.where(col <= row, weight_sum, 0.0).astype(BF16)
    maps_out[:, 0:n] = nn(ahead, ca[...])
    maps_out[:, n : 2 * n] = nn(ahead.T, ba[...])
    maps_out[:, 2 * n : 3 * n] = nn(behind, cb[...])
    maps_out[:, 3 * n :] = nn(behind.T, bb[...])
    turned_out[...] = features[...].T


def carry_kernel(index, radix, stride, first, direct, n_head, *refs):
    refs = list(refs)
    own = refs.pop(0)
    received = [refs.pop(0) for _ in range(radix - 1)]
    before = None if first else refs.pop(0)
    x, gy, turned, w_in, ba, ca, bb, cb = [refs.pop(0) for _ in range(8)]
    gx_local, maps_local, decay_local, factors = [refs.pop(0) for _ in range(4)]
    heads = decay_local.shape[0]
    n = ba.shape[1]
    length, columns = x.shape
    width = columns // heads
    seq, head = index()

    me = digit(seq, stride, radix)
    members = [me ^ j for j in range(radix)]
    gains = [[], []]
    for ref, at in [(own, 4 * n)] + [(r, 2 * n) for r in received]:
        for d, gain in enumerate(read_gains(ref[at:])):
            gains[d].append(gain)
    states = [None] * 4
    for d in range(2):
        coefficients = merge_coefficients(me, members, gains[d])
        for down in range(2):
            k = 2 * down + d
            total = jnp.zeros((n, columns), F32)
            for j, ref in enumerate(received):
                total = total + coefficients[down][j] * ref[d * n : (d + 1) * n].astype(F32)
            if not first:
                total = before[4 * n + k : 4 * n + k + 1] * total + before[k * n : (k + 1) * n]
            states[k] = total
    state_a, grad_b, grad_a, state_b = states

    grow_a, left_a, grow_b, left_b = [factors[k] for k in range(4)]
    xf, gyf = x[...].astype(F32), gy[...].astype(F32)
    row, col = iotas(length, length)
    own_rows, own_cols = iotas(8, columns)
    group = (lax.div(own_cols, width) == own_rows).astype(BF16)
    frame = lax.broadcasted_iota(jnp.int32, (length, 1), 0)

    def direction(state, grad, grow, left, b, c, at_end, later, earlier):
        gain = jnp.sum(jnp.where(frame == at_end, grow, 0.0), axis=0, keepdims=True)
        state_low, grad_low = state.astype(BF16), grad.astype(BF16)
        carried = grow * nn(c[...], state_low)
        through = gain * jnp.sum(state * grad, axis=0, keepdims=True)
        read = gyf * carried + jnp.where(frame == at_end, through, 0.0)
        grad_x = nn(b[...], grad_low).astype(BF16).astype(F32) * left
        write = grad_x * xf
        reads = nt(group, read.astype(BF16))
        writes = nt(group, write.astype(BF16))
        grad_decay = nn(reads, later, precision=HIGH) + nn(writes, earlier, precision=HIGH)
        grad_c = nt((gyf * grow).astype(BF16), state_low)
        grad_b = nt((xf * left).astype(BF16), grad_low)
        return grad_x, grad_b, grad_c, grad_decay

    gx_a, gb_a, gc_a, gd_a = direction(
        state_a, grad_a, grow_a, left_a, ba, ca, length - 1, (row >= col).astype(F32), (row < col).astype(F32)
    )
    gx_b, gb_b, gc_b, gd_b = direction(
        state_b, grad_b, grow_b, left_b, bb, cb, 0, (row <= col).astype(F32), (row > col).astype(F32)
    )
    gd_a_out, gd_b_out, own_out = refs.pop(0), refs.pop(0), refs.pop(0)
    gd_a_out[...] = gd_a[:heads] + decay_local[:, 0:length]
    gd_b_out[...] = gd_b[:heads] + decay_local[:, length:]
    grad_x = (gx_local[...] + gx_a + gx_b).astype(BF16)
    maps = maps_local[...] + jnp.concatenate([gb_a, gc_a, gb_b, gc_b], axis=1)
    maps_low = maps.astype(BF16)
    rows_out = w_in.shape[0] // n_head
    own_out[:, rows_out:] = maps
    for k in range(n_head):
        at = pl.multiple_of((head ^ k) * rows_out, rows_out)
        share = nt(grad_x, w_in[pl.ds(at, rows_out), :])
        if k == 0:
            own_out[:, 0:rows_out] = share
        else:
            ref = refs.pop(0)
            ref[:, 0:rows_out] = share.astype(BF16)
            ref[:, rows_out:] = maps_low
    if not direct:
        refs.pop(0)[...] = nn(turned[...], grad_x)
        return
    rows_w = turned.shape[0] // direct
    for k in range(direct):
        at = pl.multiple_of((seq ^ k) * rows_w, rows_w)
        share = nn(turned[pl.ds(at, rows_w), :], grad_x)
        ref = refs.pop(0)
        ref[...] = share.astype(ref.dtype)


def sum_kernel(n_head, direct, scale, *refs):
    refs = list(refs)
    own = refs.pop(0)
    others = [refs.pop(0) for _ in range(n_head - 1)]
    shares = [refs.pop(0) for _ in range(max(direct, 1))]
    gf_out, gw_out = refs.pop(0), refs.pop(0)
    columns = gf_out.shape[1]
    n = refs[0].shape[1]

    def total(part):
        return sum([other[:, part].astype(F32) for other in others], own[:, part])

    gf_out[...] = total(slice(0, columns)).astype(BF16)
    for k, ref in enumerate(refs):
        ref[...] = total(slice(columns + k * n, columns + (k + 1) * n))
    gw_out[...] = sum([share[...].astype(F32) for share in shares[1:]], shares[0][...]) * scale


def call(kernel, outs, *args, flops=0, scalars=0):
    specs = [pl.BlockSpec(memory_space=pltpu.SMEM)] * scalars
    specs += [pl.BlockSpec(memory_space=pltpu.VMEM)] * (len(args) - scalars)
    bytes_moved = sum(math.prod(a.shape) * a.dtype.itemsize for a in args)
    bytes_moved += sum(math.prod(o.shape) * o.dtype.itemsize for o in outs)
    return pl.pallas_call(
        kernel,
        out_shape=outs,
        in_specs=specs,
        out_specs=[pl.BlockSpec(memory_space=pltpu.VMEM)] * len(outs),
        cost_estimate=pl.CostEstimate(flops=flops, bytes_accessed=bytes_moved, transcendentals=0),
        compiler_params=pltpu.CompilerParams(vmem_limit_bytes=48 * 1024 * 1024),
    )(*args)


def swap(value, axis, mask):
    return lax.ppermute(value, axis, [(i, i ^ mask) for i in range(lax.axis_size(axis))])


def local(features, w_in, b_ahead, c_ahead, b_behind, c_behind, decay_ahead, decay_behind, skip_gain, grad_y):
    peers, n_head = lax.axis_size("seq"), lax.axis_size("head")
    length, depth = features.shape
    heads, columns = decay_ahead.shape[0], w_in.shape[1]
    n = b_ahead.shape[1]
    maps = (b_ahead, c_ahead, b_behind, c_behind)
    decays = (decay_ahead, decay_behind)
    seq_index = lambda: lax.axis_index("seq")
    both_index = lambda: (lax.axis_index("seq"), lax.axis_index("head"))
    shape = jax.ShapeDtypeStruct
    whole = shape((4 * n + GAIN_ROWS, columns), BF16)
    half = shape((2 * n + GAIN_ROWS, columns), BF16)
    prefix = shape((4 * n + 8, columns), F32)

    steps = radices(peers)
    only = len(steps) == 1
    x, own, *sends = call(
        functools.partial(front_kernel, seq_index, only, peers),
        [shape((length, columns), BF16), whole] + [half] * ((steps[0] - 1) if only else 0),
        features, w_in, grad_y, *maps, *decays,
        flops=2 * length * depth * columns,
    )
    gx_local, maps_local, decay_local, factors, turned = call(
        local_kernel,
        [
            shape((length, columns), F32),
            shape((length, 4 * n), F32),
            shape((heads, 2 * length), F32),
            shape((4, length, columns), F32),
            shape((depth, length), BF16),
        ],
        skip_gain, x, grad_y, features, *maps, *decays,
        flops=2 * length * depth * columns,
        scalars=1,
    )
    stride, before = 1, None
    for at, radix in enumerate(steps[:-1]):
        received = [swap(own, "seq", j * stride) for j in range(1, radix)]
        next_last = at == len(steps) - 2
        following = steps[at + 1]
        before, own, *sends = call(
            functools.partial(step_kernel, seq_index, stride, radix, at == 0, next_last, following),
            [prefix, whole] + [half] * ((following - 1) if next_last else 0),
            own, *received, *([] if at == 0 else [before]),
            flops=40 * n * columns,
        )
        stride *= radix
    received = [swap(send, "seq", j * stride) for j, send in enumerate(sends, start=1)]
    direct = peers if peers <= DIRECT_PEERS else 0
    rows_out = depth // n_head
    w_shapes = [shape((depth, columns), F32)]
    if direct:
        block = (depth // direct, columns)
        w_shapes = [shape(block, F32)] + [shape(block, BF16)] * (direct - 1)
    gd_ahead, gd_behind, own_share, *shares = call(
        functools.partial(carry_kernel, both_index, steps[-1], stride, only, direct, n_head),
        [shape((heads, length), F32)] * 2
        + [shape((length, rows_out + 4 * n), F32)]
        + [shape((length, rows_out + 4 * n), BF16)] * (n_head - 1)
        + w_shapes,
        own, *received, *([] if only else [before]),
        x, grad_y, turned, w_in, *maps, gx_local, maps_local, decay_local, factors,
        flops=6 * length * depth * columns,
    )
    head_shares, w_shares = shares[: n_head - 1], shares[n_head - 1 :]
    if direct:
        w_shares = w_shares[:1] + [swap(s, "seq", k) for k, s in enumerate(w_shares[1:], start=1)]
    else:
        w_shares = [lax.psum_scatter(w_shares[0], "seq", scatter_dimension=0, tiled=True)]
    head_shares = [swap(s, "head", k) for k, s in enumerate(head_shares, start=1)]
    grad_features, grad_w_in, *grad_maps = call(
        functools.partial(sum_kernel, n_head, direct, 1.0 / math.sqrt(length * peers)),
        [shape((length, rows_out), BF16), shape((depth // peers, columns), F32)]
        + [shape((length, n), F32)] * 4,
        own_share, *head_shares, *w_shares,
    )
    return (grad_features, grad_w_in, *grad_maps, gd_ahead, gd_behind)


def solution(mesh):
    in_specs = (
        P("seq", None),
        P(None, "head"),
        P("seq", None),
        P("seq", None),
        P("seq", None),
        P("seq", None),
        P("head", "seq"),
        P("head", "seq"),
        P("head"),
        P("seq", "head"),
    )
    out_specs = (
        P("seq", "head"),
        P("seq", "head"),
        P("seq", None),
        P("seq", None),
        P("seq", None),
        P("seq", None),
        P("head", "seq"),
        P("head", "seq"),
    )
    return jax.shard_map(local, mesh=mesh, in_specs=in_specs, out_specs=out_specs, check_vma=False)
```

time: 275 us -> 59.6 us (0.22)
  blocking collectives: 149 us -> 0 us
  waiting for transfers between devices: 70.8 us -> 24.3 us
  starting transfers between devices: 0.31 us -> 21.3 us
  other arithmetic: 16.7 us -> 0 us
  between operations: 16.5 us -> 0.8 us
  matrix products: 10.2 us -> 0 us
  Pallas kernels: 0 us -> 5.3 us
    all_gather x4 -> x0, blocking collectives: 127 us -> none  [prefix(): lax.all_gather(part.astype(kind), axis)]
    reduce_scatter x2 -> x0, waiting for transfers between devices: 53 us -> none  [the longest x1 32.6 us: local(): lax.psum_scatter(lax.dot_general(features, grad_x, (((0,), (0,)), ((), ()...]
    ppermute x0 -> x14, waiting for transfers between devices: none -> 24.3 us  [swap(): lax.ppermute(value, axis, [(i, i ^ mask) for i in range(lax.axis_size(axi...]
    unnamed x1 -> x0, blocking collectives: 21.6 us -> none
    ppermute x0 -> x14, starting transfers between devices: none -> 21.3 us  [swap(): lax.ppermute(value, axis, [(i, i ^ mask) for i in range(lax.axis_size(axi...]
    psum x1 -> x0, waiting for transfers between devices: 17.7 us -> none  [local(): lax.psum(gb_fore.astype(jnp.bfloat16), 'head').astype(jnp.float32)]
    dot_general x29 -> x0, matrix products: 10.2 us -> none  [the longest x4 1.94 us: block_step(): jnp.einsum('tn,hpn->thp', c_proj, states, precision=HIGH)]
    another operation x6 -> x0, other arithmetic: 6.35 us -> none  [the longest x2 2.54 us: block_step(): cumulative = jnp.cumsum(log_decay, axis=1)]
  transfers between devices with their start and end apart: 3 -> 14, of which waited for: 3 -> 7; matrix products, arithmetic and copies ran while one was open for 6% -> 0% of each run, Pallas kernels for 0% -> 3%
where the time goes in v1:
time: 59.6 us; the launch traced here: 59 us
  waiting for transfers between devices  24.3 us (41%)
  starting transfers between devices  21.3 us (36%)
  local copies, waits for them, and re-layouts  7.27 us (12%)
  Pallas kernels  5.3 us (9%)
  between operations  0.8 us (1%)
    ppermute x14, waiting for transfers between devices, swap(): lax.ppermute(value, axis, [(i, i ^ mask) for i in range(lax.axis_size(axi...  24.3 us
    ppermute x14, starting transfers between devices, swap(): lax.ppermute(value, axis, [(i, i ^ mask) for i in range(lax.axis_size(axi...  21.3 us
    unnamed x38, local copies, waits for them, and re-layouts  7.27 us
    pallas_call x5, Pallas kernels, call(): pl.pallas_call(kernel, out_shape=outs, in_specs=specs, out_specs=[pl.Bloc...  5.3 us
  transfers between devices with their start and end apart: 14, of which 7 were waited for; matrix products, arithmetic and copies ran while one was open for 0% of the time, Pallas kernels for 3%

profile of v1, /device:TPU:0, one launch (start us, length us, event | category | flops | bytes accessed | tf_op | source)
XLA Modules:
  0.0 59.0 jit_solution(2356855094669840634)
XLA Ops:
  0.6 1.0 %copy-done = bf16[1024,256]{1,0:T(8,128)(2,1)S(1)} copy-done((bf16[1024,256]{1,0:T(8,128)(2,1)S(1)}, bf16[1024,256]{1,0:T(8,128)(2,1)}, u32[]{:S(2)}) %copy-start) | copy-done | bytes 524312
  1.7 0.9 %copy-done.2 = bf16[128,1024]{1,0:T(8,128)(2,1)S(1)} copy-done((bf16[128,1024]{1,0:T(8,128)(2,1)S(1)}, bf16[128,1024]{1,0:T(8,128)(2,1)}, u32[]{:S(2)}) %copy-start.2) | copy-done | bytes 262168
  2.6 0.8 %copy-done.4 = bf16[128,256]{1,0:T(8,128)(2,1)S(1)} copy-done((bf16[128,256]{1,0:T(8,128)(2,1)S(1)}, bf16[128,256]{1,0:T(8,128)(2,1)}, u32[]{:S(2)}) %copy-start.4) | copy-done | bytes 65560
  3.5 0.8 %copy-done.6 = bf16[128,128]{1,0:T(8,128)(2,1)S(1)} copy-done((bf16[128,128]{1,0:T(8,128)(2,1)S(1)}, bf16[128,128]{1,0:T(8,128)(2,1)}, u32[]{:S(2)}) %copy-start.6) | copy-done | bytes 32792
  4.2 0.8 %copy-done.8 = bf16[128,128]{1,0:T(8,128)(2,1)S(1)} copy-done((bf16[128,128]{1,0:T(8,128)(2,1)S(1)}, bf16[128,128]{1,0:T(8,128)(2,1)}, u32[]{:S(2)}) %copy-start.8) | copy-done | bytes 32792
  5.0 0.8 %copy-done.10 = bf16[128,128]{1,0:T(8,128)(2,1)S(1)} copy-done((bf16[128,128]{1,0:T(8,128)(2,1)S(1)}, bf16[128,128]{1,0:T(8,128)(2,1)}, u32[]{:S(2)}) %copy-start.10) | copy-done | bytes 32792
  8.7 3.0 %collective-permute-start = (bf16[528,256]{1,0:T(8,128)(2,1)S(1)}, bf16[528,256]{1,0:T(8,128)(2,1)S(1)}, u32[]{:S(2)}, u32[]{:S(2)}) collective-permute-start(bf16[528,256]{1,0:T(8,128)(2,1)S(1)} %get-tuple-element.40.refs_0_), channel_id=1, source_target_pairs={{0,4},{4,0},{8,12},{12,8},{16,20},{20,16},{24,28},{28,24},{1,5},{5... | collective-permute-start | bytes 811016 | tf_op jit(solution)/shard_map/ppermute | solution.py:372
  11.7 6.5 %collective-permute-done.refs_1_ = bf16[528,256]{1,0:T(8,128)(2,1)S(1)} collective-permute-done((bf16[528,256]{1,0:T(8,128)(2,1)S(1)}, bf16[528,256]{1,0:T(8,128)(2,1)S(1)}, u32[]{:S(2)}, u32[]{:S(2)}) %collective-permute-start) | collective-permute-done | bytes 270368 | tf_op jit(solution)/shard_map/ppermute | solution.py:372
  18.4 1.9 %collective-permute-start.1 = (bf16[272,256]{1,0:T(8,128)(2,1)S(1)}, bf16[272,256]{1,0:T(8,128)(2,1)S(1)}, u32[]{:S(2)}, u32[]{:S(2)}) collective-permute-start(bf16[272,256]{1,0:T(8,128)(2,1)S(1)} %get-tuple-element.42), channel_id=1, source_target_pairs={{0,8},{4,12},{8,0},{12,4},{16,24},{20,28},{24,16},{28,20},{1,9},{5... | collective-permute-start | bytes 417800 | tf_op jit(solution)/shard_map/ppermute | solution.py:372
  20.2 2.6 %collective-permute-start.2 = (bf16[272,256]{1,0:T(8,128)(2,1)S(1)}, bf16[272,256]{1,0:T(8,128)(2,1)S(1)}, u32[]{:S(2)}, u32[]{:S(2)}) collective-permute-start(bf16[272,256]{1,0:T(8,128)(2,1)S(1)} %get-tuple-element.43), channel_id=1, source_target_pairs={{0,16},{4,20},{8,24},{12,28},{16,0},{20,4},{24,8},{28,12},{1,17},{... | collective-permute-start | bytes 417800 | tf_op jit(solution)/shard_map/ppermute | solution.py:372
  22.9 1.7 %shard_map.163 = (f32[128,256]{1,0:T(8,128)S(1)}, f32[128,512]{1,0:T(8,128)S(1)}, f32[4,256]{1,0:T(4,128)S(1)}, f32[4,128,256]{2,1,0:T(8,128)S(1)}, bf16[1024,128]{1,0:T(8,128)(2,1)S(1)}) custom-call(f32[4]{0:T(128)S(1)} %copy-done.18, bf16[128,256]{1,0:T(8,128)(2,1)S(1)} %get-tuple-element.46.x.refs_5_, bf16[128,256]{1,0:T(8,128)(2,1)S(1)} %copy-done.5, ...), custom_call_target="tpu_custom_call" | custom-call | flops 67108864 | bytes 1712144 | tf_op jit(solution)/shard_map/pallas_call | solution.py:361
  25.0 7.9 %collective-permute-done.2.refs_2_ = bf16[272,256]{1,0:T(8,128)(2,1)S(1)} collective-permute-done((bf16[272,256]{1,0:T(8,128)(2,1)S(1)}, bf16[272,256]{1,0:T(8,128)(2,1)S(1)}, u32[]{:S(2)}, u32[]{:S(2)}) %collective-permute-start.2) | collective-permute-done | bytes 139296 | tf_op jit(solution)/shard_map/ppermute | solution.py:372
  32.9 1.8 %shard_map.164 = (f32[4,128]{1,0:T(4,128)}, f32[4,128]{1,0:T(4,128)}, f32[128,768]{1,0:T(8,128)S(1)}, bf16[128,768]{1,0:T(8,128)(2,1)S(1)}, bf16[128,768]{1,0:T(...) custom-call(bf16[528,256]{1,0:T(8,128)(2,1)S(1)} %get-tuple-element., ...), custom_call_target="tpu_custom_call" | custom-call | flops 201326592 | bytes 4767744 | tf_op jit(solution)/shard_map/pallas_call | solution.py:361
  34.8 1.5 %collective-permute-start.7 = (bf16[128,256]{1,0:T(8,128)(2,1)S(1)}, bf16[128,256]{1,0:T(8,128)(2,1)S(1)}, u32[]{:S(2)}, u32[]{:S(2)}) collective-permute-start(bf16[128,256]{1,0:T(8,128)(2,1)S(1)} %get-tuple-element.57), channel_id=1, source_target_pairs={{0,4},{4,0},{8,12},{12,8},{16,20},{20,16},{24,28},{28,24},{1,5},{5... | collective-permute-start | bytes 196616 | tf_op jit(solution)/shard_map/ppermute | solution.py:372
  36.3 2.1 %collective-permute-start.8 = (bf16[128,256]{1,0:T(8,128)(2,1)S(1)}, bf16[128,256]{1,0:T(8,128)(2,1)S(1)}, u32[]{:S(2)}, u32[]{:S(2)}) collective-permute-start(bf16[128,256]{1,0:T(8,128)(2,1)S(1)} %get-tuple-element.58), channel_id=1, source_target_pairs={{0,8},{4,12},{8,0},{12,4},{16,24},{20,28},{24,16},{28,20},{1,9},{5... | collective-permute-start | bytes 196616 | tf_op jit(solution)/shard_map/ppermute | solution.py:372
  38.3 1.5 %collective-permute-start.5 = (bf16[128,768]{1,0:T(8,128)(2,1)S(1)}, bf16[128,768]{1,0:T(8,128)(2,1)S(1)}, u32[]{:S(2)}, u32[]{:S(2)}) collective-permute-start(bf16[128,768]{1,0:T(8,128)(2,1)S(1)} %get-tuple-element.54), channel_id=1, source_target_pairs={{0,2},{1,3},{2,0},{3,1},{4,6},{5,7},{6,4},{7,5},{8,10},{9,11},{10,... | collective-permute-start | bytes 589832 | tf_op jit(solution)/shard_map/ppermute | solution.py:372
  40.6 3.0 %collective-permute-start.10 = (bf16[128,256]{1,0:T(8,128)(2,1)S(1)}, bf16[128,256]{1,0:T(8,128)(2,1)S(1)}, u32[]{:S(2)}, u32[]{:S(2)}) collective-permute-start(bf16[128,256]{1,0:T(8,128)(2,1)S(1)} %get-tuple-element.60), channel_id=1, source_target_pairs={{0,16},{4,20},{8,24},{12,28},{16,0},{20,4},{24,8},{28,12},{1,17},{... | collective-permute-start | bytes 196616 | tf_op jit(solution)/shard_map/ppermute | solution.py:372
  43.6 1.6 %collective-permute-start.11 = (bf16[128,256]{1,0:T(8,128)(2,1)S(1)}, bf16[128,256]{1,0:T(8,128)(2,1)S(1)}, u32[]{:S(2)}, u32[]{:S(2)}) collective-permute-start(bf16[128,256]{1,0:T(8,128)(2,1)S(1)} %get-tuple-element.61), channel_id=1, source_target_pairs={{0,20},{4,16},{8,28},{12,24},{16,4},{20,0},{24,12},{28,8},{1,21},{... | collective-permute-start | bytes 196616 | tf_op jit(solution)/shard_map/ppermute | solution.py:372
  45.2 2.2 %collective-permute-done.10.refs_8_ = bf16[128,256]{1,0:T(8,128)(2,1)S(1)} collective-permute-done((bf16[128,256]{1,0:T(8,128)(2,1)S(1)}, bf16[128,256]{1,0:T(8,128)(2,1)S(1)}, u32[]{:S(2)}, u32[]{:S(2)}) %collective-permute-start.10) | collective-permute-done | bytes 65568 | tf_op jit(solution)/shard_map/ppermute | solution.py:372
  47.4 0.8 %collective-permute-start.12 = (bf16[128,256]{1,0:T(8,128)(2,1)S(1)}, bf16[128,256]{1,0:T(8,128)(2,1)S(1)}, u32[]{:S(2)}, u32[]{:S(2)}) collective-permute-start(bf16[128,256]{1,0:T(8,128)(2,1)S(1)} %get-tuple-element.62), channel_id=1, source_target_pairs={{0,24},{4,28},{8,16},{12,20},{16,8},{20,12},{24,0},{28,4},{1,25},{... | collective-permute-start | bytes 196616 | tf_op jit(solution)/shard_map/ppermute | solution.py:372
  48.2 3.0 %collective-permute-done.11.refs_9_ = bf16[128,256]{1,0:T(8,128)(2,1)S(1)} collective-permute-done((bf16[128,256]{1,0:T(8,128)(2,1)S(1)}, bf16[128,256]{1,0:T(8,128)(2,1)S(1)}, u32[]{:S(2)}, u32[]{:S(2)}) %collective-permute-start.11) | collective-permute-done | bytes 65568 | tf_op jit(solution)/shard_map/ppermute | solution.py:372
  51.2 2.9 %collective-permute-start.13 = (bf16[128,256]{1,0:T(8,128)(2,1)S(1)}, bf16[128,256]{1,0:T(8,128)(2,1)S(1)}, u32[]{:S(2)}, u32[]{:S(2)}) collective-permute-start(bf16[128,256]{1,0:T(8,128)(2,1)S(1)} %get-tuple-element.63), channel_id=1, source_target_pairs={{0,28},{4,24},{8,20},{12,16},{16,12},{20,8},{24,4},{28,0},{1,29},{... | collective-permute-start | bytes 196616 | tf_op jit(solution)/shard_map/ppermute | solution.py:372
  54.1 4.1 %collective-permute-done.13.refs_11_ = bf16[128,256]{1,0:T(8,128)(2,1)S(1)} collective-permute-done((bf16[128,256]{1,0:T(8,128)(2,1)S(1)}, bf16[128,256]{1,0:T(8,128)(2,1)S(1)}, u32[]{:S(2)}, u32[]{:S(2)}) %collective-permute-start.13) | collective-permute-done | bytes 65568 | tf_op jit(solution)/shard_map/ppermute | solution.py:372
  58.2 0.8 %shard_map.165 = (bf16[128,256]{1,0:T(8,128)(2,1)}, f32[128,256]{1,0:T(8,128)}, f32[128,128]{1,0:T(8,128)}, f32[128,128]{1,0:T(8,128)}, f32[128,128]{1,0:T(8,128)}, /*index=5*/f32[128,128]{1,0:T(8,128)}) custom-call(f32[128,768]{1,0:T(8,128)S(1)} %get-tuple-element.52.refs_0_, bf16[128,768]{1,0:T(8,128)(2,1)S(1)} %collective-permute-done.4.refs_1_, ...), custom_call_target="tpu_custom_call" | custom-call | bytes 2031616 | tf_op jit(solution)/shard_map/pallas_call | solution.py:361
  (47 shorter events, 4.2 us)
Async XLA Ops:
  7.9 15.0 %copy-start.15 = (f32[4,128]{1,0:T(4,128)S(1)}, f32[4,128]{1,0:T(4,128)}, u32[]{:S(2)}) copy-start(f32[4,128]{1,0:T(4,128)} %da.3) | copy-start | bytes 6148
  7.9 15.0 %copy-start.17 = (f32[4,128]{1,0:T(4,128)S(1)}, f32[4,128]{1,0:T(4,128)}, u32[]{:S(2)}) copy-start(f32[4,128]{1,0:T(4,128)} %db.3) | copy-start | bytes 6148
  7.9 15.0 %copy-start.18 = (f32[4]{0:T(128)S(1)}, f32[4]{0:T(128)}, u32[]{:S(2)}) copy-start(f32[4]{0:T(128)} %skip.1) | copy-start | bytes 52
  8.6 14.3 %copy-start.3 = (bf16[128,1024]{1,0:T(8,128)(2,1)S(1)}, bf16[128,1024]{1,0:T(8,128)(2,1)}, u32[]{:S(2)}) copy-start(bf16[128,1024]{1,0:T(8,128)(2,1)} %features.3) | copy-start | bytes 786436
  8.6 14.3 %copy-start.5 = (bf16[128,256]{1,0:T(8,128)(2,1)S(1)}, bf16[128,256]{1,0:T(8,128)(2,1)}, u32[]{:S(2)}) copy-start(bf16[128,256]{1,0:T(8,128)(2,1)} %refs_6_.1) | copy-start | bytes 196612
  8.6 14.3 %copy-start.7 = (bf16[128,128]{1,0:T(8,128)(2,1)S(1)}, bf16[128,128]{1,0:T(8,128)(2,1)}, u32[]{:S(2)}) copy-start(bf16[128,128]{1,0:T(8,128)(2,1)} %refs_9_.1) | copy-start | bytes 98308
  8.6 14.3 %copy-start.9 = (bf16[128,128]{1,0:T(8,128)(2,1)S(1)}, bf16[128,128]{1,0:T(8,128)(2,1)}, u32[]{:S(2)}) copy-start(bf16[128,128]{1,0:T(8,128)(2,1)} %refs_10_.1) | copy-start | bytes 98308
  8.6 14.3 %copy-start.11 = (bf16[128,128]{1,0:T(8,128)(2,1)S(1)}, bf16[128,128]{1,0:T(8,128)(2,1)}, u32[]{:S(2)}) copy-start(bf16[128,128]{1,0:T(8,128)(2,1)} %refs_11_.1) | copy-start | bytes 98308
  8.6 14.3 %copy-start.13 = (bf16[128,128]{1,0:T(8,128)(2,1)S(1)}, bf16[128,128]{1,0:T(8,128)(2,1)}, u32[]{:S(2)}) copy-start(bf16[128,128]{1,0:T(8,128)(2,1)} %refs_12_.1) | copy-start | bytes 98308
  8.6 24.3 %copy-start.1 = (bf16[1024,256]{1,0:T(8,128)(2,1)S(1)}, bf16[1024,256]{1,0:T(8,128)(2,1)}, u32[]{:S(2)}) copy-start(bf16[1024,256]{1,0:T(8,128)(2,1)} %refs_8_.1) | copy-start | bytes 1572868
  8.7 9.5 %collective-permute-start = (bf16[528,256]{1,0:T(8,128)(2,1)S(1)}, bf16[528,256]{1,0:T(8,128)(2,1)S(1)}, u32[]{:S(2)}, u32[]{:S(2)}) collective-permute-start(bf16[528,256]{1,0:T(8,128)(2,1)S(1)} %get-tuple-element.40.refs_0_), channel_id=1, source_target_pairs={{0,4},{4,0},{8,12},{12,8},{16,20},{20,16},{24,28},{28,24},{1,5},{5... | collective-permute-start | bytes 811016 | tf_op jit(solution)/shard_map/ppermute | solution.py:372
  18.4 6.7 %collective-permute-start.1 = (bf16[272,256]{1,0:T(8,128)(2,1)S(1)}, bf16[272,256]{1,0:T(8,128)(2,1)S(1)}, u32[]{:S(2)}, u32[]{:S(2)}) collective-permute-start(bf16[272,256]{1,0:T(8,128)(2,1)S(1)} %get-tuple-element.42), channel_id=1, source_target_pairs={{0,8},{4,12},{8,0},{12,4},{16,24},{20,28},{24,16},{28,20},{1,9},{5... | collective-permute-start | bytes 417800 | tf_op jit(solution)/shard_map/ppermute | solution.py:372
  20.2 12.7 %collective-permute-start.2 = (bf16[272,256]{1,0:T(8,128)(2,1)S(1)}, bf16[272,256]{1,0:T(8,128)(2,1)S(1)}, u32[]{:S(2)}, u32[]{:S(2)}) collective-permute-start(bf16[272,256]{1,0:T(8,128)(2,1)S(1)} %get-tuple-element.43), channel_id=1, source_target_pairs={{0,16},{4,20},{8,24},{12,28},{16,0},{20,4},{24,8},{28,12},{1,17},{... | collective-permute-start | bytes 417800 | tf_op jit(solution)/shard_map/ppermute | solution.py:372
  22.8 10.1 %collective-permute-start.3 = (bf16[272,256]{1,0:T(8,128)(2,1)S(1)}, bf16[272,256]{1,0:T(8,128)(2,1)S(1)}, u32[]{:S(2)}, u32[]{:S(2)}) collective-permute-start(bf16[272,256]{1,0:T(8,128)(2,1)S(1)} %get-tuple-element.44), channel_id=1, source_target_pairs={{0,24},{4,28},{8,16},{12,20},{16,8},{20,12},{24,0},{28,4},{1,25},{... | collective-permute-start | bytes 417800 | tf_op jit(solution)/shard_map/ppermute | solution.py:372
  34.8 5.1 %collective-permute-start.7 = (bf16[128,256]{1,0:T(8,128)(2,1)S(1)}, bf16[128,256]{1,0:T(8,128)(2,1)S(1)}, u32[]{:S(2)}, u32[]{:S(2)}) collective-permute-start(bf16[128,256]{1,0:T(8,128)(2,1)S(1)} %get-tuple-element.57), channel_id=1, source_target_pairs={{0,4},{4,0},{8,12},{12,8},{16,20},{20,16},{24,28},{28,24},{1,5},{5... | collective-permute-start | bytes 196616 | tf_op jit(solution)/shard_map/ppermute | solution.py:372
  36.3 4.3 %collective-permute-start.8 = (bf16[128,256]{1,0:T(8,128)(2,1)S(1)}, bf16[128,256]{1,0:T(8,128)(2,1)S(1)}, u32[]{:S(2)}, u32[]{:S(2)}) collective-permute-start(bf16[128,256]{1,0:T(8,128)(2,1)S(1)} %get-tuple-element.58), channel_id=1, source_target_pairs={{0,8},{4,12},{8,0},{12,4},{16,24},{20,28},{24,16},{28,20},{1,9},{5... | collective-permute-start | bytes 196616 | tf_op jit(solution)/shard_map/ppermute | solution.py:372
  38.3 5.3 %collective-permute-start.9 = (bf16[128,256]{1,0:T(8,128)(2,1)S(1)}, bf16[128,256]{1,0:T(8,128)(2,1)S(1)}, u32[]{:S(2)}, u32[]{:S(2)}) collective-permute-start(bf16[128,256]{1,0:T(8,128)(2,1)S(1)} %get-tuple-element.59), channel_id=1, source_target_pairs={{0,12},{4,8},{8,4},{12,0},{16,28},{20,24},{24,20},{28,16},{1,13},{... | collective-permute-start | bytes 196616 | tf_op jit(solution)/shard_map/ppermute | solution.py:372
  38.3 19.8 %collective-permute-start.4 = (bf16[128,768]{1,0:T(8,128)(2,1)S(1)}, bf16[128,768]{1,0:T(8,128)(2,1)S(1)}, u32[]{:S(2)}, u32[]{:S(2)}) collective-permute-start(bf16[128,768]{1,0:T(8,128)(2,1)S(1)} %get-tuple-element.53), channel_id=1, source_target_pairs={{0,1},{1,0},{2,3},{3,2},{4,5},{5,4},{6,7},{7,6},{8,9},{9,8},{10,11... | collective-permute-start | bytes 589832 | tf_op jit(solution)/shard_map/ppermute | solution.py:372
  38.3 19.8 %collective-permute-start.5 = (bf16[128,768]{1,0:T(8,128)(2,1)S(1)}, bf16[128,768]{1,0:T(8,128)(2,1)S(1)}, u32[]{:S(2)}, u32[]{:S(2)}) collective-permute-start(bf16[128,768]{1,0:T(8,128)(2,1)S(1)} %get-tuple-element.54), channel_id=1, source_target_pairs={{0,2},{1,3},{2,0},{3,1},{4,6},{5,7},{6,4},{7,5},{8,10},{9,11},{10,... | collective-permute-start | bytes 589832 | tf_op jit(solution)/shard_map/ppermute | solution.py:372
  39.8 18.3 %collective-permute-start.6 = (bf16[128,768]{1,0:T(8,128)(2,1)S(1)}, bf16[128,768]{1,0:T(8,128)(2,1)S(1)}, u32[]{:S(2)}, u32[]{:S(2)}) collective-permute-start(bf16[128,768]{1,0:T(8,128)(2,1)S(1)} %get-tuple-element.55), channel_id=1, source_target_pairs={{0,3},{1,2},{2,1},{3,0},{4,7},{5,6},{6,5},{7,4},{8,11},{9,10},{10,... | collective-permute-start | bytes 589832 | tf_op jit(solution)/shard_map/ppermute | solution.py:372
  40.6 6.8 %collective-permute-start.10 = (bf16[128,256]{1,0:T(8,128)(2,1)S(1)}, bf16[128,256]{1,0:T(8,128)(2,1)S(1)}, u32[]{:S(2)}, u32[]{:S(2)}) collective-permute-start(bf16[128,256]{1,0:T(8,128)(2,1)S(1)} %get-tuple-element.60), channel_id=1, source_target_pairs={{0,16},{4,20},{8,24},{12,28},{16,0},{20,4},{24,8},{28,12},{1,17},{... | collective-permute-start | bytes 196616 | tf_op jit(solution)/shard_map/ppermute | solution.py:372
  43.6 7.6 %collective-permute-start.11 = (bf16[128,256]{1,0:T(8,128)(2,1)S(1)}, bf16[128,256]{1,0:T(8,128)(2,1)S(1)}, u32[]{:S(2)}, u32[]{:S(2)}) collective-permute-start(bf16[128,256]{1,0:T(8,128)(2,1)S(1)} %get-tuple-element.61), channel_id=1, source_target_pairs={{0,20},{4,16},{8,28},{12,24},{16,4},{20,0},{24,12},{28,8},{1,21},{... | collective-permute-start | bytes 196616 | tf_op jit(solution)/shard_map/ppermute | solution.py:372
  47.4 6.7 %collective-permute-start.12 = (bf16[128,256]{1,0:T(8,128)(2,1)S(1)}, bf16[128,256]{1,0:T(8,128)(2,1)S(1)}, u32[]{:S(2)}, u32[]{:S(2)}) collective-permute-start(bf16[128,256]{1,0:T(8,128)(2,1)S(1)} %get-tuple-element.62), channel_id=1, source_target_pairs={{0,24},{4,28},{8,16},{12,20},{16,8},{20,12},{24,0},{28,4},{1,25},{... | collective-permute-start | bytes 196616 | tf_op jit(solution)/shard_map/ppermute | solution.py:372
  51.2 7.0 %collective-permute-start.13 = (bf16[128,256]{1,0:T(8,128)(2,1)S(1)}, bf16[128,256]{1,0:T(8,128)(2,1)S(1)}, u32[]{:S(2)}, u32[]{:S(2)}) collective-permute-start(bf16[128,256]{1,0:T(8,128)(2,1)S(1)} %get-tuple-element.63), channel_id=1, source_target_pairs={{0,28},{4,24},{8,20},{12,16},{16,12},{20,8},{24,4},{28,0},{1,29},{... | collective-permute-start | bytes 196616 | tf_op jit(solution)/shard_map/ppermute | solution.py:372
  (9 other events, 7.2 us)

commit v2 on v1

--- a/solution.py
+++ b/solution.py
@@ -12,7 +12,7 @@
 BF16 = jnp.bfloat16
 HIGH = lax.Precision.HIGHEST
 GAIN_ROWS = 16
-DIRECT_PEERS = 8
+HELD_LIMIT = 48
 
 
 def nn(a, b, **kw):
@@ -130,11 +130,25 @@
         ref[2 * n :] = block
 
 
-def front_kernel(me, last, peers_out, features, w_in, gy, ba, ca, bb, cb, da, db, x_out, own_out, *sends):
+def front_kernel(me, last, *refs):
+    refs = list(refs)
+    sources = [refs.pop(0) for _ in range(9)]
+    x_out, own_out = refs.pop(0), refs.pop(0)
+    sems = refs.pop()
+    held = refs[-9:]
+    sends = refs[:-9]
+    copies = [pltpu.make_async_copy(s, h, sems.at[k]) for k, (s, h) in enumerate(zip(sources, held))]
+    for copy in copies:
+        copy.start()
+    da, db, gy, ba, ca, bb, cb, features, w_in = held
+    for copy in copies[:2]:
+        copy.wait()
     width = w_in.shape[1] // da.shape[0]
+    grow_a, left_a, grow_b, left_b = decay_factors(da[...], db[...], width)
+    for copy in copies[2:]:
+        copy.wait()
     x = nn(features[...], w_in[...]).astype(BF16)
     x_out[...] = x
-    grow_a, left_a, grow_b, left_b = decay_factors(da[...], db[...], width)
     xf, gyf = x.astype(F32), gy[...].astype(F32)
     length = x.shape[0]
     up0 = nn(ba[...].T, (xf * left_a).astype(BF16))
@@ -247,7 +261,7 @@
     turned_out[...] = features[...].T
 
 
-def carry_kernel(index, radix, stride, first, direct, n_head, *refs):
+def carry_kernel(index, radix, stride, first, peers, n_head, *refs):
     refs = list(refs)
     own = refs.pop(0)
     received = [refs.pop(0) for _ in range(radix - 1)]
@@ -324,22 +338,15 @@
             ref = refs.pop(0)
             ref[:, 0:rows_out] = share.astype(BF16)
             ref[:, rows_out:] = maps_low
-    if not direct:
-        refs.pop(0)[...] = nn(turned[...], grad_x)
-        return
-    rows_w = turned.shape[0] // direct
-    for k in range(direct):
-        at = pl.multiple_of((seq ^ k) * rows_w, rows_w)
-        share = nn(turned[pl.ds(at, rows_w), :], grad_x)
-        ref = refs.pop(0)
-        ref[...] = share.astype(ref.dtype)
-
-
-def sum_kernel(n_head, direct, scale, *refs):
+    share = nn(turned[...], grad_x).astype(BF16)
+    refs.pop(0)[...] = share.reshape(peers, turned.shape[0] // peers, columns)
+
+
+def sum_kernel(n_head, scale, *refs):
     refs = list(refs)
     own = refs.pop(0)
     others = [refs.pop(0) for _ in range(n_head - 1)]
-    shares = [refs.pop(0) for _ in range(max(direct, 1))]
+    shares = refs.pop(0)
     gf_out, gw_out = refs.pop(0), refs.pop(0)
     columns = gf_out.shape[1]
     n = refs[0].shape[1]
@@ -350,12 +357,18 @@
     gf_out[...] = total(slice(0, columns)).astype(BF16)
     for k, ref in enumerate(refs):
         ref[...] = total(slice(columns + k * n, columns + (k + 1) * n))
-    gw_out[...] = sum([share[...].astype(F32) for share in shares[1:]], shares[0][...]) * scale
-
-
-def call(kernel, outs, *args, flops=0, scalars=0):
+    gw_out[...] = jnp.sum(shares[...].astype(F32), axis=0) * scale
+
+
+def call(kernel, outs, *args, flops=0, scalars=0, held=False):
+    space = pltpu.HBM if held else pltpu.VMEM
     specs = [pl.BlockSpec(memory_space=pltpu.SMEM)] * scalars
-    specs += [pl.BlockSpec(memory_space=pltpu.VMEM)] * (len(args) - scalars)
+    specs += [pl.BlockSpec(memory_space=space)] * (len(args) - scalars)
+    scratch = []
+    if held:
+        scratch = [pltpu.VMEM(a.shape, a.dtype) for a in args] + [pltpu.SemaphoreType.DMA((len(args),))]
+    if held:
+        args = tuple(pltpu.with_memory_space_constraint(a, pltpu.HBM) for a in args)
     bytes_moved = sum(math.prod(a.shape) * a.dtype.itemsize for a in args)
     bytes_moved += sum(math.prod(o.shape) * o.dtype.itemsize for o in outs)
     return pl.pallas_call(
@@ -363,8 +376,9 @@
         out_shape=outs,
         in_specs=specs,
         out_specs=[pl.BlockSpec(memory_space=pltpu.VMEM)] * len(outs),
+        scratch_shapes=scratch,
         cost_estimate=pl.CostEstimate(flops=flops, bytes_accessed=bytes_moved, transcendentals=0),
-        compiler_params=pltpu.CompilerParams(vmem_limit_bytes=48 * 1024 * 1024),
+        compiler_params=pltpu.CompilerParams(vmem_limit_bytes=(HELD_LIMIT if held else 48) * 1024 * 1024),
     )(*args)
 
 
@@ -389,10 +403,11 @@
     steps = radices(peers)
     only = len(steps) == 1
     x, own, *sends = call(
-        functools.partial(front_kernel, seq_index, only, peers),
+        functools.partial(front_kernel, seq_index, only),
         [shape((length, columns), BF16), whole] + [half] * ((steps[0] - 1) if only else 0),
-        features, w_in, grad_y, *maps, *decays,
+        *decays, grad_y, *maps, features, w_in,
         flops=2 * length * depth * columns,
+        held=True,
     )
     gx_local, maps_local, decay_local, factors, turned = call(
         local_kernel,
@@ -420,33 +435,26 @@
         )
         stride *= radix
     received = [swap(send, "seq", j * stride) for j, send in enumerate(sends, start=1)]
-    direct = peers if peers <= DIRECT_PEERS else 0
     rows_out = depth // n_head
-    w_shapes = [shape((depth, columns), F32)]
-    if direct:
-        block = (depth // direct, columns)
-        w_shapes = [shape(block, F32)] + [shape(block, BF16)] * (direct - 1)
+    rows_w = depth // peers
     gd_ahead, gd_behind, own_share, *shares = call(
-        functools.partial(carry_kernel, both_index, steps[-1], stride, only, direct, n_head),
+        functools.partial(carry_kernel, both_index, steps[-1], stride, only, peers, n_head),
         [shape((heads, length), F32)] * 2
         + [shape((length, rows_out + 4 * n), F32)]
         + [shape((length, rows_out + 4 * n), BF16)] * (n_head - 1)
-        + w_shapes,
+        + [shape((peers, rows_w, columns), BF16)],
         own, *received, *([] if only else [before]),
         x, grad_y, turned, w_in, *maps, gx_local, maps_local, decay_local, factors,
         flops=6 * length * depth * columns,
     )
-    head_shares, w_shares = shares[: n_head - 1], shares[n_head - 1 :]
-    if direct:
-        w_shares = w_shares[:1] + [swap(s, "seq", k) for k, s in enumerate(w_shares[1:], start=1)]
-    else:
-        w_shares = [lax.psum_scatter(w_shares[0], "seq", scatter_dimension=0, tiled=True)]
+    *head_shares, w_shares = shares
+    w_shares = lax.all_to_all(w_shares, "seq", 0, 0)
     head_shares = [swap(s, "head", k) for k, s in enumerate(head_shares, start=1)]
     grad_features, grad_w_in, *grad_maps = call(
-        functools.partial(sum_kernel, n_head, direct, 1.0 / math.sqrt(length * peers)),
-        [shape((length, rows_out), BF16), shape((depth // peers, columns), F32)]
+        functools.partial(sum_kernel, n_head, 1.0 / math.sqrt(length * peers)),
+        [shape((length, rows_out), BF16), shape((rows_w, columns), F32)]
         + [shape((length, n), F32)] * 4,
-        own_share, *head_shares, *w_shares,
+        own_share, *head_shares, w_shares,
     )
     return (grad_features, grad_w_in, *grad_maps, gd_ahead, gd_behind)
 

time: 59.6 us -> 48.3 us (0.81)
  local copies, waits for them, and re-layouts: 7.27 us -> 0.06 us
  starting transfers between devices: 21.3 us -> 14.6 us
  Pallas kernels: 5.3 us -> 6.9 us
  waiting for transfers between devices: 24.3 us -> 25.7 us
    ppermute x14 -> x7, starting transfers between devices: 21.3 us -> 9.34 us  [swap(): lax.ppermute(value, axis, [(i, i ^ mask) for i in range(lax.axis_size(axi...]
    unnamed x38 -> x20, local copies, waits for them, and re-layouts: 7.27 us -> 0.06 us
    all_to_all x0 -> x1, starting transfers between devices: none -> 5.29 us  [local(): w_shares = lax.all_to_all(w_shares, 'seq', 0, 0)]
    all_to_all x0 -> x1, waiting for transfers between devices: none -> 1.75 us  [local(): w_shares = lax.all_to_all(w_shares, 'seq', 0, 0)]
    pallas_call x5, Pallas kernels: 5.3 us -> 6.9 us  [call(): pl.pallas_call(kernel, out_shape=outs, in_specs=specs, out_specs=[pl.Bloc...]
    ppermute x14 -> x7, waiting for transfers between devices: 24.3 us -> 23.9 us  [swap(): lax.ppermute(value, axis, [(i, i ^ mask) for i in range(lax.axis_size(axi...]
  transfers between devices with their start and end apart: 14 -> 8, of which waited for: 7 -> 6; matrix products, arithmetic and copies ran while one was open for 0% -> 0% of each run, Pallas kernels for 3% -> 4%
where the time goes in v2:
time: 48.3 us; the launch traced here: 48.1 us
  waiting for transfers between devices  25.7 us (53%)
  starting transfers between devices  14.6 us (30%)
  Pallas kernels  6.9 us (14%)
  between operations  0.8 us (2%)
    ppermute x7, waiting for transfers between devices, swap(): lax.ppermute(value, axis, [(i, i ^ mask) for i in range(lax.axis_size(axi...  23.9 us
    ppermute x7, starting transfers between devices, swap(): lax.ppermute(value, axis, [(i, i ^ mask) for i in range(lax.axis_size(axi...  9.34 us
    pallas_call x5, Pallas kernels, call(): pl.pallas_call(kernel, out_shape=outs, in_specs=specs, out_specs=[pl.Bloc...  6.9 us
    all_to_all x1, starting transfers between devices, local(): w_shares = lax.all_to_all(w_shares, 'seq', 0, 0)  5.29 us
    all_to_all x1, waiting for transfers between devices, local(): w_shares = lax.all_to_all(w_shares, 'seq', 0, 0)  1.75 us
  transfers between devices with their start and end apart: 8, of which 6 were waited for; matrix products, arithmetic and copies ran while one was open for 0% of the time, Pallas kernels for 4%

profile of v2, /device:TPU:0, one launch (start us, length us, event | category | flops | bytes accessed | tf_op | source)
XLA Modules:
  0.0 48.1 jit_solution(10683324173576961036)
XLA Ops:
  0.7 1.9 %shard_map.161 = (bf16[128,256]{1,0:T(8,128)(2,1)S(1)}, bf16[528,256]{1,0:T(8,128)(2,1)S(1)}) custom-call(f32[4,128]{1,0:T(4,128)} %da.1, f32[4,128]{1,0:T(4,128)} %db.1, bf16[128,256]{1,0:T(8,128)(2,1)} %refs_6_.3, bf16[128,128]{1,0:T(8,128)(2,1)} %refs_9_.1, bf16[128,128]{1,0:T(8,128)(2,1)} %refs_10_.1, bf16[128,128]{1,0:T(8,128)(2,1)} %refs_11_.1, ...), custom_call_target="tpu_custom_call" | custom-call | flops 67108864 | bytes 1323008 | tf_op jit(solution)/shard_map/pallas_call | solution.py:374
  2.6 0.0 copy-start.1
  2.6 0.0 copy-start.2
  2.6 0.0 copy-start.3
  2.6 0.0 copy-start.4
  2.6 0.0 copy-start.5
  2.6 0.0 copy-start.6
  2.6 0.0 copy-start
  2.7 3.0 %collective-permute-start = (bf16[528,256]{1,0:T(8,128)(2,1)S(1)}, bf16[528,256]{1,0:T(8,128)(2,1)S(1)}, u32[]{:S(2)}, u32[]{:S(2)}) collective-permute-start(bf16[528,256]{1,0:T(8,128)(2,1)S(1)} %get-tuple-element.33.refs_0_), channel_id=1, source_target_pairs={{0,4},{4,0},{8,12},{12,8},{16,20},{20,16},{24,28},{28,24},{1,5},{5... | collective-permute-start | bytes 811016 | tf_op jit(solution)/shard_map/ppermute | solution.py:386
  5.7 6.5 %collective-permute-done.refs_1_ = bf16[528,256]{1,0:T(8,128)(2,1)S(1)} collective-permute-done((bf16[528,256]{1,0:T(8,128)(2,1)S(1)}, bf16[528,256]{1,0:T(8,128)(2,1)S(1)}, u32[]{:S(2)}, u32[]{:S(2)}) %collective-permute-start) | collective-permute-done | bytes 270368 | tf_op jit(solution)/shard_map/ppermute | solution.py:386
  12.2 0.2 shard_map.162
  12.4 1.9 %collective-permute-start.1 = (bf16[272,256]{1,0:T(8,128)(2,1)S(1)}, bf16[272,256]{1,0:T(8,128)(2,1)S(1)}, u32[]{:S(2)}, u32[]{:S(2)}) collective-permute-start(bf16[272,256]{1,0:T(8,128)(2,1)S(1)} %get-tuple-element.35), channel_id=1, source_target_pairs={{0,8},{4,12},{8,0},{12,4},{16,24},{20,28},{24,16},{28,20},{1,9},{5... | collective-permute-start | bytes 417800 | tf_op jit(solution)/shard_map/ppermute | solution.py:386
  14.2 2.6 %collective-permute-start.2 = (bf16[272,256]{1,0:T(8,128)(2,1)S(1)}, bf16[272,256]{1,0:T(8,128)(2,1)S(1)}, u32[]{:S(2)}, u32[]{:S(2)}) collective-permute-start(bf16[272,256]{1,0:T(8,128)(2,1)S(1)} %get-tuple-element.36), channel_id=1, source_target_pairs={{0,16},{4,20},{8,24},{12,28},{16,0},{20,4},{24,8},{28,12},{1,17},{... | collective-permute-start | bytes 417800 | tf_op jit(solution)/shard_map/ppermute | solution.py:386
  16.9 1.7 %shard_map.163 = (f32[128,256]{1,0:T(8,128)S(1)}, f32[128,512]{1,0:T(8,128)S(1)}, f32[4,256]{1,0:T(4,128)S(1)}, f32[4,128,256]{2,1,0:T(8,128)S(1)}, bf16[1024,128]{1,0:T(8,128)(2,1)S(1)}) custom-call(f32[4]{0:T(128)S(1)} %copy-done.9, bf16[128,256]{1,0:T(8,128)(2,1)S(1)} %get-tuple-element.39.x.refs_5_, bf16[128,256]{1,0:T(8,128)(2,1)S(1)} %copy-done.2, ...), custom_call_target="tpu_custom_call" | custom-call | flops 67108864 | bytes 1712144 | tf_op jit(solution)/shard_map/pallas_call | solution.py:374
  18.6 0.4 collective-permute-done.1.refs_1_
  19.0 7.9 %collective-permute-done.2.refs_2_ = bf16[272,256]{1,0:T(8,128)(2,1)S(1)} collective-permute-done((bf16[272,256]{1,0:T(8,128)(2,1)S(1)}, bf16[272,256]{1,0:T(8,128)(2,1)S(1)}, u32[]{:S(2)}, u32[]{:S(2)}) %collective-permute-start.2) | collective-permute-done | bytes 139296 | tf_op jit(solution)/shard_map/ppermute | solution.py:386
  26.9 2.2 %shard_map.164 = (f32[4,128]{1,0:T(4,128)}, f32[4,128]{1,0:T(4,128)}, f32[128,768]{1,0:T(8,128)S(1)}, bf16[128,768]{1,0:T(8,128)(2,1)S(1)}, bf16[128,768]{1,0:T(...) custom-call(bf16[528,256]{1,0:T(8,128)(2,1)S(1)} %get-tuple-element.34.refs_0_, ...), custom_call_target="tpu_custom_call" | custom-call | flops 201326592 | bytes 4702208 | tf_op jit(solution)/shard_map/pallas_call | solution.py:374
  29.2 5.3 %all-to-all-start = ((bf16[8,128,256]{2,1,0:T(8,128)(2,1)}), bf16[8,128,256]{2,1,0:T(8,128)(2,1)S(1)}, u32[]{:S(2)}, u32[]{:S(2)}) async-start(bf16[8,128,256]{2,1,0:T(8,128)(2,1)} %get-tuple-element.49), calls=%async_computation | async-start | bytes 1048576 | tf_op jit(solution)/shard_map/all_to_all | solution.py:451
  34.5 1.6 %collective-permute-start.5 = (bf16[128,768]{1,0:T(8,128)(2,1)S(1)}, bf16[128,768]{1,0:T(8,128)(2,1)S(1)}, u32[]{:S(2)}, u32[]{:S(2)}) collective-permute-start(bf16[128,768]{1,0:T(8,128)(2,1)S(1)} %get-tuple-element.47), channel_id=1, source_target_pairs={{0,2},{1,3},{2,0},{3,1},{4,6},{5,7},{6,4},{7,5},{8,10},{9,11},{10,... | collective-permute-start | bytes 589832 | tf_op jit(solution)/shard_map/ppermute | solution.py:386
  36.0 0.3 collective-permute-start.6
  36.3 5.9 %collective-permute-done.5.refs_2_ = bf16[128,768]{1,0:T(8,128)(2,1)S(1)} collective-permute-done((bf16[128,768]{1,0:T(8,128)(2,1)S(1)}, bf16[128,768]{1,0:T(8,128)(2,1)S(1)}, u32[]{:S(2)}, u32[]{:S(2)}) %collective-permute-start.5) | collective-permute-done | bytes 196640 | tf_op jit(solution)/shard_map/ppermute | solution.py:386
  42.2 3.3 %collective-permute-done.6.refs_3_ = bf16[128,768]{1,0:T(8,128)(2,1)S(1)} collective-permute-done((bf16[128,768]{1,0:T(8,128)(2,1)S(1)}, bf16[128,768]{1,0:T(8,128)(2,1)S(1)}, u32[]{:S(2)}, u32[]{:S(2)}) %collective-permute-start.6) | collective-permute-done | bytes 196640 | tf_op jit(solution)/shard_map/ppermute | solution.py:386
  45.5 1.7 %all-to-all-done.refs_4_ = bf16[8,128,256]{2,1,0:T(8,128)(2,1)S(1)} async-done(((bf16[8,128,256]{2,1,0:T(8,128)(2,1)}), bf16[8,128,256]{2,1,0:T(8,128)(2,1)S(1)}, u32[]{:S(2)}, u32[]{:S(2)}) %all-to-all-start) | async-done | bytes 524320 | tf_op jit(solution)/shard_map/all_to_all | solution.py:451
  47.3 0.8 %shard_map.165 = (bf16[128,256]{1,0:T(8,128)(2,1)}, f32[128,256]{1,0:T(8,128)}, f32[128,128]{1,0:T(8,128)}, f32[128,128]{1,0:T(8,128)}, f32[128,128]{1,0:T(8,128)}, /*index=5*/f32[128,128]{1,0:T(8,128)}) custom-call(f32[128,768]{1,0:T(8,128)S(1)} %get-tuple-element.45.refs_0_, bf16[128,768]{1,0:T(8,128)(2,1)S(1)} %collective-permute-done.4.refs_1_, ...), custom_call_target="tpu_custom_call" | custom-call | bytes 1966080 | tf_op jit(solution)/shard_map/pallas_call | solution.py:374
  (17 shorter events, 0.0 us)
Async XLA Ops:
  0.6 16.2 %copy-start.7 = (f32[4,128]{1,0:T(4,128)S(1)}, f32[4,128]{1,0:T(4,128)}, u32[]{:S(2)}) copy-start(f32[4,128]{1,0:T(4,128)} %da.1) | copy-start | bytes 6148
  0.6 16.2 %copy-start.8 = (f32[4,128]{1,0:T(4,128)S(1)}, f32[4,128]{1,0:T(4,128)}, u32[]{:S(2)}) copy-start(f32[4,128]{1,0:T(4,128)} %db.1) | copy-start | bytes 6148
  0.7 16.2 %copy-start.9 = (f32[4]{0:T(128)S(1)}, f32[4]{0:T(128)}, u32[]{:S(2)}) copy-start(f32[4]{0:T(128)} %skip.1) | copy-start | bytes 52
  2.6 14.3 %copy-start.1 = (bf16[128,1024]{1,0:T(8,128)(2,1)S(1)}, bf16[128,1024]{1,0:T(8,128)(2,1)}, u32[]{:S(2)}) copy-start(bf16[128,1024]{1,0:T(8,128)(2,1)} %features.1) | copy-start | bytes 786436
  2.6 14.3 %copy-start.2 = (bf16[128,256]{1,0:T(8,128)(2,1)S(1)}, bf16[128,256]{1,0:T(8,128)(2,1)}, u32[]{:S(2)}) copy-start(bf16[128,256]{1,0:T(8,128)(2,1)} %refs_6_.3) | copy-start | bytes 196612
  2.6 14.3 %copy-start.3 = (bf16[128,128]{1,0:T(8,128)(2,1)S(1)}, bf16[128,128]{1,0:T(8,128)(2,1)}, u32[]{:S(2)}) copy-start(bf16[128,128]{1,0:T(8,128)(2,1)} %refs_9_.1) | copy-start | bytes 98308
  2.6 14.3 %copy-start.4 = (bf16[128,128]{1,0:T(8,128)(2,1)S(1)}, bf16[128,128]{1,0:T(8,128)(2,1)}, u32[]{:S(2)}) copy-start(bf16[128,128]{1,0:T(8,128)(2,1)} %refs_10_.1) | copy-start | bytes 98308
  2.6 14.3 %copy-start.5 = (bf16[128,128]{1,0:T(8,128)(2,1)S(1)}, bf16[128,128]{1,0:T(8,128)(2,1)}, u32[]{:S(2)}) copy-start(bf16[128,128]{1,0:T(8,128)(2,1)} %refs_11_.1) | copy-start | bytes 98308
  2.6 14.3 %copy-start.6 = (bf16[128,128]{1,0:T(8,128)(2,1)S(1)}, bf16[128,128]{1,0:T(8,128)(2,1)}, u32[]{:S(2)}) copy-start(bf16[128,128]{1,0:T(8,128)(2,1)} %refs_12_.1) | copy-start | bytes 98308
  2.6 24.3 %copy-start = (bf16[1024,256]{1,0:T(8,128)(2,1)S(1)}, bf16[1024,256]{1,0:T(8,128)(2,1)}, u32[]{:S(2)}) copy-start(bf16[1024,256]{1,0:T(8,128)(2,1)} %refs_8_.3) | copy-start | bytes 1572868
  2.7 9.5 %collective-permute-start = (bf16[528,256]{1,0:T(8,128)(2,1)S(1)}, bf16[528,256]{1,0:T(8,128)(2,1)S(1)}, u32[]{:S(2)}, u32[]{:S(2)}) collective-permute-start(bf16[528,256]{1,0:T(8,128)(2,1)S(1)} %get-tuple-element.33.refs_0_), channel_id=1, source_target_pairs={{0,4},{4,0},{8,12},{12,8},{16,20},{20,16},{24,28},{28,24},{1,5},{5... | collective-permute-start | bytes 811016 | tf_op jit(solution)/shard_map/ppermute | solution.py:386
  12.4 6.7 %collective-permute-start.1 = (bf16[272,256]{1,0:T(8,128)(2,1)S(1)}, bf16[272,256]{1,0:T(8,128)(2,1)S(1)}, u32[]{:S(2)}, u32[]{:S(2)}) collective-permute-start(bf16[272,256]{1,0:T(8,128)(2,1)S(1)} %get-tuple-element.35), channel_id=1, source_target_pairs={{0,8},{4,12},{8,0},{12,4},{16,24},{20,28},{24,16},{28,20},{1,9},{5... | collective-permute-start | bytes 417800 | tf_op jit(solution)/shard_map/ppermute | solution.py:386
  14.2 12.7 %collective-permute-start.2 = (bf16[272,256]{1,0:T(8,128)(2,1)S(1)}, bf16[272,256]{1,0:T(8,128)(2,1)S(1)}, u32[]{:S(2)}, u32[]{:S(2)}) collective-permute-start(bf16[272,256]{1,0:T(8,128)(2,1)S(1)} %get-tuple-element.36), channel_id=1, source_target_pairs={{0,16},{4,20},{8,24},{12,28},{16,0},{20,4},{24,8},{28,12},{1,17},{... | collective-permute-start | bytes 417800 | tf_op jit(solution)/shard_map/ppermute | solution.py:386
  16.8 10.1 %collective-permute-start.3 = (bf16[272,256]{1,0:T(8,128)(2,1)S(1)}, bf16[272,256]{1,0:T(8,128)(2,1)S(1)}, u32[]{:S(2)}, u32[]{:S(2)}) collective-permute-start(bf16[272,256]{1,0:T(8,128)(2,1)S(1)} %get-tuple-element.37), channel_id=1, source_target_pairs={{0,24},{4,28},{8,16},{12,20},{16,8},{20,12},{24,0},{28,4},{1,25},{... | collective-permute-start | bytes 417800 | tf_op jit(solution)/shard_map/ppermute | solution.py:386
  29.2 18.1 %all-to-all-start = ((bf16[8,128,256]{2,1,0:T(8,128)(2,1)}), bf16[8,128,256]{2,1,0:T(8,128)(2,1)S(1)}, u32[]{:S(2)}, u32[]{:S(2)}) async-start(bf16[8,128,256]{2,1,0:T(8,128)(2,1)} %get-tuple-element.49), calls=%async_computation | async-start | bytes 1048576 | tf_op jit(solution)/shard_map/all_to_all | solution.py:451
  34.5 1.9 %collective-permute-start.4 = (bf16[128,768]{1,0:T(8,128)(2,1)S(1)}, bf16[128,768]{1,0:T(8,128)(2,1)S(1)}, u32[]{:S(2)}, u32[]{:S(2)}) collective-permute-start(bf16[128,768]{1,0:T(8,128)(2,1)S(1)} %get-tuple-element.46), channel_id=1, source_target_pairs={{0,1},{1,0},{2,3},{3,2},{4,5},{5,4},{6,7},{7,6},{8,9},{9,8},{10,11... | collective-permute-start | bytes 589832 | tf_op jit(solution)/shard_map/ppermute | solution.py:386
  34.5 7.8 %collective-permute-start.5 = (bf16[128,768]{1,0:T(8,128)(2,1)S(1)}, bf16[128,768]{1,0:T(8,128)(2,1)S(1)}, u32[]{:S(2)}, u32[]{:S(2)}) collective-permute-start(bf16[128,768]{1,0:T(8,128)(2,1)S(1)} %get-tuple-element.47), channel_id=1, source_target_pairs={{0,2},{1,3},{2,0},{3,1},{4,6},{5,7},{6,4},{7,5},{8,10},{9,11},{10,... | collective-permute-start | bytes 589832 | tf_op jit(solution)/shard_map/ppermute | solution.py:386
  36.0 9.5 %collective-permute-start.6 = (bf16[128,768]{1,0:T(8,128)(2,1)S(1)}, bf16[128,768]{1,0:T(8,128)(2,1)S(1)}, u32[]{:S(2)}, u32[]{:S(2)}) collective-permute-start(bf16[128,768]{1,0:T(8,128)(2,1)S(1)} %get-tuple-element.48), channel_id=1, source_target_pairs={{0,3},{1,2},{2,1},{3,0},{4,7},{5,6},{6,5},{7,4},{8,11},{9,10},{10,... | collective-permute-start | bytes 589832 | tf_op jit(solution)/shard_map/ppermute | solution.py:386

commit v3 on v2

v3 whole, which is shorter than its diff:
```python
import functools
import math

import jax
import jax.numpy as jnp
from jax import lax
from jax.experimental import pallas as pl
from jax.experimental.pallas import tpu as pltpu
from jax.sharding import PartitionSpec as P

F32 = jnp.float32
BF16 = jnp.bfloat16
HIGH = lax.Precision.HIGHEST
GAIN_ROWS = 16
VMEM_LIMIT = 48 * 1024 * 1024


def nn(a, b, **kw):
    return lax.dot_general(a, b, (((1,), (0,)), ((), ())), preferred_element_type=F32, **kw)


def nt(a, b, **kw):
    return lax.dot_general(a, b, (((1,), (1,)), ((), ())), preferred_element_type=F32, **kw)


def iotas(rows, cols):
    return (
        lax.broadcasted_iota(jnp.int32, (rows, cols), 0),
        lax.broadcasted_iota(jnp.int32, (rows, cols), 1),
    )


def spread_rows(values, width):
    heads, length = values.shape
    return jnp.concatenate(
        [jnp.broadcast_to(values[h : h + 1], (width, length)) for h in range(heads)], axis=0
    )


def split3(value):
    high = value.astype(BF16)
    rest = value - high.astype(F32)
    middle = rest.astype(BF16)
    low = (rest - middle.astype(F32)).astype(BF16)
    return high, middle, low


def masked_sums(masks, values):
    masks = masks.astype(BF16)
    return sum(nt(masks, part) for part in split3(values))


def decay_factors(d_ahead, d_behind, width):
    length = d_ahead.shape[1]
    row, col = iotas(length, length)
    upto = (col <= row).astype(F32)
    since = (col >= row).astype(F32)
    ahead = masked_sums(
        jnp.concatenate([upto, 1.0 - upto], axis=0), spread_rows(d_ahead, width)
    )
    behind = masked_sums(
        jnp.concatenate([since, 1.0 - since], axis=0), spread_rows(d_behind, width)
    )
    ahead, behind = jnp.exp(ahead), jnp.exp(behind)
    return ahead[:length], ahead[length:], behind[:length], behind[length:]


def radices(peers):
    bits = peers.bit_length() - 1
    return ([2] if bits % 2 else []) + [4] * (bits // 2)


def digit(index, stride, radix):
    return lax.rem(lax.div(index, stride), radix)


def read_gain(block, k=0):
    rows = block.astype(F32)[3 * k : 3 * k + 3]
    return rows[0:1] + rows[1:2] + rows[2:3]


def gain_block(*gains):
    rows = [p.astype(F32) for gain in gains for p in split3(gain)]
    pad = jnp.zeros((GAIN_ROWS - len(rows), gains[0].shape[1]), F32)
    return jnp.concatenate(rows + [pad], axis=0).astype(BF16)


def product_where(conditions, gains):
    result = jnp.ones_like(gains[0])
    for condition, gain in zip(conditions, gains):
        result = jnp.where(condition, result * gain, result)
    return result


def merge_coefficients(me, members, gains_up, gains_down):
    below, above = [], []
    others = range(1, len(members))
    for j in others:
        q = members[j]
        low = product_where(
            [jnp.logical_and(members[i] > q, members[i] < me) for i in others], [gains_up[i] for i in others]
        )
        high = product_where(
            [jnp.logical_and(members[i] < q, members[i] > me) for i in others], [gains_down[i] for i in others]
        )
        below.append(jnp.where(q < me, low, 0.0))
        above.append(jnp.where(q > me, high, 0.0))
    return below, above


def write_whole(out, up, down, gain_up, gain_down):
    n = up.shape[0]
    out[0:n] = up.astype(BF16)
    out[n : 2 * n] = down.astype(BF16)
    out[2 * n :] = gain_block(gain_up, gain_down)


def write_halves(outs, up, down, gain_up, gain_down, me):
    n = up.shape[0]
    blocks = gain_block(gain_up), gain_block(gain_down)
    up, down = up.astype(BF16), down.astype(BF16)
    for j, out in enumerate(outs, start=1):
        upward = (me ^ j) > me
        out[0:n] = jnp.where(upward, up, down)
        out[n:] = jnp.where(upward, *blocks)


def write_chunk(outs, me, last, *chunk):
    if last:
        write_halves(outs, *chunk, me())
    else:
        write_whole(outs[0], *chunk)


def start_copies(sources, targets, sems):
    copies = [pltpu.make_async_copy(s, t, sems.at[k]) for k, (s, t) in enumerate(zip(sources, targets))]
    for copy in copies:
        copy.start()
    return copies


def gradient_kernel(me, last, width, *refs):
    *refs, sems = refs
    sources, outs, held = refs[:5], refs[5:-5], refs[-5:]
    copies = start_copies(sources, held, sems)
    da, db, gy, ca, cb = held
    for copy in copies[:2]:
        copy.wait()
    factors = decay_factors(da[...], db[...], width)
    *sends, factors_out = outs
    for k in range(4):
        factors_out[k] = factors[k]
    grow_a, _, grow_b, _ = factors
    for copy in copies[2:]:
        copy.wait()
    gyf = gy[...].astype(F32)
    up = nn(cb[...].T, (gyf * grow_b).astype(BF16))
    down = nn(ca[...].T, (gyf * grow_a).astype(BF16))
    write_chunk(sends, me, last, up, down, grow_b[0:1], grow_a[gyf.shape[0] - 1 :])


def state_kernel(me, last, *refs):
    *refs, sems = refs
    sources, factors, outs, held = refs[:4], refs[4], refs[5:-4], refs[-4:]
    copies = start_copies(sources, held, sems)
    ba, bb, features, w_in = held
    for copy in copies:
        copy.wait()
    *sends, x_out = outs
    x = nn(features[...], w_in[...]).astype(BF16)
    x_out[...] = x
    xf = x.astype(F32)
    up = nn(ba[...].T, (xf * factors[1]).astype(BF16))
    down = nn(bb[...].T, (xf * factors[3]).astype(BF16))
    write_chunk(sends, me, last, up, down, factors[0, x.shape[0] - 1 :], factors[2, 0:1])


def step_kernel(index, stride, radix, first, next_last, next_radix, *refs):
    refs = list(refs)
    own = refs.pop(0)
    received = [refs.pop(0) for _ in range(radix - 1)]
    before = None if first else refs.pop(0)
    pre_out = refs.pop(0)
    n = (own.shape[0] - GAIN_ROWS) // 2
    seq = index()
    me = digit(seq, stride, radix)
    members = [me ^ j for j in range(radix)]
    loaded = [(ref[0:n].astype(F32), ref[n : 2 * n].astype(F32)) for ref in [own] + received]
    gains = [[read_gain(ref[2 * n :], k) for ref in [own] + received] for k in range(2)]
    coefficients = merge_coefficients(me, members, *gains)
    width = own.shape[1]
    new_grow = []
    totals = []
    for down in range(2):
        total = sum(coefficients[down][j - 1] * loaded[j][down] for j in range(1, radix))
        inside = [(members[j] > me) if down else (members[j] < me) for j in range(1, radix)]
        grow = product_where(inside, gains[down][1:])
        if not first:
            kept = before[2 * n + down : 2 * n + down + 1]
            total = kept * total + before[down * n : (down + 1) * n]
            grow = kept * grow
        pre_out[down * n : (down + 1) * n] = total
        new_grow.append(grow)
        group = 0.0
        for j in range(radix):
            rest = [i for i in range(radix) if i != j]
            outer = [(members[i] < members[j]) if down else (members[i] > members[j]) for i in rest]
            group = group + product_where(outer, [gains[down][i] for i in rest]) * loaded[j][down]
        totals.append(group)
    pre_out[2 * n :] = jnp.concatenate(new_grow + [jnp.zeros((6, width), F32)], axis=0)
    gain = [functools.reduce(lambda a, b: a * b, gains[k]) for k in range(2)]
    write_chunk(refs, lambda: digit(seq, stride * radix, next_radix), next_last, *totals, *gain)


def local_kernel(
    skip, x, gy, features, ba, ca, bb, cb, da, db, gx_out, maps_out, decay_out, turned_out
):
    heads, length = da.shape
    width = x.shape[1] // heads
    n = ba.shape[1]
    row, col = iotas(length, length)
    upto = (col <= row).astype(F32)
    since = (col >= row).astype(F32)
    pad = jnp.zeros((8 - heads, length), F32)
    d_ahead = jnp.concatenate([da[...], pad], axis=0)
    d_behind = jnp.concatenate([db[...], pad], axis=0)
    columns_a = masked_sums(upto, d_ahead)
    columns_b = masked_sums(since, d_behind)
    rows_a = columns_a.T
    rows_b = columns_b.T
    later, same = col > row, col == row
    raw_a = nt(ba[...], ca[...])
    raw_b = nt(bb[...], cb[...])
    affinity = jnp.where(same, raw_a + raw_b, jnp.where(later, raw_a, raw_b))
    weight_sum = jnp.zeros((length, length), F32)
    counts = jnp.concatenate([since.T, upto.T], axis=1).astype(BF16)
    cross = jnp.concatenate([row < col, row > col], axis=1).astype(F32)
    totals = []
    for h in range(heads):
        part = slice(h * width, (h + 1) * width)
        gap = jnp.where(
            later,
            rows_a[h : h + 1] - columns_a[:, h : h + 1],
            rows_b[h : h + 1] - columns_b[:, h : h + 1],
        )
        decay = jnp.exp(jnp.where(same, 0.0, gap))
        score_grad = nt(x[:, part], gy[:, part])
        weighted = score_grad * decay
        weight_sum = weight_sum + weighted
        gx_out[:, part] = nn((decay * affinity).astype(BF16), gy[:, part]) + skip[h] * gy[:, part].astype(F32)
        pieces = nn((weighted * affinity).astype(BF16), counts)
        totals.append(jnp.sum(pieces * cross, axis=0, keepdims=True))
    for h in range(heads):
        decay_out[h : h + 1] = totals[h]
    ahead = jnp.where(col >= row, weight_sum, 0.0).astype(BF16)
    behind = jnp.where(col <= row, weight_sum, 0.0).astype(BF16)
    maps_out[:, 0:n] = nn(ahead, ca[...])
    maps_out[:, n : 2 * n] = nn(ahead.T, ba[...])
    maps_out[:, 2 * n : 3 * n] = nn(behind, cb[...])
    maps_out[:, 3 * n :] = nn(behind.T, bb[...])
    turned_out[...] = features[...].T


def entering(chunks, me, radix, n):
    members = [me ^ j for j in range(radix)]
    results = []
    for received, before in chunks:
        gains = [read_gain(ref[n:]) for ref in received]
        gains = gains[:1] + gains
        coefficients = merge_coefficients(me, members, gains, gains)

        def enter(down, received=received, before=before, coefficients=coefficients):
            total = 0.0
            for coefficient, ref in zip(coefficients[down], received):
                total = total + coefficient * ref[0:n].astype(F32)
            if before is not None:
                total = before[2 * n + down : 2 * n + down + 1] * total + before[down * n : (down + 1) * n]
            return total

        results.append(enter)
    return results


def take_chunks(refs, radix, first, count):
    chunks = []
    for _ in range(count):
        received = [refs.pop(0) for _ in range(radix - 1)]
        chunks.append((received, None if first else refs.pop(0)))
    return chunks


def carry_kernel(index, steps, stride, direct, *refs):
    refs = list(refs)
    chunks = take_chunks(refs, steps[-1], len(steps) == 1, 1)
    turned, ba, bb, gx_local, factors, gx_out = [refs.pop(0) for _ in range(6)]
    seq = index()
    me = digit(seq, stride, steps[-1])
    (gradient,) = entering(chunks, me, steps[-1], ba.shape[1])
    grad_x = gx_local[...]
    for b, grad, left in ((ba, gradient(1), factors[1]), (bb, gradient(0), factors[3])):
        grad_x = grad_x + nn(b[...], grad.astype(BF16)).astype(BF16).astype(F32) * left
    grad_x = grad_x.astype(BF16)
    gx_out[...] = grad_x
    if not direct:
        refs.pop(0)[...] = nn(turned[...], grad_x).astype(BF16)
        return
    rows = refs[0].shape[1]
    for far in (1, 0):
        for j in range(1, steps[0]):
            out = refs.pop(0)
            for k in range(2):
                at = (me ^ (2 * far + k)) * steps[0] + (digit(seq, 1, steps[0]) ^ j)
                at = pl.multiple_of(at * rows, rows)
                out[k] = nn(turned[pl.ds(at, rows), :], grad_x).astype(BF16)


def fold_kernel(index, steps, far, turned, grad_x, *refs):
    received, outs = refs[: steps[0] - 1], refs[-2:]
    rows = received[0].shape[1]
    seq = index()
    for k in range(2):
        at = (digit(seq, steps[0], steps[1]) ^ (2 * far + k)) * steps[0] + digit(seq, 1, steps[0])
        share = nn(turned[pl.ds(pl.multiple_of(at * rows, rows), rows), :], grad_x[...])
        total = sum([ref[k].astype(F32) for ref in received], share)
        outs[k][...] = total.astype(outs[k].dtype)


def share_kernel(index, radix, stride, first, n_head, *refs):
    refs = list(refs)
    chunks = take_chunks(refs, radix, first, 2)
    grad_x, x, gy, w_in, ba, ca, bb, cb = [refs.pop(0) for _ in range(8)]
    maps_local, decay_local, factors = [refs.pop(0) for _ in range(3)]
    gd_a_out, gd_b_out, own_out, send_out, maps_out = refs
    heads = decay_local.shape[0]
    n = ba.shape[1]
    length, columns = x.shape
    width = columns // heads
    seq, head = index()
    gradient, state = entering(chunks, digit(seq, stride, radix), radix, n)
    grow_a, left_a, grow_b, left_b = [factors[k] for k in range(4)]
    xf, gyf = x[...].astype(F32), gy[...].astype(F32)
    row, col = iotas(length, length)
    own_rows, own_cols = iotas(8, columns)
    group = (lax.div(own_cols, width) == own_rows).astype(BF16)
    frame = lax.broadcasted_iota(jnp.int32, (length, 1), 0)

    def direction(state, grad, grow, left, b, c, at_end, later, earlier):
        gain = jnp.sum(jnp.where(frame == at_end, grow, 0.0), axis=0, keepdims=True)
        state_low, grad_low = state.astype(BF16), grad.astype(BF16)
        carried = grow * nn(c[...], state_low)
        through = gain * jnp.sum(state * grad, axis=0, keepdims=True)
        read = gyf * carried + jnp.where(frame == at_end, through, 0.0)
        write = nn(b[...], grad_low).astype(BF16).astype(F32) * left * xf
        reads = nt(group, read.astype(BF16))
        writes = nt(group, write.astype(BF16))
        grad_decay = nn(reads, later, precision=HIGH) + nn(writes, earlier, precision=HIGH)
        grad_c = nt((gyf * grow).astype(BF16), state_low)
        grad_b = nt((xf * left).astype(BF16), grad_low)
        return grad_b, grad_c, grad_decay

    gb_a, gc_a, gd_a = direction(
        state(0), gradient(1), grow_a, left_a, ba, ca, length - 1,
        (row >= col).astype(F32), (row < col).astype(F32),
    )
    gb_b, gc_b, gd_b = direction(
        state(1), gradient(0), grow_b, left_b, bb, cb, 0,
        (row <= col).astype(F32), (row > col).astype(F32),
    )
    gd_a_out[...] = gd_a[:heads] + decay_local[:, 0:length]
    gd_b_out[...] = gd_b[:heads] + decay_local[:, length:]
    maps = maps_local[...] + jnp.concatenate([gb_a, gc_a, gb_b, gc_b], axis=1)
    rows_out = w_in.shape[0] // n_head
    half = n_head // 2 * rows_out
    own_out[:, half:] = maps
    maps_out[...] = maps.astype(BF16)
    for high in range(n_head // 2):
        part = slice(high * rows_out, (high + 1) * rows_out)
        for away in range(2):
            at = pl.multiple_of((high * 2 + (lax.rem(head, 2) ^ away)) * rows_out, rows_out)
            share = nt(grad_x[...], w_in[pl.ds(at, rows_out), :])
            if away:
                send_out[:, part] = share.astype(BF16)
            else:
                own_out[:, part] = share


def pair_kernel(index, stride, rows_out, maps_at, own, received, received_maps, *refs):
    own_out, send_out, maps_out = refs[-3:]
    me = digit(index(), stride, 2)
    half = maps_at // 2
    maps = own[:, maps_at:] + received_maps[...].astype(F32)
    own_out[:, half:] = maps
    maps_out[...] = maps.astype(BF16)
    for high in range(half // rows_out):
        part = slice(high * rows_out, (high + 1) * rows_out)
        for away in range(2):
            at = pl.multiple_of((high * 2 + (me ^ away)) * rows_out, rows_out)
            total = own[:, pl.ds(at, rows_out)] + received[:, pl.ds(at, rows_out)].astype(F32)
            if away:
                send_out[:, part] = total.astype(BF16)
            else:
                own_out[:, part] = total


def head_kernel(own, other, other_maps, gf_out, *map_outs):
    columns, n = gf_out.shape[1], map_outs[0].shape[1]
    gf_out[...] = (own[:, 0:columns] + other[...].astype(F32)).astype(BF16)
    for k, out in enumerate(map_outs):
        at = columns + k * n
        out[...] = own[:, at : at + n] + other_maps[:, k * n : (k + 1) * n].astype(F32)


def weight_kernel(scale, *refs):
    *parts, out = refs
    total = 0.0
    for part in parts:
        piece = part[...].astype(F32)
        total = total + (jnp.sum(piece, axis=0) if piece.ndim == 3 else piece)
    out[...] = total * scale


def call(kernel, outs, *args, flops=0, scalars=0, held=0):
    specs = [pl.BlockSpec(memory_space=pltpu.SMEM)] * scalars
    specs += [pl.BlockSpec(memory_space=pltpu.HBM)] * held
    specs += [pl.BlockSpec(memory_space=pltpu.VMEM)] * (len(args) - scalars - held)
    outs = list(outs) + [jax.ShapeDtypeStruct(a.shape, a.dtype) for a in args[:held]]
    if held:
        args = tuple(pltpu.with_memory_space_constraint(a, pltpu.HBM) for a in args[:held]) + args[held:]
    bytes_moved = sum(math.prod(a.shape) * a.dtype.itemsize for a in args)
    bytes_moved += sum(math.prod(o.shape) * o.dtype.itemsize for o in outs)
    return pl.pallas_call(
        kernel,
        out_shape=outs,
        in_specs=specs,
        out_specs=[pl.BlockSpec(memory_space=pltpu.VMEM)] * len(outs),
        scratch_shapes=[pltpu.SemaphoreType.DMA((held,))] if held else [],
        cost_estimate=pl.CostEstimate(flops=flops, bytes_accessed=bytes_moved, transcendentals=0),
        compiler_params=pltpu.CompilerParams(vmem_limit_bytes=VMEM_LIMIT),
    )(*args)


def swap(value, axis, mask):
    return lax.ppermute(value, axis, [(i, i ^ mask) for i in range(lax.axis_size(axis))])


def far_first(sends, stride):
    jobs = list(enumerate(sends, start=1))
    return [swap(send, "seq", j * stride) for j, send in reversed(jobs)][::-1]


def local(features, w_in, b_ahead, c_ahead, b_behind, c_behind, decay_ahead, decay_behind, skip_gain, grad_y):
    peers, n_head = lax.axis_size("seq"), lax.axis_size("head")
    length, depth = features.shape
    heads, columns = decay_ahead.shape[0], w_in.shape[1]
    n = b_ahead.shape[1]
    seq_index = lambda: lax.axis_index("seq")
    head_index = lambda: lax.axis_index("head")
    both_index = lambda: (lax.axis_index("seq"), lax.axis_index("head"))
    shape = jax.ShapeDtypeStruct
    square = shape((length, columns), BF16)
    whole = shape((2 * n + GAIN_ROWS, columns), BF16)
    half = shape((n + GAIN_ROWS, columns), BF16)
    prefix = shape((2 * n + 8, columns), F32)

    steps = radices(peers)
    only = len(steps) == 1
    chunk_shapes = [half] * (steps[0] - 1) if only else [whole]
    *gradients, factors, da, db, gy, ca, cb = call(
        functools.partial(gradient_kernel, seq_index, only, columns // heads),
        chunk_shapes + [shape((4, length, columns), F32)],
        decay_ahead, decay_behind, grad_y, c_ahead, c_behind,
        flops=4 * length * n * columns,
        held=5,
    )
    *states, x, ba, bb, fs, wi = call(
        functools.partial(state_kernel, seq_index, only),
        chunk_shapes + [square],
        b_ahead, b_behind, features, w_in, factors,
        flops=2 * length * depth * columns,
        held=4,
    )
    maps = (ba, ca, bb, cb)
    gx_local, maps_local, decay_local, turned = call(
        local_kernel,
        [
            shape((length, columns), F32),
            shape((length, 4 * n), F32),
            shape((heads, 2 * length), F32),
            shape((depth, length), BF16),
        ],
        skip_gain, x, gy, fs, *maps, da, db,
        flops=2 * length * depth * columns,
        scalars=1,
    )
    arrived = []
    for chunk in (gradients, states):
        stride, before = 1, None
        for at, radix in enumerate(steps[:-1]):
            received = [swap(chunk[0], "seq", j * stride) for j in range(1, radix)]
            next_last = at == len(steps) - 2
            following = steps[at + 1]
            before, *chunk = call(
                functools.partial(step_kernel, seq_index, stride, radix, at == 0, next_last, following),
                [prefix] + ([half] * (following - 1) if next_last else [whole]),
                chunk[0], *received, *([] if at == 0 else [before]),
                flops=20 * n * columns,
            )
            stride *= radix
        arrived.append(far_first(chunk, stride) + ([] if only else [before]))
    rows_out, rows_w = depth // n_head, depth // peers
    direct = len(steps) == 2 and rows_w % 16 == 0
    pieces = [shape((2, rows_w, columns), BF16)] * (2 * (steps[0] - 1)) if direct else [shape((depth, columns), BF16)]
    grad_x, *sends = call(
        functools.partial(carry_kernel, seq_index, steps, stride, direct),
        [square] + pieces,
        *arrived[0], turned, ba, bb, gx_local, factors,
        flops=length * depth * columns,
    )
    after = []
    if direct:
        received = [swap(send, "seq", 1 + k % (steps[0] - 1)) for k, send in enumerate(sends)]
        block, block_low = shape((rows_w, columns), F32), shape((rows_w, columns), BF16)
        each = len(received) // 2
        fold = lambda distance, outs, *args: call(
            functools.partial(fold_kernel, seq_index, steps, distance),
            outs, turned, grad_x, *args,
            flops=4 * rows_w * length * columns,
        )
        far = fold(1, [block_low, block_low], *received[:each])
        near = fold(0, [block, block_low], *received[each:], far[0])
        weight_parts = [near[0]] + [
            swap(send, "seq", j * stride) for send, j in ((far[1], 3), (far[0], 2), (near[1], 1))
        ]
        after = [near[0]]
    else:
        weight_parts = [lax.all_to_all(sends[0].reshape(peers, rows_w, columns), "seq", 0, 0)]
    def head_shapes(blocks):
        wide = blocks * rows_out
        return [shape((length, wide + 4 * n), F32), shape((length, wide), BF16), shape((length, 4 * n), BF16)]

    mask, blocks = 2, n_head // 2
    gd_ahead, gd_behind, own_share, *sends = call(
        functools.partial(share_kernel, both_index, steps[-1], stride, only, n_head),
        [shape((heads, length), F32)] * 2 + head_shapes(blocks),
        *arrived[0], *arrived[1], grad_x, x, gy, wi, *maps, maps_local, decay_local, factors,
        flops=3 * length * depth * columns,
    )
    others = [swap(send, "head", 1) for send in sends]
    while mask < n_head:
        own_share, *sends = call(
            functools.partial(pair_kernel, head_index, mask, rows_out, blocks * rows_out),
            head_shapes(blocks // 2),
            own_share, *others, *after,
            flops=4 * length * depth,
        )
        others = [swap(send, "head", mask) for send in sends]
        mask, blocks = mask * 2, blocks // 2
    grad_features, *grad_maps = call(
        head_kernel,
        [shape((length, rows_out), BF16)] + [shape((length, n), F32)] * 4,
        own_share, *others,
    )
    (grad_w_in,) = call(
        functools.partial(weight_kernel, 1.0 / math.sqrt(length * peers)),
        [shape((rows_w, columns), F32)],
        *weight_parts,
    )
    return (grad_features, grad_w_in, *grad_maps, gd_ahead, gd_behind)


def solution(mesh):
    in_specs = (
        P("seq", None),
        P(None, "head"),
        P("seq", None),
        P("seq", None),
        P("seq", None),
        P("seq", None),
        P("head", "seq"),
        P("head", "seq"),
        P("head"),
        P("seq", "head"),
    )
    out_specs = (
        P("seq", "head"),
        P("seq", "head"),
        P("seq", None),
        P("seq", None),
        P("seq", None),
        P("seq", None),
        P("head", "seq"),
        P("head", "seq"),
    )
    return jax.shard_map(local, mesh=mesh, in_specs=in_specs, out_specs=out_specs, check_vma=False)
```

time: 48.3 us -> 42.4 us (0.88)
  waiting for transfers between devices: 25.7 us -> 9.77 us
  starting transfers between devices: 14.6 us -> 22.3 us
  Pallas kernels: 6.9 us -> 8.73 us
  local copies, waits for them, and re-layouts: 0.06 us -> 0.65 us
    ppermute x7 -> x17, waiting for transfers between devices: 23.9 us -> 9.77 us  [swap(): lax.ppermute(value, axis, [(i, i ^ mask) for i in range(lax.axis_size(axi...]
    ppermute x7 -> x17, starting transfers between devices: 9.34 us -> 22.3 us  [swap(): lax.ppermute(value, axis, [(i, i ^ mask) for i in range(lax.axis_size(axi...]
    all_to_all x1 -> x0, starting transfers between devices: 5.29 us -> none  [local(): w_shares = lax.all_to_all(w_shares, 'seq', 0, 0)]
    pallas_call x5 -> x12, Pallas kernels: 6.9 us -> 8.73 us  [call(): pl.pallas_call(kernel, out_shape=outs, in_specs=specs, out_specs=[pl.Bloc...]
    all_to_all x1 -> x0, waiting for transfers between devices: 1.75 us -> none  [local(): w_shares = lax.all_to_all(w_shares, 'seq', 0, 0)]
    unnamed x20 -> x2, local copies, waits for them, and re-layouts: 0.06 us -> 0.65 us
  transfers between devices with their start and end apart: 8 -> 17, of which waited for: 6 -> 6; matrix products, arithmetic and copies ran while one was open for 0% -> 0% of each run, Pallas kernels for 4% -> 16%
where the time goes in v3:
time: 42.4 us; the launch traced here: 42.2 us
  starting transfers between devices  22.3 us (53%)
  waiting for transfers between devices  9.77 us (23%)
  Pallas kernels  8.73 us (21%)
  between operations  0.74 us (2%)
  local copies, waits for them, and re-layouts  0.65 us (2%)
    ppermute x17, starting transfers between devices, swap(): lax.ppermute(value, axis, [(i, i ^ mask) for i in range(lax.axis_size(axi...  22.3 us
    ppermute x17, waiting for transfers between devices, swap(): lax.ppermute(value, axis, [(i, i ^ mask) for i in range(lax.axis_size(axi...  9.77 us
    pallas_call x12, Pallas kernels, call(): pl.pallas_call(kernel, out_shape=outs, in_specs=specs, out_specs=[pl.Bloc...  8.73 us
  transfers between devices with their start and end apart: 17, of which 6 were waited for; matrix products, arithmetic and copies ran while one was open for 0% of the time, Pallas kernels for 16%

profile of v3, /device:TPU:0, one launch (start us, length us, event | category | flops | bytes accessed | tf_op | source)
XLA Modules:
  0.0 42.2 jit_solution(8875075257889053218)
XLA Ops:
  0.6 1.3 %shard_map.161 = (bf16[272,256]{1,0:T(8,128)(2,1)S(1)}, f32[4,128,256]{2,1,0:T(8,128)S(1)}, f32[4,128]{1,0:T(4,128)S(1)}, f32[4,128]{1,0:T(4,128)S(1)}, bf16[128...) custom-call(f32[4,128]{1,0:T(4,128)} %refs_0_.2, f32[4,128]{1,0:T(4,128)} %refs_1_.2, ...), custom_call_target="tpu_custom_call" | custom-call | flops 16777216 | bytes 933888 | tf_op jit(solution)/shard_map/pallas_call | solution.py:431
  2.0 3.0 %collective-permute-start = (bf16[272,256]{1,0:T(8,128)(2,1)S(1)}, bf16[272,256]{1,0:T(8,128)(2,1)S(1)}, u32[]{:S(2)}, u32[]{:S(2)}) collective-permute-start(bf16[272,256]{1,0:T(8,128)(2,1)S(1)} %get-tuple-element.53.refs_0_), channel_id=1, source_target_pairs={{0,4},{4,0},{8,12},{12,8},{16,20},{20,16},{24,28},{28,24},{1,5},{5... | collective-permute-start | bytes 417800 | tf_op jit(solution)/shard_map/ppermute | solution.py:443
  5.0 1.7 %shard_map.163 = (bf16[272,256]{1,0:T(8,128)(2,1)S(1)}, bf16[128,256]{1,0:T(8,128)(2,1)S(1)}, bf16[128,128]{1,0:T(8,128)(2,1)S(1)}, bf16[128,128]{1,0:T(8,128)(2...) custom-call(bf16[128,128]{1,0:T(8,128)(2,1)} %refs_0_.3, bf16[128,128]{1,0:T(8,128)(2,1)} %refs_1_.3, ...), custom_call_target="tpu_custom_call" | custom-call | flops 67108864 | bytes 2433024 | tf_op jit(solution)/shard_map/pallas_call | solution.py:431
  6.8 2.3 %collective-permute-done.refs_1_ = bf16[272,256]{1,0:T(8,128)(2,1)S(1)} collective-permute-done((bf16[272,256]{1,0:T(8,128)(2,1)S(1)}, bf16[272,256]{1,0:T(8,128)(2,1)S(1)}, u32[]{:S(2)}, u32[]{:S(2)}) %collective-permute-start) | collective-permute-done | bytes 139296 | tf_op jit(solution)/shard_map/ppermute | solution.py:443
  9.2 1.6 %collective-permute-start.1 = (bf16[144,256]{1,0:T(8,128)(2,1)S(1)}, bf16[144,256]{1,0:T(8,128)(2,1)S(1)}, u32[]{:S(2)}, u32[]{:S(2)}) collective-permute-start(bf16[144,256]{1,0:T(8,128)(2,1)S(1)} %get-tuple-element.54), channel_id=1, source_target_pairs={{0,8},{4,12},{8,0},{12,4},{16,24},{20,28},{24,16},{28,20},{1,9},{5... | collective-permute-start | bytes 221192 | tf_op jit(solution)/shard_map/ppermute | solution.py:443
  10.8 2.6 %collective-permute-start.2 = (bf16[144,256]{1,0:T(8,128)(2,1)S(1)}, bf16[144,256]{1,0:T(8,128)(2,1)S(1)}, u32[]{:S(2)}, u32[]{:S(2)}) collective-permute-start(bf16[144,256]{1,0:T(8,128)(2,1)S(1)} %get-tuple-element.55), channel_id=1, source_target_pairs={{0,16},{4,20},{8,24},{12,28},{16,0},{20,4},{24,8},{28,12},{1,17},{... | collective-permute-start | bytes 221192 | tf_op jit(solution)/shard_map/ppermute | solution.py:443
  13.8 0.7 %collective-permute-start.5 = (bf16[144,256]{1,0:T(8,128)(2,1)S(1)}, bf16[144,256]{1,0:T(8,128)(2,1)S(1)}, u32[]{:S(2)}, u32[]{:S(2)}) collective-permute-start(bf16[144,256]{1,0:T(8,128)(2,1)S(1)} %get-tuple-element.60), channel_id=1, source_target_pairs={{0,8},{4,12},{8,0},{12,4},{16,24},{20,28},{24,16},{28,20},{1,9},{5... | collective-permute-start | bytes 221192 | tf_op jit(solution)/shard_map/ppermute | solution.py:443
  14.4 3.5 %collective-permute-start.6 = (bf16[144,256]{1,0:T(8,128)(2,1)S(1)}, bf16[144,256]{1,0:T(8,128)(2,1)S(1)}, u32[]{:S(2)}, u32[]{:S(2)}) collective-permute-start(bf16[144,256]{1,0:T(8,128)(2,1)S(1)} %get-tuple-element.61), channel_id=1, source_target_pairs={{0,16},{4,20},{8,24},{12,28},{16,0},{20,4},{24,8},{28,12},{1,17},{... | collective-permute-start | bytes 221192 | tf_op jit(solution)/shard_map/ppermute | solution.py:443
  18.2 0.7 %copy-done = f32[4]{0:T(128)S(1)} copy-done((f32[4]{0:T(128)S(1)}, f32[4]{0:T(128)}, u32[]{:S(2)}) %copy-start) | copy-done | bytes 40
  18.9 1.5 %shard_map.165 = (f32[128,256]{1,0:T(8,128)S(1)}, f32[128,512]{1,0:T(8,128)S(1)}, f32[4,256]{1,0:T(4,128)S(1)}, bf16[1024,128]{1,0:T(8,128)(2,1)S(1)}) custom-call(f32[4]{0:T(128)S(1)} %copy-done, bf16[128,256]{1,0:T(8,128)(2,1)S(1)} %get-tuple-element.64.x.refs_9_, bf16[128,256]{1,0:T(8,128)(2,1)S(1)} %get-tuple-element.65.gy.refs_10_, ...), custom_call_target="tpu_custom_call" | custom-call | flops 67108864 | bytes 1187856 | tf_op jit(solution)/shard_map/pallas_call | solution.py:431
  20.4 0.5 %shard_map.166 = (bf16[128,256]{1,0:T(8,128)(2,1)S(1)}, bf16[2,128,256]{2,1,0:T(8,128)(2,1)S(1)}, bf16[2,128,256]{2,1,0:T(8,128)(2,1)S(1)}) custom-call(bf16[144,256]{1,0:T(8,128)(2,1)S(1)} %collective-permute-done.1.refs_0_, bf16[144,256]{1,0:T(8,128)(2,1)S(1)} %collective-permute-done.2.refs_1_, bf16[144,256]{1,0:T(8,128)(2,1)S(1)} %collective-permute-done.3.refs_2_, ...), custom_call_target="tpu_custom_call" | custom-call | flops 33554432 | bytes 1802240 | tf_op jit(solution)/shard_map/pallas_call | solution.py:431
  20.9 3.7 %collective-permute-start.11 = (bf16[2,128,256]{2,1,0:T(8,128)(2,1)S(1)}, bf16[2,128,256]{2,1,0:T(8,128)(2,1)S(1)}, u32[]{:S(2)}, u32[]{:S(2)}) collective-permute-start(bf16[2,128,256]{2,1,0:T(8,128)(2,1)S(1)} %get-tuple-element.83), channel_id=1, source_target_pairs={{0,4},{4,0},{8,12},{12,8},{16,20},{20,16},{24,28},{28,24},{1,5},{5... | collective-permute-start | bytes 393224 | tf_op jit(solution)/shard_map/ppermute | solution.py:443
  24.7 1.7 %shard_map.167 = (f32[4,128]{1,0:T(4,128)}, f32[4,128]{1,0:T(4,128)}, f32[128,1024]{1,0:T(8,128)S(1)}, bf16[128,512]{1,0:T(8,128)(2,1)S(1)}, bf16[128,512]{1,0:T(8,128)(2,1)S(1)}) custom-call(bf16[144,256]{1,0:T(8,128)(2,1)S(1)} %collective-permute-done.1.refs_0_, bf16[144,256]{1,0:T(8,128)(2,1)S(1)} %collective-permute-done.2.refs_1_, ...), custom_call_target="tpu_custom_call" | custom-call | flops 100663296 | bytes 3416064 | tf_op jit(solution)/shard_map/pallas_call | solution.py:431
  26.4 0.5 %collective-permute-start.9 = (bf16[128,512]{1,0:T(8,128)(2,1)S(1)}, bf16[128,512]{1,0:T(8,128)(2,1)S(1)}, u32[]{:S(2)}, u32[]{:S(2)}) collective-permute-start(bf16[128,512]{1,0:T(8,128)(2,1)S(1)} %get-tuple-element.81), channel_id=1, source_target_pairs={{0,1},{1,0},{2,3},{3,2},{4,5},{5,4},{6,7},{7,6},{8,9},{9,8},{10,11... | collective-permute-start | bytes 393224 | tf_op jit(solution)/shard_map/ppermute | solution.py:443
  26.9 0.6 %collective-permute-done.11.refs_0_ = bf16[2,128,256]{2,1,0:T(8,128)(2,1)S(1)} collective-permute-done((bf16[2,128,256]{2,1,0:T(8,128)(2,1)S(1)}, bf16[2,128,256]{2,1,0:T(8,128)(2,1)S(1)}, u32[]{:S(2)}, u32[]{:S(2)}) %collective-permute-start.11) | collective-permute-done | bytes 131104 | tf_op jit(solution)/shard_map/ppermute | solution.py:443
  27.7 1.8 %collective-permute-done.10.refs_0_ = bf16[2,128,256]{2,1,0:T(8,128)(2,1)S(1)} collective-permute-done((bf16[2,128,256]{2,1,0:T(8,128)(2,1)S(1)}, bf16[2,128,256]{2,1,0:T(8,128)(2,1)S(1)}, u32[]{:S(2)}, u32[]{:S(2)}) %collective-permute-start.10) | collective-permute-done | bytes 131104 | tf_op jit(solution)/shard_map/ppermute | solution.py:443
  29.8 1.6 %collective-permute-start.13 = (bf16[128,512]{1,0:T(8,128)(2,1)S(1)}, bf16[128,512]{1,0:T(8,128)(2,1)S(1)}, u32[]{:S(2)}, u32[]{:S(2)}) collective-permute-start(bf16[128,512]{1,0:T(8,128)(2,1)S(1)} %get-tuple-element.88), channel_id=1, source_target_pairs={{0,2},{1,3},{2,0},{3,1},{4,6},{5,7},{6,4},{7,5},{8,10},{9,11},{10,... | collective-permute-start | bytes 393224 | tf_op jit(solution)/shard_map/ppermute | solution.py:443
  31.4 1.9 %collective-permute-start.16 = (bf16[128,256]{1,0:T(8,128)(2,1)S(1)}, bf16[128,256]{1,0:T(8,128)(2,1)S(1)}, u32[]{:S(2)}, u32[]{:S(2)}) collective-permute-start(bf16[128,256]{1,0:T(8,128)(2,1)S(1)} %get-tuple-element.91), channel_id=1, source_target_pairs={{0,8},{4,12},{8,0},{12,4},{16,24},{20,28},{24,16},{28,20},{1,9},{5... | collective-permute-start | bytes 196616 | tf_op jit(solution)/shard_map/ppermute | solution.py:443
  33.3 2.0 %collective-permute-start.14 = (bf16[128,256]{1,0:T(8,128)(2,1)S(1)}, bf16[128,256]{1,0:T(8,128)(2,1)S(1)}, u32[]{:S(2)}, u32[]{:S(2)}) collective-permute-start(bf16[128,256]{1,0:T(8,128)(2,1)S(1)} %get-tuple-element.90), channel_id=1, source_target_pairs={{0,24},{4,28},{8,16},{12,20},{16,8},{20,12},{24,0},{28,4},{1,25},{... | collective-permute-start | bytes 196616 | tf_op jit(solution)/shard_map/ppermute | solution.py:443
  35.3 0.5 %collective-permute-start.12 = (bf16[128,256]{1,0:T(8,128)(2,1)S(1)}, bf16[128,256]{1,0:T(8,128)(2,1)S(1)}, u32[]{:S(2)}, u32[]{:S(2)}) collective-permute-start(bf16[128,256]{1,0:T(8,128)(2,1)S(1)} %get-tuple-element.87), channel_id=1, source_target_pairs={{0,2},{1,3},{2,0},{3,1},{4,6},{5,7},{6,4},{7,5},{8,10},{9,11},{10,... | collective-permute-start | bytes 196616 | tf_op jit(solution)/shard_map/ppermute | solution.py:443
  35.9 3.5 %collective-permute-done.14.refs_1_ = bf16[128,256]{1,0:T(8,128)(2,1)S(1)} collective-permute-done((bf16[128,256]{1,0:T(8,128)(2,1)S(1)}, bf16[128,256]{1,0:T(8,128)(2,1)S(1)}, u32[]{:S(2)}, u32[]{:S(2)}) %collective-permute-start.14) | collective-permute-done | bytes 65568 | tf_op jit(solution)/shard_map/ppermute | solution.py:443
  39.4 1.4 %collective-permute-done.15.refs_2_ = bf16[128,256]{1,0:T(8,128)(2,1)S(1)} collective-permute-done((bf16[128,256]{1,0:T(8,128)(2,1)S(1)}, bf16[128,256]{1,0:T(8,128)(2,1)S(1)}, u32[]{:S(2)}, u32[]{:S(2)}) %collective-permute-start.15) | collective-permute-done | bytes 65568 | tf_op jit(solution)/shard_map/ppermute | solution.py:443
  40.8 0.7 %shard_map.172 = f32[128,256]{1,0:T(8,128)} custom-call(f32[128,256]{1,0:T(8,128)S(1)} %get-tuple-element.85.refs_0_, bf16[128,256]{1,0:T(8,128)(2,1)S(1)} %collective-permute-done.14.refs_1_, bf16[128,256]{1,0:T(8,128)(2,1)S(1)} %collective-permute-done.15.refs_2_, bf16[128,256]{1,0:T(8,128)(2,1)S(1)} %collective-permute-done.16.refs_3_), custom_call_target="tpu_custom_call" | custom-call | bytes 458752 | tf_op jit(solution)/shard_map/pallas_call | solution.py:431
  41.5 0.7 %shard_map.171 = (bf16[128,256]{1,0:T(8,128)(2,1)}, f32[128,128]{1,0:T(8,128)}, f32[128,128]{1,0:T(8,128)}, f32[128,128]{1,0:T(8,128)}, f32[128,128]{1,0:T(8,128)}) custom-call(f32[128,768]{1,0:T(8,128)S(1)} %get-tuple-element.86.own, bf16[128,256]{1,0:T(8,128)(2,1)S(1)} %collective-permute-done.12.other, bf16[128,512]{1,0:T(8,128)(2,1)S(1)} %collective-permute-done.13.other_maps), custom_call_target="tpu_custom_call" | custom-call | bytes 917504 | tf_op jit(solution)/shard_map/pallas_call | solution.py:431
  (24 shorter events, 1.5 us)
Async XLA Ops:
  2.0 7.1 %collective-permute-start = (bf16[272,256]{1,0:T(8,128)(2,1)S(1)}, bf16[272,256]{1,0:T(8,128)(2,1)S(1)}, u32[]{:S(2)}, u32[]{:S(2)}) collective-permute-start(bf16[272,256]{1,0:T(8,128)(2,1)S(1)} %get-tuple-element.53.refs_0_), channel_id=1, source_target_pairs={{0,4},{4,0},{8,12},{12,8},{16,20},{20,16},{24,28},{28,24},{1,5},{5... | collective-permute-start | bytes 417800 | tf_op jit(solution)/shard_map/ppermute | solution.py:443
  6.7 7.0 %collective-permute-start.4 = (bf16[272,256]{1,0:T(8,128)(2,1)S(1)}, bf16[272,256]{1,0:T(8,128)(2,1)S(1)}, u32[]{:S(2)}, u32[]{:S(2)}) collective-permute-start(bf16[272,256]{1,0:T(8,128)(2,1)S(1)} %get-tuple-element.59.refs_0_), channel_id=1, source_target_pairs={{0,4},{4,0},{8,12},{12,8},{16,20},{20,16},{24,28},{28,24},{1,5},{5... | collective-permute-start | bytes 417800 | tf_op jit(solution)/shard_map/ppermute | solution.py:443
  9.2 8.7 %collective-permute-start.1 = (bf16[144,256]{1,0:T(8,128)(2,1)S(1)}, bf16[144,256]{1,0:T(8,128)(2,1)S(1)}, u32[]{:S(2)}, u32[]{:S(2)}) collective-permute-start(bf16[144,256]{1,0:T(8,128)(2,1)S(1)} %get-tuple-element.54), channel_id=1, source_target_pairs={{0,8},{4,12},{8,0},{12,4},{16,24},{20,28},{24,16},{28,20},{1,9},{5... | collective-permute-start | bytes 221192 | tf_op jit(solution)/shard_map/ppermute | solution.py:443
  10.8 9.6 %collective-permute-start.2 = (bf16[144,256]{1,0:T(8,128)(2,1)S(1)}, bf16[144,256]{1,0:T(8,128)(2,1)S(1)}, u32[]{:S(2)}, u32[]{:S(2)}) collective-permute-start(bf16[144,256]{1,0:T(8,128)(2,1)S(1)} %get-tuple-element.55), channel_id=1, source_target_pairs={{0,16},{4,20},{8,24},{12,28},{16,0},{20,4},{24,8},{28,12},{1,17},{... | collective-permute-start | bytes 221192 | tf_op jit(solution)/shard_map/ppermute | solution.py:443
  13.4 7.0 %collective-permute-start.3 = (bf16[144,256]{1,0:T(8,128)(2,1)S(1)}, bf16[144,256]{1,0:T(8,128)(2,1)S(1)}, u32[]{:S(2)}, u32[]{:S(2)}) collective-permute-start(bf16[144,256]{1,0:T(8,128)(2,1)S(1)} %get-tuple-element.56), channel_id=1, source_target_pairs={{0,24},{4,28},{8,16},{12,20},{16,8},{20,12},{24,0},{28,4},{1,25},{... | collective-permute-start | bytes 221192 | tf_op jit(solution)/shard_map/ppermute | solution.py:443
  13.8 10.9 %collective-permute-start.5 = (bf16[144,256]{1,0:T(8,128)(2,1)S(1)}, bf16[144,256]{1,0:T(8,128)(2,1)S(1)}, u32[]{:S(2)}, u32[]{:S(2)}) collective-permute-start(bf16[144,256]{1,0:T(8,128)(2,1)S(1)} %get-tuple-element.60), channel_id=1, source_target_pairs={{0,8},{4,12},{8,0},{12,4},{16,24},{20,28},{24,16},{28,20},{1,9},{5... | collective-permute-start | bytes 221192 | tf_op jit(solution)/shard_map/ppermute | solution.py:443
  14.4 10.3 %collective-permute-start.6 = (bf16[144,256]{1,0:T(8,128)(2,1)S(1)}, bf16[144,256]{1,0:T(8,128)(2,1)S(1)}, u32[]{:S(2)}, u32[]{:S(2)}) collective-permute-start(bf16[144,256]{1,0:T(8,128)(2,1)S(1)} %get-tuple-element.61), channel_id=1, source_target_pairs={{0,16},{4,20},{8,24},{12,28},{16,0},{20,4},{24,8},{28,12},{1,17},{... | collective-permute-start | bytes 221192 | tf_op jit(solution)/shard_map/ppermute | solution.py:443
  17.9 6.8 %collective-permute-start.7 = (bf16[144,256]{1,0:T(8,128)(2,1)S(1)}, bf16[144,256]{1,0:T(8,128)(2,1)S(1)}, u32[]{:S(2)}, u32[]{:S(2)}) collective-permute-start(bf16[144,256]{1,0:T(8,128)(2,1)S(1)} %get-tuple-element.62), channel_id=1, source_target_pairs={{0,24},{4,28},{8,16},{12,20},{16,8},{20,12},{24,0},{28,4},{1,25},{... | collective-permute-start | bytes 221192 | tf_op jit(solution)/shard_map/ppermute | solution.py:443
  18.2 0.7 %copy-start = (f32[4]{0:T(128)S(1)}, f32[4]{0:T(128)}, u32[]{:S(2)}) copy-start(f32[4]{0:T(128)} %skip.1) | copy-start | bytes 52
  20.9 6.6 %collective-permute-start.11 = (bf16[2,128,256]{2,1,0:T(8,128)(2,1)S(1)}, bf16[2,128,256]{2,1,0:T(8,128)(2,1)S(1)}, u32[]{:S(2)}, u32[]{:S(2)}) collective-permute-start(bf16[2,128,256]{2,1,0:T(8,128)(2,1)S(1)} %get-tuple-element.83), channel_id=1, source_target_pairs={{0,4},{4,0},{8,12},{12,8},{16,20},{20,16},{24,28},{28,24},{1,5},{5... | collective-permute-start | bytes 393224 | tf_op jit(solution)/shard_map/ppermute | solution.py:443
  24.6 5.0 %collective-permute-start.10 = (bf16[2,128,256]{2,1,0:T(8,128)(2,1)S(1)}, bf16[2,128,256]{2,1,0:T(8,128)(2,1)S(1)}, u32[]{:S(2)}, u32[]{:S(2)}) collective-permute-start(bf16[2,128,256]{2,1,0:T(8,128)(2,1)S(1)} %get-tuple-element.82), channel_id=1, source_target_pairs={{0,4},{4,0},{8,12},{12,8},{16,20},{20,16},{24,28},{28,24},{1,5},{5... | collective-permute-start | bytes 393224 | tf_op jit(solution)/shard_map/ppermute | solution.py:443
  26.4 3.3 %collective-permute-start.8 = (bf16[128,512]{1,0:T(8,128)(2,1)S(1)}, bf16[128,512]{1,0:T(8,128)(2,1)S(1)}, u32[]{:S(2)}, u32[]{:S(2)}) collective-permute-start(bf16[128,512]{1,0:T(8,128)(2,1)S(1)} %get-tuple-element.80), channel_id=1, source_target_pairs={{0,1},{1,0},{2,3},{3,2},{4,5},{5,4},{6,7},{7,6},{8,9},{9,8},{10,11... | collective-permute-start | bytes 393224 | tf_op jit(solution)/shard_map/ppermute | solution.py:443
  26.4 3.3 %collective-permute-start.9 = (bf16[128,512]{1,0:T(8,128)(2,1)S(1)}, bf16[128,512]{1,0:T(8,128)(2,1)S(1)}, u32[]{:S(2)}, u32[]{:S(2)}) collective-permute-start(bf16[128,512]{1,0:T(8,128)(2,1)S(1)} %get-tuple-element.81), channel_id=1, source_target_pairs={{0,1},{1,0},{2,3},{3,2},{4,5},{5,4},{6,7},{7,6},{8,9},{9,8},{10,11... | collective-permute-start | bytes 393224 | tf_op jit(solution)/shard_map/ppermute | solution.py:443
  29.8 11.6 %collective-permute-start.13 = (bf16[128,512]{1,0:T(8,128)(2,1)S(1)}, bf16[128,512]{1,0:T(8,128)(2,1)S(1)}, u32[]{:S(2)}, u32[]{:S(2)}) collective-permute-start(bf16[128,512]{1,0:T(8,128)(2,1)S(1)} %get-tuple-element.88), channel_id=1, source_target_pairs={{0,2},{1,3},{2,0},{3,1},{4,6},{5,7},{6,4},{7,5},{8,10},{9,11},{10,... | collective-permute-start | bytes 393224 | tf_op jit(solution)/shard_map/ppermute | solution.py:443
  31.4 4.5 %collective-permute-start.16 = (bf16[128,256]{1,0:T(8,128)(2,1)S(1)}, bf16[128,256]{1,0:T(8,128)(2,1)S(1)}, u32[]{:S(2)}, u32[]{:S(2)}) collective-permute-start(bf16[128,256]{1,0:T(8,128)(2,1)S(1)} %get-tuple-element.91), channel_id=1, source_target_pairs={{0,8},{4,12},{8,0},{12,4},{16,24},{20,28},{24,16},{28,20},{1,9},{5... | collective-permute-start | bytes 196616 | tf_op jit(solution)/shard_map/ppermute | solution.py:443
  33.3 6.1 %collective-permute-start.14 = (bf16[128,256]{1,0:T(8,128)(2,1)S(1)}, bf16[128,256]{1,0:T(8,128)(2,1)S(1)}, u32[]{:S(2)}, u32[]{:S(2)}) collective-permute-start(bf16[128,256]{1,0:T(8,128)(2,1)S(1)} %get-tuple-element.90), channel_id=1, source_target_pairs={{0,24},{4,28},{8,16},{12,20},{16,8},{20,12},{24,0},{28,4},{1,25},{... | collective-permute-start | bytes 196616 | tf_op jit(solution)/shard_map/ppermute | solution.py:443
  35.3 5.5 %collective-permute-start.15 = (bf16[128,256]{1,0:T(8,128)(2,1)S(1)}, bf16[128,256]{1,0:T(8,128)(2,1)S(1)}, u32[]{:S(2)}, u32[]{:S(2)}) collective-permute-start(bf16[128,256]{1,0:T(8,128)(2,1)S(1)} %get-tuple-element.84.refs_1_), channel_id=1, source_target_pairs={{0,16},{4,20},{8,24},{12,28},{16,0},{20,4},{24,8},{28,12},{1,17},{... | collective-permute-start | bytes 196616 | tf_op jit(solution)/shard_map/ppermute | solution.py:443
  35.3 6.1 %collective-permute-start.12 = (bf16[128,256]{1,0:T(8,128)(2,1)S(1)}, bf16[128,256]{1,0:T(8,128)(2,1)S(1)}, u32[]{:S(2)}, u32[]{:S(2)}) collective-permute-start(bf16[128,256]{1,0:T(8,128)(2,1)S(1)} %get-tuple-element.87), channel_id=1, source_target_pairs={{0,2},{1,3},{2,0},{3,1},{4,6},{5,7},{6,4},{7,5},{8,10},{9,11},{10,... | collective-permute-start | bytes 196616 | tf_op jit(solution)/shard_map/ppermute | solution.py:443

commit v4 on v3

--- a/solution.py
+++ b/solution.py
@@ -12,6 +12,7 @@
 BF16 = jnp.bfloat16
 HIGH = lax.Precision.HIGHEST
 GAIN_ROWS = 16
+FLOPS_PER_MICRO = 1.15e9
 VMEM_LIMIT = 48 * 1024 * 1024
 
 
@@ -141,9 +142,9 @@
 
 def gradient_kernel(me, last, width, *refs):
     *refs, sems = refs
-    sources, outs, held = refs[:5], refs[5:-5], refs[-5:]
+    sources, outs, held = refs[:6], refs[6:-6], refs[-6:]
     copies = start_copies(sources, held, sems)
-    da, db, gy, ca, cb = held
+    da, db, gy, ca, cb, _ = held
     for copy in copies[:2]:
         copy.wait()
     factors = decay_factors(da[...], db[...], width)
@@ -179,8 +180,8 @@
     refs = list(refs)
     own = refs.pop(0)
     received = [refs.pop(0) for _ in range(radix - 1)]
-    before = None if first else refs.pop(0)
-    pre_out = refs.pop(0)
+    before, outs = refs[0], refs[-(next_radix if next_last else 2) :]
+    pre_out, *outs = outs
     n = (own.shape[0] - GAIN_ROWS) // 2
     seq = index()
     me = digit(seq, stride, radix)
@@ -209,7 +210,7 @@
         totals.append(group)
     pre_out[2 * n :] = jnp.concatenate(new_grow + [jnp.zeros((6, width), F32)], axis=0)
     gain = [functools.reduce(lambda a, b: a * b, gains[k]) for k in range(2)]
-    write_chunk(refs, lambda: digit(seq, stride * radix, next_radix), next_last, *totals, *gain)
+    write_chunk(outs, lambda: digit(seq, stride * radix, next_radix), next_last, *totals, *gain)
 
 
 def local_kernel(
@@ -247,7 +248,7 @@
         score_grad = nt(x[:, part], gy[:, part])
         weighted = score_grad * decay
         weight_sum = weight_sum + weighted
-        gx_out[:, part] = nn((decay * affinity).astype(BF16), gy[:, part]) + skip[h] * gy[:, part].astype(F32)
+        gx_out[:, part] = nn((decay * affinity).astype(BF16), gy[:, part]) + skip[:, h : h + 1] * gy[:, part].astype(F32)
         pieces = nn((weighted * affinity).astype(BF16), counts)
         totals.append(jnp.sum(pieces * cross, axis=0, keepdims=True))
     for h in range(heads):
@@ -261,10 +262,12 @@
     turned_out[...] = features[...].T
 
 
-def entering(chunks, me, radix, n):
-    members = [me ^ j for j in range(radix)]
+def entering(chunks, seq, peers, n):
     results = []
     for received, before in chunks:
+        radix = len(received) + 1
+        me = digit(seq, peers // radix, radix)
+        members = [me ^ j for j in range(radix)]
         gains = [read_gain(ref[n:]) for ref in received]
         gains = gains[:1] + gains
         coefficients = merge_coefficients(me, members, gains, gains)
@@ -281,9 +284,9 @@
     return results
 
 
-def take_chunks(refs, radix, first, count):
+def take_chunks(refs, lasts, first):
     chunks = []
-    for _ in range(count):
+    for radix in lasts:
         received = [refs.pop(0) for _ in range(radix - 1)]
         chunks.append((received, None if first else refs.pop(0)))
     return chunks
@@ -291,92 +294,69 @@
 
 def carry_kernel(index, steps, stride, direct, *refs):
     refs = list(refs)
-    chunks = take_chunks(refs, steps[-1], len(steps) == 1, 1)
-    turned, ba, bb, gx_local, factors, gx_out = [refs.pop(0) for _ in range(6)]
+    chunks = take_chunks(refs, steps[-1:], len(steps) == 1)
+    turned, ba, bb, gx_local, factors = refs[:5]
+    gx_out, grad_out, *outs = refs[-steps[0] - 1 :] if direct else refs[-3:]
     seq = index()
     me = digit(seq, stride, steps[-1])
-    (gradient,) = entering(chunks, me, steps[-1], ba.shape[1])
+    (gradient,) = entering(chunks, seq, stride * steps[-1], ba.shape[1])
     grad_x = gx_local[...]
-    for b, grad, left in ((ba, gradient(1), factors[1]), (bb, gradient(0), factors[3])):
-        grad_x = grad_x + nn(b[...], grad.astype(BF16)).astype(BF16).astype(F32) * left
+    for k, (b, left) in enumerate(((ba, factors[1]), (bb, factors[3]))):
+        grad = gradient(1 - k).astype(BF16)
+        grad_out[k] = grad
+        grad_x = grad_x + nn(b[...], grad).astype(BF16).astype(F32) * left
     grad_x = grad_x.astype(BF16)
     gx_out[...] = grad_x
     if not direct:
-        refs.pop(0)[...] = nn(turned[...], grad_x).astype(BF16)
+        outs[0][...] = nn(turned[...], grad_x).astype(BF16)
         return
-    rows = refs[0].shape[1]
-    for far in (1, 0):
-        for j in range(1, steps[0]):
-            out = refs.pop(0)
-            for k in range(2):
-                at = (me ^ (2 * far + k)) * steps[0] + (digit(seq, 1, steps[0]) ^ j)
-                at = pl.multiple_of(at * rows, rows)
-                out[k] = nn(turned[pl.ds(at, rows), :], grad_x).astype(BF16)
-
-
-def fold_kernel(index, steps, far, turned, grad_x, *refs):
-    received, outs = refs[: steps[0] - 1], refs[-2:]
+    rows = outs[0].shape[1]
+    for j, out in enumerate(outs, start=1):
+        for k in range(4):
+            at = (me ^ k) * steps[0] + (digit(seq, 1, steps[0]) ^ j)
+            out[k] = nn(turned[pl.ds(pl.multiple_of(at * rows, rows), rows), :], grad_x).astype(BF16)
+
+
+def fold_kernel(index, steps, turned, grad_x, *refs):
+    received, outs = refs[: steps[0] - 1], refs[-4:]
     rows = received[0].shape[1]
     seq = index()
-    for k in range(2):
-        at = (digit(seq, steps[0], steps[1]) ^ (2 * far + k)) * steps[0] + digit(seq, 1, steps[0])
+    for k in range(4):
+        at = (digit(seq, steps[0], steps[1]) ^ k) * steps[0] + digit(seq, 1, steps[0])
         share = nn(turned[pl.ds(pl.multiple_of(at * rows, rows), rows), :], grad_x[...])
         total = sum([ref[k].astype(F32) for ref in received], share)
         outs[k][...] = total.astype(outs[k].dtype)
 
 
-def share_kernel(index, radix, stride, first, n_head, *refs):
-    refs = list(refs)
-    chunks = take_chunks(refs, radix, first, 2)
-    grad_x, x, gy, w_in, ba, ca, bb, cb = [refs.pop(0) for _ in range(8)]
-    maps_local, decay_local, factors = [refs.pop(0) for _ in range(3)]
-    gd_a_out, gd_b_out, own_out, send_out, maps_out = refs
+def head_groups(heads, columns):
+    rows, cols = iotas(8, columns)
+    return (lax.div(cols, columns // heads) == rows).astype(BF16)
+
+
+def share_kernel(index, n_head, grad_x, grads, x, w_in, ba, bb, maps_local, decay_local, factors, *outs):
+    decay_out, own_out, send_out = outs
     heads = decay_local.shape[0]
     n = ba.shape[1]
     length, columns = x.shape
-    width = columns // heads
-    seq, head = index()
-    gradient, state = entering(chunks, digit(seq, stride, radix), radix, n)
-    grow_a, left_a, grow_b, left_b = [factors[k] for k in range(4)]
-    xf, gyf = x[...].astype(F32), gy[...].astype(F32)
+    xf = x[...].astype(F32)
     row, col = iotas(length, length)
-    own_rows, own_cols = iotas(8, columns)
-    group = (lax.div(own_cols, width) == own_rows).astype(BF16)
-    frame = lax.broadcasted_iota(jnp.int32, (length, 1), 0)
-
-    def direction(state, grad, grow, left, b, c, at_end, later, earlier):
-        gain = jnp.sum(jnp.where(frame == at_end, grow, 0.0), axis=0, keepdims=True)
-        state_low, grad_low = state.astype(BF16), grad.astype(BF16)
-        carried = grow * nn(c[...], state_low)
-        through = gain * jnp.sum(state * grad, axis=0, keepdims=True)
-        read = gyf * carried + jnp.where(frame == at_end, through, 0.0)
-        write = nn(b[...], grad_low).astype(BF16).astype(F32) * left * xf
-        reads = nt(group, read.astype(BF16))
-        writes = nt(group, write.astype(BF16))
-        grad_decay = nn(reads, later, precision=HIGH) + nn(writes, earlier, precision=HIGH)
-        grad_c = nt((gyf * grow).astype(BF16), state_low)
-        grad_b = nt((xf * left).astype(BF16), grad_low)
-        return grad_b, grad_c, grad_decay
-
-    gb_a, gc_a, gd_a = direction(
-        state(0), gradient(1), grow_a, left_a, ba, ca, length - 1,
-        (row >= col).astype(F32), (row < col).astype(F32),
-    )
-    gb_b, gc_b, gd_b = direction(
-        state(1), gradient(0), grow_b, left_b, bb, cb, 0,
-        (row <= col).astype(F32), (row > col).astype(F32),
-    )
-    gd_a_out[...] = gd_a[:heads] + decay_local[:, 0:length]
-    gd_b_out[...] = gd_b[:heads] + decay_local[:, length:]
-    maps = maps_local[...] + jnp.concatenate([gb_a, gc_a, gb_b, gc_b], axis=1)
+    group = head_groups(heads, columns)
     rows_out = w_in.shape[0] // n_head
     half = n_head // 2 * rows_out
-    own_out[:, half:] = maps
-    maps_out[...] = maps.astype(BF16)
+    for k, (b, earlier) in enumerate(((ba, row < col), (bb, row > col))):
+        left, grad = factors[2 * k + 1], grads[k]
+        write = nn(b[...], grad).astype(BF16).astype(F32) * left * xf
+        writes = nt(group, write.astype(BF16))
+        part = slice(k * length, (k + 1) * length)
+        decay_out[:, part] = decay_local[:, part] + nn(writes, earlier.astype(F32), precision=HIGH)[:heads]
+        grad_b = maps_local[:, 2 * k * n : (2 * k + 1) * n] + nt((xf * left).astype(BF16), grad)
+        at = half + k * n
+        own_out[:, at : at + n] = grad_b
+        send_out[:, at : at + n] = grad_b.astype(BF16)
     for high in range(n_head // 2):
         part = slice(high * rows_out, (high + 1) * rows_out)
         for away in range(2):
-            at = pl.multiple_of((high * 2 + (lax.rem(head, 2) ^ away)) * rows_out, rows_out)
+            at = pl.multiple_of((high * 2 + (lax.rem(index(), 2) ^ away)) * rows_out, rows_out)
             share = nt(grad_x[...], w_in[pl.ds(at, rows_out), :])
             if away:
                 send_out[:, part] = share.astype(BF16)
@@ -384,13 +364,40 @@
                 own_out[:, part] = share
 
 
-def pair_kernel(index, stride, rows_out, maps_at, own, received, received_maps, *refs):
-    own_out, send_out, maps_out = refs[-3:]
+def state_share_kernel(index, radix, first, peers, *refs):
+    refs = list(refs)
+    chunks = take_chunks(refs, [radix], first)
+    grads, gy, ca, cb, maps_local, decay_part, factors = [refs.pop(0) for _ in range(7)]
+    gd_outs, own_out, send_out = refs[-4:-2], refs[-2], refs[-1]
+    heads = decay_part.shape[0]
+    n = ca.shape[1]
+    length, columns = gy.shape
+    (state,) = entering(chunks, index(), peers, n)
+    gyf = gy[...].astype(F32)
+    row, col = iotas(length, length)
+    group = head_groups(heads, columns)
+    frame = lax.broadcasted_iota(jnp.int32, (length, 1), 0)
+    for k, (c, at_end, later) in enumerate(((ca, length - 1, row >= col), (cb, 0, row <= col))):
+        grow, entered = factors[2 * k], state(k)
+        low = entered.astype(BF16)
+        gain = grow[at_end : at_end + 1]
+        through = gain * jnp.sum(entered * grads[k].astype(F32), axis=0, keepdims=True)
+        read = gyf * (grow * nn(c[...], low)) + jnp.where(frame == at_end, through, 0.0)
+        reads = nt(group, read.astype(BF16))
+        gd = nn(reads, later.astype(F32), precision=HIGH)[:heads]
+        gd_outs[k][...] = gd + decay_part[:, k * length : (k + 1) * length]
+        grad_c = maps_local[:, (2 * k + 1) * n : (2 * k + 2) * n] + nt((gyf * grow).astype(BF16), low)
+        own_out[:, k * n : (k + 1) * n] = grad_c
+        send_out[:, k * n : (k + 1) * n] = grad_c.astype(BF16)
+
+
+def pair_kernel(index, stride, rows_out, maps_at, own, received, *refs):
+    own_out, send_out = refs[-2:]
     me = digit(index(), stride, 2)
     half = maps_at // 2
-    maps = own[:, maps_at:] + received_maps[...].astype(F32)
+    maps = own[:, maps_at:] + received[:, maps_at:].astype(F32)
     own_out[:, half:] = maps
-    maps_out[...] = maps.astype(BF16)
+    send_out[:, half:] = maps.astype(BF16)
     for high in range(half // rows_out):
         part = slice(high * rows_out, (high + 1) * rows_out)
         for away in range(2):
@@ -402,39 +409,35 @@
                 own_out[:, part] = total
 
 
-def head_kernel(own, other, other_maps, gf_out, *map_outs):
+def last_kernel(scale, own, other, own_c, other_c, *refs):
+    parts, gf_out, gw_out, map_outs = refs[:-6], refs[-6], refs[-5], refs[-4:]
     columns, n = gf_out.shape[1], map_outs[0].shape[1]
-    gf_out[...] = (own[:, 0:columns] + other[...].astype(F32)).astype(BF16)
-    for k, out in enumerate(map_outs):
-        at = columns + k * n
-        out[...] = own[:, at : at + n] + other_maps[:, k * n : (k + 1) * n].astype(F32)
-
-
-def weight_kernel(scale, *refs):
-    *parts, out = refs
+    gf_out[...] = (own[:, 0:columns] + other[:, 0:columns].astype(F32)).astype(BF16)
+    for k in range(2):
+        at, at_c = columns + k * n, k * n
+        map_outs[2 * k][...] = own[:, at : at + n] + other[:, at : at + n].astype(F32)
+        map_outs[2 * k + 1][...] = own_c[:, at_c : at_c + n] + other_c[:, at_c : at_c + n].astype(F32)
     total = 0.0
     for part in parts:
         piece = part[...].astype(F32)
         total = total + (jnp.sum(piece, axis=0) if piece.ndim == 3 else piece)
-    out[...] = total * scale
-
-
-def call(kernel, outs, *args, flops=0, scalars=0, held=0):
-    specs = [pl.BlockSpec(memory_space=pltpu.SMEM)] * scalars
-    specs += [pl.BlockSpec(memory_space=pltpu.HBM)] * held
-    specs += [pl.BlockSpec(memory_space=pltpu.VMEM)] * (len(args) - scalars - held)
+    gw_out[...] = total * scale
+
+
+def call(kernel, outs, *args, micros=0.0, held=0):
+    specs = [pl.BlockSpec(memory_space=pltpu.HBM)] * held
+    specs += [pl.BlockSpec(memory_space=pltpu.VMEM)] * (len(args) - held)
     outs = list(outs) + [jax.ShapeDtypeStruct(a.shape, a.dtype) for a in args[:held]]
     if held:
         args = tuple(pltpu.with_memory_space_constraint(a, pltpu.HBM) for a in args[:held]) + args[held:]
-    bytes_moved = sum(math.prod(a.shape) * a.dtype.itemsize for a in args)
-    bytes_moved += sum(math.prod(o.shape) * o.dtype.itemsize for o in outs)
+    cost = pl.CostEstimate(flops=int(micros * FLOPS_PER_MICRO), bytes_accessed=0, transcendentals=0)
     return pl.pallas_call(
         kernel,
         out_shape=outs,
         in_specs=specs,
         out_specs=[pl.BlockSpec(memory_space=pltpu.VMEM)] * len(outs),
         scratch_shapes=[pltpu.SemaphoreType.DMA((held,))] if held else [],
-        cost_estimate=pl.CostEstimate(flops=flops, bytes_accessed=bytes_moved, transcendentals=0),
+        cost_estimate=cost,
         compiler_params=pltpu.CompilerParams(vmem_limit_bytes=VMEM_LIMIT),
     )(*args)
 
@@ -455,7 +458,6 @@
     n = b_ahead.shape[1]
     seq_index = lambda: lax.axis_index("seq")
     head_index = lambda: lax.axis_index("head")
-    both_index = lambda: (lax.axis_index("seq"), lax.axis_index("head"))
     shape = jax.ShapeDtypeStruct
     square = shape((length, columns), BF16)
     whole = shape((2 * n + GAIN_ROWS, columns), BF16)
@@ -465,18 +467,18 @@
     steps = radices(peers)
     only = len(steps) == 1
     chunk_shapes = [half] * (steps[0] - 1) if only else [whole]
-    *gradients, factors, da, db, gy, ca, cb = call(
+    *gradients, factors, da, db, gy, ca, cb, skip = call(
         functools.partial(gradient_kernel, seq_index, only, columns // heads),
         chunk_shapes + [shape((4, length, columns), F32)],
-        decay_ahead, decay_behind, grad_y, c_ahead, c_behind,
-        flops=4 * length * n * columns,
-        held=5,
+        decay_ahead, decay_behind, grad_y, c_ahead, c_behind, skip_gain.reshape(1, heads),
+        micros=1.35,
+        held=6,
     )
     *states, x, ba, bb, fs, wi = call(
         functools.partial(state_kernel, seq_index, only),
         chunk_shapes + [square],
         b_ahead, b_behind, features, w_in, factors,
-        flops=2 * length * depth * columns,
+        micros=1.65,
         held=4,
     )
     maps = (ba, ca, bb, cb)
@@ -488,82 +490,84 @@
             shape((heads, 2 * length), F32),
             shape((depth, length), BF16),
         ],
-        skip_gain, x, gy, fs, *maps, da, db,
-        flops=2 * length * depth * columns,
-        scalars=1,
-    )
-    arrived = []
-    for chunk in (gradients, states):
+        skip, x, gy, fs, *maps, da, db,
+        micros=0.9,
+    )
+    def merges(chunk):
         stride, before = 1, None
         for at, radix in enumerate(steps[:-1]):
             received = [swap(chunk[0], "seq", j * stride) for j in range(1, radix)]
             next_last = at == len(steps) - 2
             following = steps[at + 1]
+            count = (following - 1) if next_last else 1
             before, *chunk = call(
                 functools.partial(step_kernel, seq_index, stride, radix, at == 0, next_last, following),
-                [prefix] + ([half] * (following - 1) if next_last else [whole]),
+                [prefix] + ([half] if next_last else [whole]) * count,
                 chunk[0], *received, *([] if at == 0 else [before]),
-                flops=20 * n * columns,
+                micros=0.15,
             )
             stride *= radix
-        arrived.append(far_first(chunk, stride) + ([] if only else [before]))
+        return far_first(chunk, stride) + ([] if only else [before])
+
+    stride = peers // steps[-1]
+    gradient_in = merges(gradients)
+    state_in = merges(states)
     rows_out, rows_w = depth // n_head, depth // peers
     direct = len(steps) == 2 and rows_w % 16 == 0
-    pieces = [shape((2, rows_w, columns), BF16)] * (2 * (steps[0] - 1)) if direct else [shape((depth, columns), BF16)]
-    grad_x, *sends = call(
+    pieces = [shape((4, rows_w, columns), BF16)] * (steps[0] - 1) if direct else [shape((depth, columns), BF16)]
+    grad_x, grads, *sends = call(
         functools.partial(carry_kernel, seq_index, steps, stride, direct),
-        [square] + pieces,
-        *arrived[0], turned, ba, bb, gx_local, factors,
-        flops=length * depth * columns,
-    )
-    after = []
+        [square, shape((2, n, columns), BF16)] + pieces,
+        *gradient_in, turned, ba, bb, gx_local, factors,
+        micros=0.5,
+    )
     if direct:
-        received = [swap(send, "seq", 1 + k % (steps[0] - 1)) for k, send in enumerate(sends)]
-        block, block_low = shape((rows_w, columns), F32), shape((rows_w, columns), BF16)
-        each = len(received) // 2
-        fold = lambda distance, outs, *args: call(
-            functools.partial(fold_kernel, seq_index, steps, distance),
-            outs, turned, grad_x, *args,
-            flops=4 * rows_w * length * columns,
+        received = [swap(send, "seq", j) for j, send in enumerate(sends, start=1)]
+        own_weight, *sends = call(
+            functools.partial(fold_kernel, seq_index, steps),
+            [shape((rows_w, columns), F32)] + [shape((rows_w, columns), BF16)] * 3,
+            turned, grad_x, *received,
+            micros=0.22,
         )
-        far = fold(1, [block_low, block_low], *received[:each])
-        near = fold(0, [block, block_low], *received[each:], far[0])
-        weight_parts = [near[0]] + [
-            swap(send, "seq", j * stride) for send, j in ((far[1], 3), (far[0], 2), (near[1], 1))
-        ]
-        after = [near[0]]
+        weight_parts = [own_weight] + far_first(sends, stride)
     else:
         weight_parts = [lax.all_to_all(sends[0].reshape(peers, rows_w, columns), "seq", 0, 0)]
     def head_shapes(blocks):
-        wide = blocks * rows_out
-        return [shape((length, wide + 4 * n), F32), shape((length, wide), BF16), shape((length, 4 * n), BF16)]
-
-    mask, blocks = 2, n_head // 2
-    gd_ahead, gd_behind, own_share, *sends = call(
-        functools.partial(share_kernel, both_index, steps[-1], stride, only, n_head),
-        [shape((heads, length), F32)] * 2 + head_shapes(blocks),
-        *arrived[0], *arrived[1], grad_x, x, gy, wi, *maps, maps_local, decay_local, factors,
-        flops=3 * length * depth * columns,
-    )
-    others = [swap(send, "head", 1) for send in sends]
-    while mask < n_head:
-        own_share, *sends = call(
-            functools.partial(pair_kernel, head_index, mask, rows_out, blocks * rows_out),
-            head_shapes(blocks // 2),
-            own_share, *others, *after,
-            flops=4 * length * depth,
-        )
-        others = [swap(send, "head", mask) for send in sends]
-        mask, blocks = mask * 2, blocks // 2
-    grad_features, *grad_maps = call(
-        head_kernel,
-        [shape((length, rows_out), BF16)] + [shape((length, n), F32)] * 4,
-        own_share, *others,
-    )
-    (grad_w_in,) = call(
-        functools.partial(weight_kernel, 1.0 / math.sqrt(length * peers)),
-        [shape((rows_w, columns), F32)],
-        *weight_parts,
+        wide = (length, blocks * rows_out + 2 * n)
+        return [shape(wide, F32), shape(wide, BF16)]
+
+    def head_sums(own, send, blocks):
+        other, mask = swap(send, "head", 1), 2
+        while mask < n_head:
+            own, send = call(
+                functools.partial(pair_kernel, head_index, mask, rows_out, blocks * rows_out),
+                head_shapes(blocks // 2),
+                own, other,
+                micros=0.2,
+            )
+            other = swap(send, "head", mask)
+            mask, blocks = mask * 2, blocks // 2
+        return own, other
+
+    decay_part, *shares = call(
+        functools.partial(share_kernel, head_index, n_head),
+        [shape((heads, 2 * length), F32)] + head_shapes(n_head // 2),
+        grad_x, grads, x, wi, ba, bb, maps_local, decay_local, factors,
+        micros=1.0,
+    )
+    shares = head_sums(*shares, n_head // 2)
+    gd_ahead, gd_behind, *shares_c = call(
+        functools.partial(state_share_kernel, seq_index, steps[-1], only, peers),
+        [shape((heads, length), F32)] * 2 + head_shapes(0),
+        *state_in, grads, gy, ca, cb, maps_local, decay_part, factors,
+        micros=1.4,
+    )
+    shares_c = head_sums(*shares_c, 0)
+    grad_features, grad_w_in, *grad_maps = call(
+        functools.partial(last_kernel, 1.0 / math.sqrt(length * peers)),
+        [shape((length, rows_out), BF16), shape((rows_w, columns), F32)] + [shape((length, n), F32)] * 4,
+        *shares, *shares_c, *weight_parts,
+        micros=0.8,
     )
     return (grad_features, grad_w_in, *grad_maps, gd_ahead, gd_behind)
 

time: 42.4 us -> 40.6 us (0.958)
  Pallas kernels: 8.73 us -> 8.06 us
  local copies, waits for them, and re-layouts: 0.65 us -> 0 us
    pallas_call x12, Pallas kernels: 8.73 us -> 8.06 us  [call(): pl.pallas_call(kernel, out_shape=outs, in_specs=specs, out_specs=[pl.Bloc...]
    unnamed x2 -> x0, local copies, waits for them, and re-layouts: 0.65 us -> none
    ppermute x17 -> x16, starting transfers between devices: 22.3 us -> 22 us  [swap(): lax.ppermute(value, axis, [(i, i ^ mask) for i in range(lax.axis_size(axi...]
    ppermute x17 -> x16, waiting for transfers between devices: 9.77 us -> 9.7 us  [swap(): lax.ppermute(value, axis, [(i, i ^ mask) for i in range(lax.axis_size(axi...]
  transfers between devices with their start and end apart: 17 -> 16, of which waited for: 6 -> 5; matrix products, arithmetic and copies ran while one was open for 0% -> 0% of each run, Pallas kernels for 16% -> 15%
where the time goes in v4:
time: 40.6 us; the launch traced here: 40.5 us
  starting transfers between devices  22 us (54%)
  waiting for transfers between devices  9.7 us (24%)
  Pallas kernels  8.06 us (20%)
  between operations  0.74 us (2%)
    ppermute x16, starting transfers between devices, swap(): lax.ppermute(value, axis, [(i, i ^ mask) for i in range(lax.axis_size(axi...  22 us
    ppermute x16, waiting for transfers between devices, swap(): lax.ppermute(value, axis, [(i, i ^ mask) for i in range(lax.axis_size(axi...  9.7 us
    pallas_call x12, Pallas kernels, call(): pl.pallas_call(kernel, out_shape=outs, in_specs=specs, out_specs=[pl.Bloc...  8.06 us
  transfers between devices with their start and end apart: 16, of which 5 were waited for; matrix products, arithmetic and copies ran while one was open for 0% of the time, Pallas kernels for 15%

profile of v4, /device:TPU:0, one launch (start us, length us, event | category | flops | bytes accessed | tf_op | source)
XLA Modules:
  0.0 40.5 jit_solution(16082290363306605266)
XLA Ops:
  0.6 1.4 %shard_map.161 = (bf16[272,256]{1,0:T(8,128)(2,1)S(1)}, f32[4,128,256]{2,1,0:T(8,128)S(1)}, f32[4,128]{1,0:T(4,128)S(1)}, f32[4,128]{1,0:T(4,128)S(1)}, bf16[128...) custom-call(f32[4,128]{1,0:T(4,128)} %refs_0_.2, ...), custom_call_target="tpu_custom_call" | custom-call | flops 1552499968 | tf_op jit(solution)/shard_map/pallas_call | solution.py:434
  2.0 3.0 %collective-permute-start = (bf16[272,256]{1,0:T(8,128)(2,1)S(1)}, bf16[272,256]{1,0:T(8,128)(2,1)S(1)}, u32[]{:S(2)}, u32[]{:S(2)}) collective-permute-start(bf16[272,256]{1,0:T(8,128)(2,1)S(1)} %get-tuple-element.58.refs_0_), channel_id=1, source_target_pairs={{0,4},{4,0},{8,12},{12,8},{16,20},{20,16},{24,28},{28,24},{1,5},{5... | collective-permute-start | bytes 417800 | tf_op jit(solution)/shard_map/ppermute | solution.py:446
  5.0 1.6 %shard_map.163 = (bf16[272,256]{1,0:T(8,128)(2,1)S(1)}, bf16[128,256]{1,0:T(8,128)(2,1)S(1)}, bf16[128,128]{1,0:T(8,128)(2,1)S(1)}, bf16[128,128]{1,0:T(8,128)(2...) custom-call(bf16[128,128]{1,0:T(8,128)(2,1)} %refs_0_.3, bf16[128,128]{1,0:T(8,128)(2,1)} %refs_1_.3, ...), custom_call_target="tpu_custom_call" | custom-call | flops 1897500032 | tf_op jit(solution)/shard_map/pallas_call | solution.py:434
  6.8 2.3 %collective-permute-done.refs_1_ = bf16[272,256]{1,0:T(8,128)(2,1)S(1)} collective-permute-done((bf16[272,256]{1,0:T(8,128)(2,1)S(1)}, bf16[272,256]{1,0:T(8,128)(2,1)S(1)}, u32[]{:S(2)}, u32[]{:S(2)}) %collective-permute-start) | collective-permute-done | bytes 139296 | tf_op jit(solution)/shard_map/ppermute | solution.py:446
  9.2 1.6 %collective-permute-start.1 = (bf16[144,256]{1,0:T(8,128)(2,1)S(1)}, bf16[144,256]{1,0:T(8,128)(2,1)S(1)}, u32[]{:S(2)}, u32[]{:S(2)}) collective-permute-start(bf16[144,256]{1,0:T(8,128)(2,1)S(1)} %get-tuple-element.59), channel_id=1, source_target_pairs={{0,8},{4,12},{8,0},{12,4},{16,24},{20,28},{24,16},{28,20},{1,9},{5... | collective-permute-start | bytes 221192 | tf_op jit(solution)/shard_map/ppermute | solution.py:446
  10.8 2.6 %collective-permute-start.2 = (bf16[144,256]{1,0:T(8,128)(2,1)S(1)}, bf16[144,256]{1,0:T(8,128)(2,1)S(1)}, u32[]{:S(2)}, u32[]{:S(2)}) collective-permute-start(bf16[144,256]{1,0:T(8,128)(2,1)S(1)} %get-tuple-element.60), channel_id=1, source_target_pairs={{0,16},{4,20},{8,24},{12,28},{16,0},{20,4},{24,8},{28,12},{1,17},{... | collective-permute-start | bytes 221192 | tf_op jit(solution)/shard_map/ppermute | solution.py:446
  13.4 0.3 collective-permute-start.3
  13.7 0.9 %shard_map.164 = (f32[128,256]{1,0:T(8,128)S(1)}, f32[128,512]{1,0:T(8,128)S(1)}, f32[4,256]{1,0:T(4,128)S(1)}, bf16[1024,128]{1,0:T(8,128)(2,1)S(1)}) custom-call(f32[1,4]{1,0:T(1,128)S(1)} %get-tuple-element.63.skip, bf16[128,256]{1,0:T(8,128)(2,1)S(1)} %get-tuple-element.65.x, bf16[128,256]{1,0:T(8,128)(2,1)S(1)} %get-tuple-element.66.gy.refs_5_, ...), custom_call_target="tpu_custom_call" | custom-call | flops 1035000000 | tf_op jit(solution)/shard_map/pallas_call | solution.py:434
  14.7 0.7 %collective-permute-start.7 = (bf16[144,256]{1,0:T(8,128)(2,1)S(1)}, bf16[144,256]{1,0:T(8,128)(2,1)S(1)}, u32[]{:S(2)}, u32[]{:S(2)}) collective-permute-start(bf16[144,256]{1,0:T(8,128)(2,1)S(1)} %get-tuple-element.86), channel_id=1, source_target_pairs={{0,8},{4,12},{8,0},{12,4},{16,24},{20,28},{24,16},{28,20},{1,9},{5... | collective-permute-start | bytes 221192 | tf_op jit(solution)/shard_map/ppermute | solution.py:446
  15.4 3.5 %collective-permute-start.8 = (bf16[144,256]{1,0:T(8,128)(2,1)S(1)}, bf16[144,256]{1,0:T(8,128)(2,1)S(1)}, u32[]{:S(2)}, u32[]{:S(2)}) collective-permute-start(bf16[144,256]{1,0:T(8,128)(2,1)S(1)} %get-tuple-element.87), channel_id=1, source_target_pairs={{0,16},{4,20},{8,24},{12,28},{16,0},{20,4},{24,8},{28,12},{1,17},{... | collective-permute-start | bytes 221192 | tf_op jit(solution)/shard_map/ppermute | solution.py:446
  18.9 0.3 collective-permute-start.9
  19.2 0.6 %collective-permute-done.3.refs_2_ = bf16[144,256]{1,0:T(8,128)(2,1)S(1)} collective-permute-done((bf16[144,256]{1,0:T(8,128)(2,1)S(1)}, bf16[144,256]{1,0:T(8,128)(2,1)S(1)}, u32[]{:S(2)}, u32[]{:S(2)}) %collective-permute-start.3) | collective-permute-done | bytes 73760 | tf_op jit(solution)/shard_map/ppermute | solution.py:446
  19.8 0.5 %shard_map.165 = (bf16[128,256]{1,0:T(8,128)(2,1)S(1)}, bf16[2,128,256]{2,1,0:T(8,128)(2,1)S(1)}, bf16[4,128,256]{2,1,0:T(8,128)(2,1)S(1)}) custom-call(bf16[144,256]{1,0:T(8,128)(2,1)S(1)} %collective-permute-done.1.refs_0_, bf16[144,256]{1,0:T(8,128)(2,1)S(1)} %collective-permute-done.2.refs_1_, bf16[144,256]{1,0:T(8,128)(2,1)S(1)} %collective-permute-done.3.refs_2_, ...), custom_call_target="tpu_custom_call" | custom-call | flops 575000000 | tf_op jit(solution)/shard_map/pallas_call | solution.py:434
  20.3 2.4 %collective-permute-start.12 = (bf16[4,128,256]{2,1,0:T(8,128)(2,1)S(1)}, bf16[4,128,256]{2,1,0:T(8,128)(2,1)S(1)}, u32[]{:S(2)}, u32[]{:S(2)}) collective-permute-start(bf16[4,128,256]{2,1,0:T(8,128)(2,1)S(1)} %get-tuple-element.95), channel_id=1, source_target_pairs={{0,4},{4,0},{8,12},{12,8},{16,20},{20,16},{24,28},{28,24},{1,5},{5... | collective-permute-start | bytes 786440 | tf_op jit(solution)/shard_map/ppermute | solution.py:446
  22.7 1.0 %shard_map.166 = (f32[4,256]{1,0:T(4,128)S(1)}, f32[128,768]{1,0:T(8,128)S(1)}, bf16[128,768]{1,0:T(8,128)(2,1)S(1)}) custom-call(bf16[128,256]{1,0:T(8,128)(2,1)S(1)} %get-tuple-element.76.grad_x, bf16[2,128,256]{2,1,0:T(8,128)(2,1)S(1)} %get-tuple-element.77.grads.refs_4_, bf16[128,256]{1,0:T(8,128)(2,1)S(1)} %get-tuple-element.65.x, ...), custom_call_target="tpu_custom_call" | custom-call | flops 1150000000 | tf_op jit(solution)/shard_map/pallas_call | solution.py:434
  23.9 1.2 %collective-permute-done.9.refs_2_ = bf16[144,256]{1,0:T(8,128)(2,1)S(1)} collective-permute-done((bf16[144,256]{1,0:T(8,128)(2,1)S(1)}, bf16[144,256]{1,0:T(8,128)(2,1)S(1)}, u32[]{:S(2)}, u32[]{:S(2)}) %collective-permute-start.9) | collective-permute-done | bytes 73760 | tf_op jit(solution)/shard_map/ppermute | solution.py:446
  25.1 1.4 %shard_map.169 = (f32[4,128]{1,0:T(4,128)}, f32[4,128]{1,0:T(4,128)}, f32[128,256]{1,0:T(8,128)S(1)}, bf16[128,256]{1,0:T(8,128)(2,1)S(1)}) custom-call(bf16[144,256]{1,0:T(8,128)(2,1)S(1)} %collective-permute-done.7.refs_0_, bf16[144,256]{1,0:T(8,128)(2,1)S(1)} %collective-permute-done.8.refs_1_, bf16[144,256]{1,0:T(8,128)(2,1)S(1)} %collective-permute-done.9.refs_2_, ...), custom_call_target="tpu_custom_call" | custom-call | flops 1610000000 | tf_op jit(solution)/shard_map/pallas_call | solution.py:434
  26.6 1.6 %collective-permute-start.5 = (bf16[128,512]{1,0:T(8,128)(2,1)S(1)}, bf16[128,512]{1,0:T(8,128)(2,1)S(1)}, u32[]{:S(2)}, u32[]{:S(2)}) collective-permute-start(bf16[128,512]{1,0:T(8,128)(2,1)S(1)} %get-tuple-element.84), channel_id=1, source_target_pairs={{0,2},{1,3},{2,0},{3,1},{4,6},{5,7},{6,4},{7,5},{8,10},{9,11},{10,... | collective-permute-start | bytes 393224 | tf_op jit(solution)/shard_map/ppermute | solution.py:446
  28.2 1.2 %collective-permute-start.11 = (bf16[128,256]{1,0:T(8,128)(2,1)S(1)}, bf16[128,256]{1,0:T(8,128)(2,1)S(1)}, u32[]{:S(2)}, u32[]{:S(2)}) collective-permute-start(bf16[128,256]{1,0:T(8,128)(2,1)S(1)} %get-tuple-element.94), channel_id=1, source_target_pairs={{0,2},{1,3},{2,0},{3,1},{4,6},{5,7},{6,4},{7,5},{8,10},{9,11},{10,... | collective-permute-start | bytes 196616 | tf_op jit(solution)/shard_map/ppermute | solution.py:446
  29.6 2.3 %collective-permute-start.13 = (bf16[128,256]{1,0:T(8,128)(2,1)S(1)}, bf16[128,256]{1,0:T(8,128)(2,1)S(1)}, u32[]{:S(2)}, u32[]{:S(2)}) collective-permute-start(bf16[128,256]{1,0:T(8,128)(2,1)S(1)} %get-tuple-element.97), channel_id=1, source_target_pairs={{0,8},{4,12},{8,0},{12,4},{16,24},{20,28},{24,16},{28,20},{1,9},{5... | collective-permute-start | bytes 196616 | tf_op jit(solution)/shard_map/ppermute | solution.py:446
  31.9 0.4 collective-permute-start.14
  32.2 2.1 %collective-permute-start.15 = (bf16[128,256]{1,0:T(8,128)(2,1)S(1)}, bf16[128,256]{1,0:T(8,128)(2,1)S(1)}, u32[]{:S(2)}, u32[]{:S(2)}) collective-permute-start(bf16[128,256]{1,0:T(8,128)(2,1)S(1)} %get-tuple-element.99), channel_id=1, source_target_pairs={{0,24},{4,28},{8,16},{12,20},{16,8},{20,12},{24,0},{28,4},{1,25},{... | collective-permute-start | bytes 196616 | tf_op jit(solution)/shard_map/ppermute | solution.py:446
  34.3 5.3 %collective-permute-done.14.refs_2_ = bf16[128,256]{1,0:T(8,128)(2,1)S(1)} collective-permute-done((bf16[128,256]{1,0:T(8,128)(2,1)S(1)}, bf16[128,256]{1,0:T(8,128)(2,1)S(1)}, u32[]{:S(2)}, u32[]{:S(2)}) %collective-permute-start.14) | collective-permute-done | bytes 65568 | tf_op jit(solution)/shard_map/ppermute | solution.py:446
  39.7 0.8 %shard_map.172 = (bf16[128,256]{1,0:T(8,128)(2,1)}, f32[128,256]{1,0:T(8,128)}, f32[128,128]{1,0:T(8,128)}, f32[128,128]{1,0:T(8,128)}, f32[128,128]{1,0:T(8,128)}, /*index=5*/f32[128,128]{1,0:T(8,128)}) custom-call(f32[128,512]{1,0:T(8,128)S(1)} %get-tuple-element.83.own, bf16[128,512]{1,0:T(8,128)(2,1)S(1)} %collective-permute-done.5.other, ...), custom_call_target="tpu_custom_call" | custom-call | flops 920000000 | tf_op jit(solution)/shard_map/pallas_call | solution.py:434
  (20 shorter events, 0.9 us)
Async XLA Ops:
  2.0 7.1 %collective-permute-start = (bf16[272,256]{1,0:T(8,128)(2,1)S(1)}, bf16[272,256]{1,0:T(8,128)(2,1)S(1)}, u32[]{:S(2)}, u32[]{:S(2)}) collective-permute-start(bf16[272,256]{1,0:T(8,128)(2,1)S(1)} %get-tuple-element.58.refs_0_), channel_id=1, source_target_pairs={{0,4},{4,0},{8,12},{12,8},{16,20},{20,16},{24,28},{28,24},{1,5},{5... | collective-permute-start | bytes 417800 | tf_op jit(solution)/shard_map/ppermute | solution.py:446
  6.7 7.9 %collective-permute-start.6 = (bf16[272,256]{1,0:T(8,128)(2,1)S(1)}, bf16[272,256]{1,0:T(8,128)(2,1)S(1)}, u32[]{:S(2)}, u32[]{:S(2)}) collective-permute-start(bf16[272,256]{1,0:T(8,128)(2,1)S(1)} %get-tuple-element.85.refs_0_), channel_id=1, source_target_pairs={{0,4},{4,0},{8,12},{12,8},{16,20},{20,16},{24,28},{28,24},{1,5},{5... | collective-permute-start | bytes 417800 | tf_op jit(solution)/shard_map/ppermute | solution.py:446
  9.2 9.6 %collective-permute-start.1 = (bf16[144,256]{1,0:T(8,128)(2,1)S(1)}, bf16[144,256]{1,0:T(8,128)(2,1)S(1)}, u32[]{:S(2)}, u32[]{:S(2)}) collective-permute-start(bf16[144,256]{1,0:T(8,128)(2,1)S(1)} %get-tuple-element.59), channel_id=1, source_target_pairs={{0,8},{4,12},{8,0},{12,4},{16,24},{20,28},{24,16},{28,20},{1,9},{5... | collective-permute-start | bytes 221192 | tf_op jit(solution)/shard_map/ppermute | solution.py:446
  10.8 8.4 %collective-permute-start.2 = (bf16[144,256]{1,0:T(8,128)(2,1)S(1)}, bf16[144,256]{1,0:T(8,128)(2,1)S(1)}, u32[]{:S(2)}, u32[]{:S(2)}) collective-permute-start(bf16[144,256]{1,0:T(8,128)(2,1)S(1)} %get-tuple-element.60), channel_id=1, source_target_pairs={{0,16},{4,20},{8,24},{12,28},{16,0},{20,4},{24,8},{28,12},{1,17},{... | collective-permute-start | bytes 221192 | tf_op jit(solution)/shard_map/ppermute | solution.py:446
  13.4 6.4 %collective-permute-start.3 = (bf16[144,256]{1,0:T(8,128)(2,1)S(1)}, bf16[144,256]{1,0:T(8,128)(2,1)S(1)}, u32[]{:S(2)}, u32[]{:S(2)}) collective-permute-start(bf16[144,256]{1,0:T(8,128)(2,1)S(1)} %get-tuple-element.61), channel_id=1, source_target_pairs={{0,24},{4,28},{8,16},{12,20},{16,8},{20,12},{24,0},{28,4},{1,25},{... | collective-permute-start | bytes 221192 | tf_op jit(solution)/shard_map/ppermute | solution.py:446
  14.7 9.0 %collective-permute-start.7 = (bf16[144,256]{1,0:T(8,128)(2,1)S(1)}, bf16[144,256]{1,0:T(8,128)(2,1)S(1)}, u32[]{:S(2)}, u32[]{:S(2)}) collective-permute-start(bf16[144,256]{1,0:T(8,128)(2,1)S(1)} %get-tuple-element.86), channel_id=1, source_target_pairs={{0,8},{4,12},{8,0},{12,4},{16,24},{20,28},{24,16},{28,20},{1,9},{5... | collective-permute-start | bytes 221192 | tf_op jit(solution)/shard_map/ppermute | solution.py:446
  15.4 8.6 %collective-permute-start.8 = (bf16[144,256]{1,0:T(8,128)(2,1)S(1)}, bf16[144,256]{1,0:T(8,128)(2,1)S(1)}, u32[]{:S(2)}, u32[]{:S(2)}) collective-permute-start(bf16[144,256]{1,0:T(8,128)(2,1)S(1)} %get-tuple-element.87), channel_id=1, source_target_pairs={{0,16},{4,20},{8,24},{12,28},{16,0},{20,4},{24,8},{28,12},{1,17},{... | collective-permute-start | bytes 221192 | tf_op jit(solution)/shard_map/ppermute | solution.py:446
  18.9 6.3 %collective-permute-start.9 = (bf16[144,256]{1,0:T(8,128)(2,1)S(1)}, bf16[144,256]{1,0:T(8,128)(2,1)S(1)}, u32[]{:S(2)}, u32[]{:S(2)}) collective-permute-start(bf16[144,256]{1,0:T(8,128)(2,1)S(1)} %get-tuple-element.88), channel_id=1, source_target_pairs={{0,24},{4,28},{8,16},{12,20},{16,8},{20,12},{24,0},{28,4},{1,25},{... | collective-permute-start | bytes 221192 | tf_op jit(solution)/shard_map/ppermute | solution.py:446
  20.3 9.1 %collective-permute-start.12 = (bf16[4,128,256]{2,1,0:T(8,128)(2,1)S(1)}, bf16[4,128,256]{2,1,0:T(8,128)(2,1)S(1)}, u32[]{:S(2)}, u32[]{:S(2)}) collective-permute-start(bf16[4,128,256]{2,1,0:T(8,128)(2,1)S(1)} %get-tuple-element.95), channel_id=1, source_target_pairs={{0,4},{4,0},{8,12},{12,8},{16,20},{20,16},{24,28},{28,24},{1,5},{5... | collective-permute-start | bytes 786440 | tf_op jit(solution)/shard_map/ppermute | solution.py:446
  23.6 2.9 %collective-permute-start.4 = (bf16[128,768]{1,0:T(8,128)(2,1)S(1)}, bf16[128,768]{1,0:T(8,128)(2,1)S(1)}, u32[]{:S(2)}, u32[]{:S(2)}) collective-permute-start(bf16[128,768]{1,0:T(8,128)(2,1)S(1)} %get-tuple-element.82), channel_id=1, source_target_pairs={{0,1},{1,0},{2,3},{3,2},{4,5},{5,4},{6,7},{7,6},{8,9},{9,8},{10,11... | collective-permute-start | bytes 589832 | tf_op jit(solution)/shard_map/ppermute | solution.py:446
  26.5 1.6 %collective-permute-start.10 = (bf16[128,256]{1,0:T(8,128)(2,1)S(1)}, bf16[128,256]{1,0:T(8,128)(2,1)S(1)}, u32[]{:S(2)}, u32[]{:S(2)}) collective-permute-start(bf16[128,256]{1,0:T(8,128)(2,1)S(1)} %get-tuple-element.92), channel_id=1, source_target_pairs={{0,1},{1,0},{2,3},{3,2},{4,5},{5,4},{6,7},{7,6},{8,9},{9,8},{10,11... | collective-permute-start | bytes 196616 | tf_op jit(solution)/shard_map/ppermute | solution.py:446
  26.6 13.1 %collective-permute-start.5 = (bf16[128,512]{1,0:T(8,128)(2,1)S(1)}, bf16[128,512]{1,0:T(8,128)(2,1)S(1)}, u32[]{:S(2)}, u32[]{:S(2)}) collective-permute-start(bf16[128,512]{1,0:T(8,128)(2,1)S(1)} %get-tuple-element.84), channel_id=1, source_target_pairs={{0,2},{1,3},{2,0},{3,1},{4,6},{5,7},{6,4},{7,5},{8,10},{9,11},{10,... | collective-permute-start | bytes 393224 | tf_op jit(solution)/shard_map/ppermute | solution.py:446
  28.2 6.2 %collective-permute-start.11 = (bf16[128,256]{1,0:T(8,128)(2,1)S(1)}, bf16[128,256]{1,0:T(8,128)(2,1)S(1)}, u32[]{:S(2)}, u32[]{:S(2)}) collective-permute-start(bf16[128,256]{1,0:T(8,128)(2,1)S(1)} %get-tuple-element.94), channel_id=1, source_target_pairs={{0,2},{1,3},{2,0},{3,1},{4,6},{5,7},{6,4},{7,5},{8,10},{9,11},{10,... | collective-permute-start | bytes 196616 | tf_op jit(solution)/shard_map/ppermute | solution.py:446
  29.6 4.7 %collective-permute-start.13 = (bf16[128,256]{1,0:T(8,128)(2,1)S(1)}, bf16[128,256]{1,0:T(8,128)(2,1)S(1)}, u32[]{:S(2)}, u32[]{:S(2)}) collective-permute-start(bf16[128,256]{1,0:T(8,128)(2,1)S(1)} %get-tuple-element.97), channel_id=1, source_target_pairs={{0,8},{4,12},{8,0},{12,4},{16,24},{20,28},{24,16},{28,20},{1,9},{5... | collective-permute-start | bytes 196616 | tf_op jit(solution)/shard_map/ppermute | solution.py:446
  31.9 7.8 %collective-permute-start.14 = (bf16[128,256]{1,0:T(8,128)(2,1)S(1)}, bf16[128,256]{1,0:T(8,128)(2,1)S(1)}, u32[]{:S(2)}, u32[]{:S(2)}) collective-permute-start(bf16[128,256]{1,0:T(8,128)(2,1)S(1)} %get-tuple-element.98), channel_id=1, source_target_pairs={{0,16},{4,20},{8,24},{12,28},{16,0},{20,4},{24,8},{28,12},{1,17},{... | collective-permute-start | bytes 196616 | tf_op jit(solution)/shard_map/ppermute | solution.py:446
  32.2 7.4 %collective-permute-start.15 = (bf16[128,256]{1,0:T(8,128)(2,1)S(1)}, bf16[128,256]{1,0:T(8,128)(2,1)S(1)}, u32[]{:S(2)}, u32[]{:S(2)}) collective-permute-start(bf16[128,256]{1,0:T(8,128)(2,1)S(1)} %get-tuple-element.99), channel_id=1, source_target_pairs={{0,24},{4,28},{8,16},{12,20},{16,8},{20,12},{24,0},{28,4},{1,25},{... | collective-permute-start | bytes 196616 | tf_op jit(solution)/shard_map/ppermute | solution.py:446

commit v5 on v4

--- a/solution.py
+++ b/solution.py
@@ -287,7 +287,7 @@
 def take_chunks(refs, lasts, first):
     chunks = []
     for radix in lasts:
-        received = [refs.pop(0) for _ in range(radix - 1)]
+        received = [refs.pop(0) for _ in range(radix - 1)][::-1]
         chunks.append((received, None if first else refs.pop(0)))
     return chunks
 
@@ -364,11 +364,11 @@
                 own_out[:, part] = share
 
 
-def state_share_kernel(index, radix, first, peers, *refs):
+def state_share_kernel(index, steps, peers, *refs):
     refs = list(refs)
-    chunks = take_chunks(refs, [radix], first)
+    chunks = take_chunks(refs, steps[-1:], len(steps) == 1)
     grads, gy, ca, cb, maps_local, decay_part, factors = [refs.pop(0) for _ in range(7)]
-    gd_outs, own_out, send_out = refs[-4:-2], refs[-2], refs[-1]
+    *gd_outs, own_out, send_out = refs
     heads = decay_part.shape[0]
     n = ca.shape[1]
     length, columns = gy.shape
@@ -391,14 +391,20 @@
         send_out[:, k * n : (k + 1) * n] = grad_c.astype(BF16)
 
 
-def pair_kernel(index, stride, rows_out, maps_at, own, received, *refs):
-    own_out, send_out = refs[-2:]
+def pair_kernel(index, stride, rows_out, blocks, count, *refs):
+    parts, own_out, send_out = refs[:count], refs[-2], refs[-1]
     me = digit(index(), stride, 2)
-    half = maps_at // 2
-    maps = own[:, maps_at:] + received[:, maps_at:].astype(F32)
+    own, received = parts[0], parts[1]
+    at = blocks * rows_out
+    half = at // 2
+    maps = []
+    for mine, other in zip(parts[0::2], parts[1::2]):
+        maps.append(mine[:, at:] + other[:, at:].astype(F32))
+        at = 0
+    maps = jnp.concatenate(maps, axis=1)
     own_out[:, half:] = maps
     send_out[:, half:] = maps.astype(BF16)
-    for high in range(half // rows_out):
+    for high in range(blocks // 2):
         part = slice(high * rows_out, (high + 1) * rows_out)
         for away in range(2):
             at = pl.multiple_of((high * 2 + (me ^ away)) * rows_out, rows_out)
@@ -409,14 +415,13 @@
                 own_out[:, part] = total
 
 
-def last_kernel(scale, own, other, own_c, other_c, *refs):
+def last_kernel(scale, own, other, *refs):
     parts, gf_out, gw_out, map_outs = refs[:-6], refs[-6], refs[-5], refs[-4:]
     columns, n = gf_out.shape[1], map_outs[0].shape[1]
     gf_out[...] = (own[:, 0:columns] + other[:, 0:columns].astype(F32)).astype(BF16)
-    for k in range(2):
-        at, at_c = columns + k * n, k * n
-        map_outs[2 * k][...] = own[:, at : at + n] + other[:, at : at + n].astype(F32)
-        map_outs[2 * k + 1][...] = own_c[:, at_c : at_c + n] + other_c[:, at_c : at_c + n].astype(F32)
+    for k, out in enumerate((map_outs[0], map_outs[2], map_outs[1], map_outs[3])):
+        at = columns + k * n
+        out[...] = own[:, at : at + n] + other[:, at : at + n].astype(F32)
     total = 0.0
     for part in parts:
         piece = part[...].astype(F32)
@@ -448,7 +453,7 @@
 
 def far_first(sends, stride):
     jobs = list(enumerate(sends, start=1))
-    return [swap(send, "seq", j * stride) for j, send in reversed(jobs)][::-1]
+    return [swap(send, "seq", j * stride) for j, send in reversed(jobs)]
 
 
 def local(features, w_in, b_ahead, c_ahead, b_behind, c_behind, decay_ahead, decay_behind, skip_gain, grad_y):
@@ -521,52 +526,51 @@
         *gradient_in, turned, ba, bb, gx_local, factors,
         micros=0.5,
     )
+    def head_shapes(blocks, maps):
+        wide = (length, blocks * rows_out + maps * n)
+        return [shape(wide, F32), shape(wide, BF16)]
+
+    decay_part, own, send = call(
+        functools.partial(share_kernel, head_index, n_head),
+        [shape((heads, 2 * length), F32)] + head_shapes(n_head // 2, 2),
+        grad_x, grads, x, wi, ba, bb, maps_local, decay_local, factors,
+        micros=1.0,
+    )
+    shares = [own, swap(send, "head", 1)]
+    received = [swap(send, "seq", j) for j, send in enumerate(sends, start=1)] if direct else []
+    gd_ahead, gd_behind, own, send = call(
+        functools.partial(state_share_kernel, seq_index, steps, peers),
+        [shape((heads, length), F32)] * 2 + head_shapes(0, 2),
+        *state_in, grads, gy, ca, cb, maps_local, decay_part, factors,
+        micros=1.4,
+    )
+    shares += [own, swap(send, "head", 1)]
+    after = []
     if direct:
-        received = [swap(send, "seq", j) for j, send in enumerate(sends, start=1)]
         own_weight, *sends = call(
             functools.partial(fold_kernel, seq_index, steps),
             [shape((rows_w, columns), F32)] + [shape((rows_w, columns), BF16)] * 3,
-            turned, grad_x, *received,
+            turned, grad_x, *received, own,
             micros=0.22,
         )
         weight_parts = [own_weight] + far_first(sends, stride)
+        after = [own_weight]
     else:
         weight_parts = [lax.all_to_all(sends[0].reshape(peers, rows_w, columns), "seq", 0, 0)]
-    def head_shapes(blocks):
-        wide = (length, blocks * rows_out + 2 * n)
-        return [shape(wide, F32), shape(wide, BF16)]
-
-    def head_sums(own, send, blocks):
-        other, mask = swap(send, "head", 1), 2
-        while mask < n_head:
-            own, send = call(
-                functools.partial(pair_kernel, head_index, mask, rows_out, blocks * rows_out),
-                head_shapes(blocks // 2),
-                own, other,
-                micros=0.2,
-            )
-            other = swap(send, "head", mask)
-            mask, blocks = mask * 2, blocks // 2
-        return own, other
-
-    decay_part, *shares = call(
-        functools.partial(share_kernel, head_index, n_head),
-        [shape((heads, 2 * length), F32)] + head_shapes(n_head // 2),
-        grad_x, grads, x, wi, ba, bb, maps_local, decay_local, factors,
-        micros=1.0,
-    )
-    shares = head_sums(*shares, n_head // 2)
-    gd_ahead, gd_behind, *shares_c = call(
-        functools.partial(state_share_kernel, seq_index, steps[-1], only, peers),
-        [shape((heads, length), F32)] * 2 + head_shapes(0),
-        *state_in, grads, gy, ca, cb, maps_local, decay_part, factors,
-        micros=1.4,
-    )
-    shares_c = head_sums(*shares_c, 0)
+    mask, blocks = 2, n_head // 2
+    while mask < n_head:
+        own, send = call(
+            functools.partial(pair_kernel, head_index, mask, rows_out, blocks, len(shares)),
+            head_shapes(blocks // 2, 4),
+            *shares, *after,
+            micros=0.25,
+        )
+        shares = [own, swap(send, "head", mask)]
+        mask, blocks = mask * 2, blocks // 2
     grad_features, grad_w_in, *grad_maps = call(
         functools.partial(last_kernel, 1.0 / math.sqrt(length * peers)),
         [shape((length, rows_out), BF16), shape((rows_w, columns), F32)] + [shape((length, n), F32)] * 4,
-        *shares, *shares_c, *weight_parts,
+        *shares, *weight_parts,
         micros=0.8,
     )
     return (grad_features, grad_w_in, *grad_maps, gd_ahead, gd_behind)

time: 40.6 us -> 39.3 us (0.968)
  starting transfers between devices: 22 us -> 19.6 us
  waiting for transfers between devices: 9.7 us -> 10.7 us
    ppermute x16 -> x15, starting transfers between devices: 22 us -> 19.6 us  [swap(): lax.ppermute(value, axis, [(i, i ^ mask) for i in range(lax.axis_size(axi...]
    ppermute x16 -> x15, waiting for transfers between devices: 9.7 us -> 10.7 us  [swap(): lax.ppermute(value, axis, [(i, i ^ mask) for i in range(lax.axis_size(axi...]
    pallas_call x12 -> x11, Pallas kernels: 8.06 us -> 8.07 us  [call(): pl.pallas_call(kernel, out_shape=outs, in_specs=specs, out_specs=[pl.Bloc...]
  transfers between devices with their start and end apart: 16 -> 15, of which waited for: 5 -> 6; matrix products, arithmetic and copies ran while one was open for 0% -> 0% of each run, Pallas kernels for 15% -> 15%
where the time goes in v5:
time: 39.3 us; the launch traced here: 39.1 us
  starting transfers between devices  19.6 us (50%)
  waiting for transfers between devices  10.7 us (27%)
  Pallas kernels  8.07 us (21%)
  between operations  0.75 us (2%)
    ppermute x15, starting transfers between devices, swap(): lax.ppermute(value, axis, [(i, i ^ mask) for i in range(lax.axis_size(axi...  19.6 us
    ppermute x15, waiting for transfers between devices, swap(): lax.ppermute(value, axis, [(i, i ^ mask) for i in range(lax.axis_size(axi...  10.7 us
    pallas_call x11, Pallas kernels, call(): pl.pallas_call(kernel, out_shape=outs, in_specs=specs, out_specs=[pl.Bloc...  8.07 us
  transfers between devices with their start and end apart: 15, of which 6 were waited for; matrix products, arithmetic and copies ran while one was open for 0% of the time, Pallas kernels for 15%

profile of v5, /device:TPU:0, one launch (start us, length us, event | category | flops | bytes accessed | tf_op | source)
XLA Modules:
  0.0 39.1 jit_solution(12867703331524279532)
XLA Ops:
  0.6 1.4 %shard_map.161 = (bf16[272,256]{1,0:T(8,128)(2,1)S(1)}, f32[4,128,256]{2,1,0:T(8,128)S(1)}, f32[4,128]{1,0:T(4,128)S(1)}, f32[4,128]{1,0:T(4,128)S(1)}, bf16[128...) custom-call(f32[4,128]{1,0:T(4,128)} %refs_0_.2, ...), custom_call_target="tpu_custom_call" | custom-call | flops 1552499968 | tf_op jit(solution)/shard_map/pallas_call | solution.py:439
  2.0 3.0 %collective-permute-start = (bf16[272,256]{1,0:T(8,128)(2,1)S(1)}, bf16[272,256]{1,0:T(8,128)(2,1)S(1)}, u32[]{:S(2)}, u32[]{:S(2)}) collective-permute-start(bf16[272,256]{1,0:T(8,128)(2,1)S(1)} %get-tuple-element.56.refs_0_), channel_id=1, source_target_pairs={{0,4},{4,0},{8,12},{12,8},{16,20},{20,16},{24,28},{28,24},{1,5},{5... | collective-permute-start | bytes 417800 | tf_op jit(solution)/shard_map/ppermute | solution.py:451
  5.0 1.6 %shard_map.163 = (bf16[272,256]{1,0:T(8,128)(2,1)S(1)}, bf16[128,256]{1,0:T(8,128)(2,1)S(1)}, bf16[128,128]{1,0:T(8,128)(2,1)S(1)}, bf16[128,128]{1,0:T(8,128)(2...) custom-call(bf16[128,128]{1,0:T(8,128)(2,1)} %refs_0_.3, bf16[128,128]{1,0:T(8,128)(2,1)} %refs_1_.3, ...), custom_call_target="tpu_custom_call" | custom-call | flops 1897500032 | tf_op jit(solution)/shard_map/pallas_call | solution.py:439
  6.8 2.3 %collective-permute-done.refs_1_ = bf16[272,256]{1,0:T(8,128)(2,1)S(1)} collective-permute-done((bf16[272,256]{1,0:T(8,128)(2,1)S(1)}, bf16[272,256]{1,0:T(8,128)(2,1)S(1)}, u32[]{:S(2)}, u32[]{:S(2)}) %collective-permute-start) | collective-permute-done | bytes 139296 | tf_op jit(solution)/shard_map/ppermute | solution.py:451
  9.2 3.6 %collective-permute-start.1 = (bf16[144,256]{1,0:T(8,128)(2,1)S(1)}, bf16[144,256]{1,0:T(8,128)(2,1)S(1)}, u32[]{:S(2)}, u32[]{:S(2)}) collective-permute-start(bf16[144,256]{1,0:T(8,128)(2,1)S(1)} %get-tuple-element.57), channel_id=1, source_target_pairs={{0,24},{4,28},{8,16},{12,20},{16,8},{20,12},{24,0},{28,4},{1,25},{... | collective-permute-start | bytes 221192 | tf_op jit(solution)/shard_map/ppermute | solution.py:451
  12.8 0.9 %collective-permute-start.3 = (bf16[144,256]{1,0:T(8,128)(2,1)S(1)}, bf16[144,256]{1,0:T(8,128)(2,1)S(1)}, u32[]{:S(2)}, u32[]{:S(2)}) collective-permute-start(bf16[144,256]{1,0:T(8,128)(2,1)S(1)} %get-tuple-element.59), channel_id=1, source_target_pairs={{0,8},{4,12},{8,0},{12,4},{16,24},{20,28},{24,16},{28,20},{1,9},{5... | collective-permute-start | bytes 221192 | tf_op jit(solution)/shard_map/ppermute | solution.py:451
  13.7 0.9 %shard_map.164 = (f32[128,256]{1,0:T(8,128)S(1)}, f32[128,512]{1,0:T(8,128)S(1)}, f32[4,256]{1,0:T(4,128)S(1)}, bf16[1024,128]{1,0:T(8,128)(2,1)S(1)}) custom-call(f32[1,4]{1,0:T(1,128)S(1)} %get-tuple-element.61.skip, bf16[128,256]{1,0:T(8,128)(2,1)S(1)} %get-tuple-element.63.x, bf16[128,256]{1,0:T(8,128)(2,1)S(1)} %get-tuple-element.64.gy.refs_5_, ...), custom_call_target="tpu_custom_call" | custom-call | flops 1035000000 | tf_op jit(solution)/shard_map/pallas_call | solution.py:439
  14.7 3.6 %collective-permute-start.6 = (bf16[144,256]{1,0:T(8,128)(2,1)S(1)}, bf16[144,256]{1,0:T(8,128)(2,1)S(1)}, u32[]{:S(2)}, u32[]{:S(2)}) collective-permute-start(bf16[144,256]{1,0:T(8,128)(2,1)S(1)} %get-tuple-element.82), channel_id=1, source_target_pairs={{0,24},{4,28},{8,16},{12,20},{16,8},{20,12},{24,0},{28,4},{1,25},{... | collective-permute-start | bytes 221192 | tf_op jit(solution)/shard_map/ppermute | solution.py:451
  18.3 0.9 %collective-permute-start.8 = (bf16[144,256]{1,0:T(8,128)(2,1)S(1)}, bf16[144,256]{1,0:T(8,128)(2,1)S(1)}, u32[]{:S(2)}, u32[]{:S(2)}) collective-permute-start(bf16[144,256]{1,0:T(8,128)(2,1)S(1)} %get-tuple-element.84), channel_id=1, source_target_pairs={{0,8},{4,12},{8,0},{12,4},{16,24},{20,28},{24,16},{28,20},{1,9},{5... | collective-permute-start | bytes 221192 | tf_op jit(solution)/shard_map/ppermute | solution.py:451
  19.2 2.7 %collective-permute-done.2.refs_1_ = bf16[144,256]{1,0:T(8,128)(2,1)S(1)} collective-permute-done((bf16[144,256]{1,0:T(8,128)(2,1)S(1)}, bf16[144,256]{1,0:T(8,128)(2,1)S(1)}, u32[]{:S(2)}, u32[]{:S(2)}) %collective-permute-start.2) | collective-permute-done | bytes 73760 | tf_op jit(solution)/shard_map/ppermute | solution.py:451
  21.9 0.5 %shard_map.165 = (bf16[128,256]{1,0:T(8,128)(2,1)S(1)}, bf16[2,128,256]{2,1,0:T(8,128)(2,1)S(1)}, bf16[4,128,256]{2,1,0:T(8,128)(2,1)S(1)}) custom-call(bf16[144,256]{1,0:T(8,128)(2,1)S(1)} %collective-permute-done.1.refs_0_, bf16[144,256]{1,0:T(8,128)(2,1)S(1)} %collective-permute-done.2.refs_1_, bf16[144,256]{1,0:T(8,128)(2,1)S(1)} %collective-permute-done.3.refs_2_, ...), custom_call_target="tpu_custom_call" | custom-call | flops 575000000 | tf_op jit(solution)/shard_map/pallas_call | solution.py:439
  22.4 1.2 %collective-permute-start.10 = (bf16[4,128,256]{2,1,0:T(8,128)(2,1)S(1)}, bf16[4,128,256]{2,1,0:T(8,128)(2,1)S(1)}, u32[]{:S(2)}, u32[]{:S(2)}) collective-permute-start(bf16[4,128,256]{2,1,0:T(8,128)(2,1)S(1)} %get-tuple-element.89), channel_id=1, source_target_pairs={{0,4},{4,0},{8,12},{12,8},{16,20},{20,16},{24,28},{28,24},{1,5},{5... | collective-permute-start | bytes 786440 | tf_op jit(solution)/shard_map/ppermute | solution.py:451
  23.6 1.0 %shard_map.166 = (f32[4,256]{1,0:T(4,128)S(1)}, f32[128,768]{1,0:T(8,128)S(1)}, bf16[128,768]{1,0:T(8,128)(2,1)S(1)}) custom-call(bf16[128,256]{1,0:T(8,128)(2,1)S(1)} %get-tuple-element.74.grad_x, bf16[2,128,256]{2,1,0:T(8,128)(2,1)S(1)} %get-tuple-element.75.grads.refs_4_, bf16[128,256]{1,0:T(8,128)(2,1)S(1)} %get-tuple-element.63.x, ...), custom_call_target="tpu_custom_call" | custom-call | flops 1150000000 | tf_op jit(solution)/shard_map/pallas_call | solution.py:439
  24.7 0.2 collective-permute-done.7.refs_1_
  24.8 1.4 %shard_map.168 = (f32[4,128]{1,0:T(4,128)}, f32[4,128]{1,0:T(4,128)}, f32[128,256]{1,0:T(8,128)S(1)}, bf16[128,256]{1,0:T(8,128)(2,1)S(1)}) custom-call(bf16[144,256]{1,0:T(8,128)(2,1)S(1)} %collective-permute-done.6.refs_0_, bf16[144,256]{1,0:T(8,128)(2,1)S(1)} %collective-permute-done.7.refs_1_, bf16[144,256]{1,0:T(8,128)(2,1)S(1)} %collective-permute-done.8.refs_2_, ...), custom_call_target="tpu_custom_call" | custom-call | flops 1610000000 | tf_op jit(solution)/shard_map/pallas_call | solution.py:439
  26.3 0.3 collective-permute-start.9
  26.6 2.2 %collective-permute-done.10.refs_0_ = bf16[4,128,256]{2,1,0:T(8,128)(2,1)S(1)} collective-permute-done((bf16[4,128,256]{2,1,0:T(8,128)(2,1)S(1)}, bf16[4,128,256]{2,1,0:T(8,128)(2,1)S(1)}, u32[]{:S(2)}, u32[]{:S(2)}) %collective-permute-start.10) | collective-permute-done | bytes 262176 | tf_op jit(solution)/shard_map/ppermute | solution.py:451
  28.8 0.2 shard_map.169
  29.1 1.6 %collective-permute-start.11 = (bf16[128,768]{1,0:T(8,128)(2,1)S(1)}, bf16[128,768]{1,0:T(8,128)(2,1)S(1)}, u32[]{:S(2)}, u32[]{:S(2)}) collective-permute-start(bf16[128,768]{1,0:T(8,128)(2,1)S(1)} %get-tuple-element.92), channel_id=1, source_target_pairs={{0,2},{1,3},{2,0},{3,1},{4,6},{5,7},{6,4},{7,5},{8,10},{9,11},{10,... | collective-permute-start | bytes 589832 | tf_op jit(solution)/shard_map/ppermute | solution.py:451
  30.7 1.2 %collective-permute-start.12 = (bf16[128,256]{1,0:T(8,128)(2,1)S(1)}, bf16[128,256]{1,0:T(8,128)(2,1)S(1)}, u32[]{:S(2)}, u32[]{:S(2)}) collective-permute-start(bf16[128,256]{1,0:T(8,128)(2,1)S(1)} %get-tuple-element.93), channel_id=1, source_target_pairs={{0,24},{4,28},{8,16},{12,20},{16,8},{20,12},{24,0},{28,4},{1,25},{... | collective-permute-start | bytes 196616 | tf_op jit(solution)/shard_map/ppermute | solution.py:451
  31.9 3.2 %collective-permute-start.14 = (bf16[128,256]{1,0:T(8,128)(2,1)S(1)}, bf16[128,256]{1,0:T(8,128)(2,1)S(1)}, u32[]{:S(2)}, u32[]{:S(2)}) collective-permute-start(bf16[128,256]{1,0:T(8,128)(2,1)S(1)} %get-tuple-element.95), channel_id=1, source_target_pairs={{0,8},{4,12},{8,0},{12,4},{16,24},{20,28},{24,16},{28,20},{1,9},{5... | collective-permute-start | bytes 196616 | tf_op jit(solution)/shard_map/ppermute | solution.py:451
  35.1 2.2 %collective-permute-done.12.refs_1_ = bf16[128,256]{1,0:T(8,128)(2,1)S(1)} collective-permute-done((bf16[128,256]{1,0:T(8,128)(2,1)S(1)}, bf16[128,256]{1,0:T(8,128)(2,1)S(1)}, u32[]{:S(2)}, u32[]{:S(2)}) %collective-permute-start.12) | collective-permute-done | bytes 65568 | tf_op jit(solution)/shard_map/ppermute | solution.py:451
  37.3 1.0 %collective-permute-done.13.refs_2_ = bf16[128,256]{1,0:T(8,128)(2,1)S(1)} collective-permute-done((bf16[128,256]{1,0:T(8,128)(2,1)S(1)}, bf16[128,256]{1,0:T(8,128)(2,1)S(1)}, u32[]{:S(2)}, u32[]{:S(2)}) %collective-permute-start.13) | collective-permute-done | bytes 65568 | tf_op jit(solution)/shard_map/ppermute | solution.py:451
  38.3 0.8 %shard_map.171 = (bf16[128,256]{1,0:T(8,128)(2,1)}, f32[128,256]{1,0:T(8,128)}, f32[128,128]{1,0:T(8,128)}, f32[128,128]{1,0:T(8,128)}, f32[128,128]{1,0:T(8,128)}, /*index=5*/f32[128,128]{1,0:T(8,128)}) custom-call(f32[128,768]{1,0:T(8,128)S(1)} %get-tuple-element.91.own, bf16[128,768]{1,0:T(8,128)(2,1)S(1)} %collective-permute-done.11.other, ...), custom_call_target="tpu_custom_call" | custom-call | flops 920000000 | tf_op jit(solution)/shard_map/pallas_call | solution.py:439
  (17 shorter events, 0.5 us)
Async XLA Ops:
  2.0 7.1 %collective-permute-start = (bf16[272,256]{1,0:T(8,128)(2,1)S(1)}, bf16[272,256]{1,0:T(8,128)(2,1)S(1)}, u32[]{:S(2)}, u32[]{:S(2)}) collective-permute-start(bf16[272,256]{1,0:T(8,128)(2,1)S(1)} %get-tuple-element.56.refs_0_), channel_id=1, source_target_pairs={{0,4},{4,0},{8,12},{12,8},{16,20},{20,16},{24,28},{28,24},{1,5},{5... | collective-permute-start | bytes 417800 | tf_op jit(solution)/shard_map/ppermute | solution.py:451
  6.7 7.9 %collective-permute-start.5 = (bf16[272,256]{1,0:T(8,128)(2,1)S(1)}, bf16[272,256]{1,0:T(8,128)(2,1)S(1)}, u32[]{:S(2)}, u32[]{:S(2)}) collective-permute-start(bf16[272,256]{1,0:T(8,128)(2,1)S(1)} %get-tuple-element.81.refs_0_), channel_id=1, source_target_pairs={{0,4},{4,0},{8,12},{12,8},{16,20},{20,16},{24,28},{28,24},{1,5},{5... | collective-permute-start | bytes 417800 | tf_op jit(solution)/shard_map/ppermute | solution.py:451
  9.2 9.1 %collective-permute-start.1 = (bf16[144,256]{1,0:T(8,128)(2,1)S(1)}, bf16[144,256]{1,0:T(8,128)(2,1)S(1)}, u32[]{:S(2)}, u32[]{:S(2)}) collective-permute-start(bf16[144,256]{1,0:T(8,128)(2,1)S(1)} %get-tuple-element.57), channel_id=1, source_target_pairs={{0,24},{4,28},{8,16},{12,20},{16,8},{20,12},{24,0},{28,4},{1,25},{... | collective-permute-start | bytes 221192 | tf_op jit(solution)/shard_map/ppermute | solution.py:451
  12.8 9.1 %collective-permute-start.2 = (bf16[144,256]{1,0:T(8,128)(2,1)S(1)}, bf16[144,256]{1,0:T(8,128)(2,1)S(1)}, u32[]{:S(2)}, u32[]{:S(2)}) collective-permute-start(bf16[144,256]{1,0:T(8,128)(2,1)S(1)} %get-tuple-element.58), channel_id=1, source_target_pairs={{0,16},{4,20},{8,24},{12,28},{16,0},{20,4},{24,8},{28,12},{1,17},{... | collective-permute-start | bytes 221192 | tf_op jit(solution)/shard_map/ppermute | solution.py:451
  12.8 9.1 %collective-permute-start.3 = (bf16[144,256]{1,0:T(8,128)(2,1)S(1)}, bf16[144,256]{1,0:T(8,128)(2,1)S(1)}, u32[]{:S(2)}, u32[]{:S(2)}) collective-permute-start(bf16[144,256]{1,0:T(8,128)(2,1)S(1)} %get-tuple-element.59), channel_id=1, source_target_pairs={{0,8},{4,12},{8,0},{12,4},{16,24},{20,28},{24,16},{28,20},{1,9},{5... | collective-permute-start | bytes 221192 | tf_op jit(solution)/shard_map/ppermute | solution.py:451
  14.7 10.0 %collective-permute-start.6 = (bf16[144,256]{1,0:T(8,128)(2,1)S(1)}, bf16[144,256]{1,0:T(8,128)(2,1)S(1)}, u32[]{:S(2)}, u32[]{:S(2)}) collective-permute-start(bf16[144,256]{1,0:T(8,128)(2,1)S(1)} %get-tuple-element.82), channel_id=1, source_target_pairs={{0,24},{4,28},{8,16},{12,20},{16,8},{20,12},{24,0},{28,4},{1,25},{... | collective-permute-start | bytes 221192 | tf_op jit(solution)/shard_map/ppermute | solution.py:451
  18.3 6.5 %collective-permute-start.7 = (bf16[144,256]{1,0:T(8,128)(2,1)S(1)}, bf16[144,256]{1,0:T(8,128)(2,1)S(1)}, u32[]{:S(2)}, u32[]{:S(2)}) collective-permute-start(bf16[144,256]{1,0:T(8,128)(2,1)S(1)} %get-tuple-element.83), channel_id=1, source_target_pairs={{0,16},{4,20},{8,24},{12,28},{16,0},{20,4},{24,8},{28,12},{1,17},{... | collective-permute-start | bytes 221192 | tf_op jit(solution)/shard_map/ppermute | solution.py:451
  18.3 6.5 %collective-permute-start.8 = (bf16[144,256]{1,0:T(8,128)(2,1)S(1)}, bf16[144,256]{1,0:T(8,128)(2,1)S(1)}, u32[]{:S(2)}, u32[]{:S(2)}) collective-permute-start(bf16[144,256]{1,0:T(8,128)(2,1)S(1)} %get-tuple-element.84), channel_id=1, source_target_pairs={{0,8},{4,12},{8,0},{12,4},{16,24},{20,28},{24,16},{28,20},{1,9},{5... | collective-permute-start | bytes 221192 | tf_op jit(solution)/shard_map/ppermute | solution.py:451
  22.4 6.4 %collective-permute-start.10 = (bf16[4,128,256]{2,1,0:T(8,128)(2,1)S(1)}, bf16[4,128,256]{2,1,0:T(8,128)(2,1)S(1)}, u32[]{:S(2)}, u32[]{:S(2)}) collective-permute-start(bf16[4,128,256]{2,1,0:T(8,128)(2,1)S(1)} %get-tuple-element.89), channel_id=1, source_target_pairs={{0,4},{4,0},{8,12},{12,8},{16,20},{20,16},{24,28},{28,24},{1,5},{5... | collective-permute-start | bytes 786440 | tf_op jit(solution)/shard_map/ppermute | solution.py:451
  24.6 4.5 %collective-permute-start.4 = (bf16[128,768]{1,0:T(8,128)(2,1)S(1)}, bf16[128,768]{1,0:T(8,128)(2,1)S(1)}, u32[]{:S(2)}, u32[]{:S(2)}) collective-permute-start(bf16[128,768]{1,0:T(8,128)(2,1)S(1)} %get-tuple-element.80), channel_id=1, source_target_pairs={{0,1},{1,0},{2,3},{3,2},{4,5},{5,4},{6,7},{7,6},{8,9},{9,8},{10,11... | collective-permute-start | bytes 589832 | tf_op jit(solution)/shard_map/ppermute | solution.py:451
  26.3 2.8 %collective-permute-start.9 = (bf16[128,256]{1,0:T(8,128)(2,1)S(1)}, bf16[128,256]{1,0:T(8,128)(2,1)S(1)}, u32[]{:S(2)}, u32[]{:S(2)}) collective-permute-start(bf16[128,256]{1,0:T(8,128)(2,1)S(1)} %get-tuple-element.88), channel_id=1, source_target_pairs={{0,1},{1,0},{2,3},{3,2},{4,5},{5,4},{6,7},{7,6},{8,9},{9,8},{10,11... | collective-permute-start | bytes 196616 | tf_op jit(solution)/shard_map/ppermute | solution.py:451
  29.1 9.2 %collective-permute-start.11 = (bf16[128,768]{1,0:T(8,128)(2,1)S(1)}, bf16[128,768]{1,0:T(8,128)(2,1)S(1)}, u32[]{:S(2)}, u32[]{:S(2)}) collective-permute-start(bf16[128,768]{1,0:T(8,128)(2,1)S(1)} %get-tuple-element.92), channel_id=1, source_target_pairs={{0,2},{1,3},{2,0},{3,1},{4,6},{5,7},{6,4},{7,5},{8,10},{9,11},{10,... | collective-permute-start | bytes 589832 | tf_op jit(solution)/shard_map/ppermute | solution.py:451
  30.7 6.5 %collective-permute-start.12 = (bf16[128,256]{1,0:T(8,128)(2,1)S(1)}, bf16[128,256]{1,0:T(8,128)(2,1)S(1)}, u32[]{:S(2)}, u32[]{:S(2)}) collective-permute-start(bf16[128,256]{1,0:T(8,128)(2,1)S(1)} %get-tuple-element.93), channel_id=1, source_target_pairs={{0,24},{4,28},{8,16},{12,20},{16,8},{20,12},{24,0},{28,4},{1,25},{... | collective-permute-start | bytes 196616 | tf_op jit(solution)/shard_map/ppermute | solution.py:451
  31.9 6.4 %collective-permute-start.13 = (bf16[128,256]{1,0:T(8,128)(2,1)S(1)}, bf16[128,256]{1,0:T(8,128)(2,1)S(1)}, u32[]{:S(2)}, u32[]{:S(2)}) collective-permute-start(bf16[128,256]{1,0:T(8,128)(2,1)S(1)} %get-tuple-element.94), channel_id=1, source_target_pairs={{0,16},{4,20},{8,24},{12,28},{16,0},{20,4},{24,8},{28,12},{1,17},{... | collective-permute-start | bytes 196616 | tf_op jit(solution)/shard_map/ppermute | solution.py:451
  31.9 6.4 %collective-permute-start.14 = (bf16[128,256]{1,0:T(8,128)(2,1)S(1)}, bf16[128,256]{1,0:T(8,128)(2,1)S(1)}, u32[]{:S(2)}, u32[]{:S(2)}) collective-permute-start(bf16[128,256]{1,0:T(8,128)(2,1)S(1)} %get-tuple-element.95), channel_id=1, source_target_pairs={{0,8},{4,12},{8,0},{12,4},{16,24},{20,28},{24,16},{28,20},{1,9},{5... | collective-permute-start | bytes 196616 | tf_op jit(solution)/shard_map/ppermute | solution.py:451

commit v6 on v5

--- a/solution.py
+++ b/solution.py
@@ -109,21 +109,21 @@
     return below, above
 
 
-def write_whole(out, up, down, gain_up, gain_down):
+def write_whole(out, up, down, gains):
     n = up.shape[0]
     out[0:n] = up.astype(BF16)
     out[n : 2 * n] = down.astype(BF16)
-    out[2 * n :] = gain_block(gain_up, gain_down)
-
-
-def write_halves(outs, up, down, gain_up, gain_down, me):
+    if gains:
+        out[2 * n :] = gain_block(*gains)
+
+
+def write_halves(outs, up, down, gains, me):
     n = up.shape[0]
-    blocks = gain_block(gain_up), gain_block(gain_down)
     up, down = up.astype(BF16), down.astype(BF16)
     for j, out in enumerate(outs, start=1):
-        upward = (me ^ j) > me
-        out[0:n] = jnp.where(upward, up, down)
-        out[n:] = jnp.where(upward, *blocks)
+        out[0:n] = jnp.where((me ^ j) > me, up, down)
+        if gains:
+            out[n:] = gain_block(*gains)
 
 
 def write_chunk(outs, me, last, *chunk):
@@ -157,7 +157,7 @@
     gyf = gy[...].astype(F32)
     up = nn(cb[...].T, (gyf * grow_b).astype(BF16))
     down = nn(ca[...].T, (gyf * grow_a).astype(BF16))
-    write_chunk(sends, me, last, up, down, grow_b[0:1], grow_a[gyf.shape[0] - 1 :])
+    write_chunk(sends, me, last, up, down, (grow_a[gyf.shape[0] - 1 :], grow_b[0:1]))
 
 
 def state_kernel(me, last, *refs):
@@ -173,23 +173,24 @@
     xf = x.astype(F32)
     up = nn(ba[...].T, (xf * factors[1]).astype(BF16))
     down = nn(bb[...].T, (xf * factors[3]).astype(BF16))
-    write_chunk(sends, me, last, up, down, factors[0, x.shape[0] - 1 :], factors[2, 0:1])
-
-
-def step_kernel(index, stride, radix, first, next_last, next_radix, *refs):
+    write_chunk(sends, me, last, up, down, ())
+
+
+def step_kernel(index, stride, radix, first, next_last, next_radix, states, *refs):
     refs = list(refs)
-    own = refs.pop(0)
-    received = [refs.pop(0) for _ in range(radix - 1)]
+    members_in = [refs.pop(0) for _ in range(radix)]
+    gains_in = [refs.pop(0) for _ in range(radix)] if states else members_in
     before, outs = refs[0], refs[-(next_radix if next_last else 2) :]
     pre_out, *outs = outs
-    n = (own.shape[0] - GAIN_ROWS) // 2
+    n = (gains_in[0].shape[0] - GAIN_ROWS) // 2
     seq = index()
     me = digit(seq, stride, radix)
     members = [me ^ j for j in range(radix)]
-    loaded = [(ref[0:n].astype(F32), ref[n : 2 * n].astype(F32)) for ref in [own] + received]
-    gains = [[read_gain(ref[2 * n :], k) for ref in [own] + received] for k in range(2)]
+    loaded = [(ref[0:n].astype(F32), ref[n : 2 * n].astype(F32)) for ref in members_in]
+    both = [[read_gain(ref[2 * n :], k) for ref in gains_in] for k in range(2)]
+    gains = both if states else both[::-1]
     coefficients = merge_coefficients(me, members, *gains)
-    width = own.shape[1]
+    width = members_in[0].shape[1]
     new_grow = []
     totals = []
     for down in range(2):
@@ -209,8 +210,8 @@
             group = group + product_where(outer, [gains[down][i] for i in rest]) * loaded[j][down]
         totals.append(group)
     pre_out[2 * n :] = jnp.concatenate(new_grow + [jnp.zeros((6, width), F32)], axis=0)
-    gain = [functools.reduce(lambda a, b: a * b, gains[k]) for k in range(2)]
-    write_chunk(outs, lambda: digit(seq, stride * radix, next_radix), next_last, *totals, *gain)
+    new = () if states else [functools.reduce(lambda a, b: a * b, both[k]) for k in range(2)]
+    write_chunk(outs, lambda: digit(seq, stride * radix, next_radix), next_last, *totals, new)
 
 
 def local_kernel(
@@ -262,44 +263,38 @@
     turned_out[...] = features[...].T
 
 
-def entering(chunks, seq, peers, n):
-    results = []
-    for received, before in chunks:
-        radix = len(received) + 1
-        me = digit(seq, peers // radix, radix)
-        members = [me ^ j for j in range(radix)]
-        gains = [read_gain(ref[n:]) for ref in received]
-        gains = gains[:1] + gains
-        coefficients = merge_coefficients(me, members, gains, gains)
-
-        def enter(down, received=received, before=before, coefficients=coefficients):
-            total = 0.0
-            for coefficient, ref in zip(coefficients[down], received):
-                total = total + coefficient * ref[0:n].astype(F32)
-            if before is not None:
-                total = before[2 * n + down : 2 * n + down + 1] * total + before[down * n : (down + 1) * n]
-            return total
-
-        results.append(enter)
-    return results
-
-
-def take_chunks(refs, lasts, first):
-    chunks = []
-    for radix in lasts:
-        received = [refs.pop(0) for _ in range(radix - 1)][::-1]
-        chunks.append((received, None if first else refs.pop(0)))
-    return chunks
+def entering(received, decays, before, seq, peers, n, states):
+    radix = len(received) + 1
+    me = digit(seq, peers // radix, radix)
+    members = [me ^ j for j in range(radix)]
+    ahead, behind = [[read_gain(ref[n:], k) for ref in decays[:1] + decays] for k in range(2)]
+    gains = (ahead, behind) if states else (behind, ahead)
+    coefficients = merge_coefficients(me, members, *gains)
+
+    def enter(down):
+        total = 0.0
+        for coefficient, ref in zip(coefficients[down], received):
+            total = total + coefficient * ref[0:n].astype(F32)
+        if before is not None:
+            total = before[2 * n + down : 2 * n + down + 1] * total + before[down * n : (down + 1) * n]
+        return total
+
+    return enter
+
+
+def take_chunk(refs, radix, first):
+    received = [refs.pop(0) for _ in range(radix - 1)][::-1]
+    return received, None if first else refs.pop(0)
 
 
 def carry_kernel(index, steps, stride, direct, *refs):
     refs = list(refs)
-    chunks = take_chunks(refs, steps[-1:], len(steps) == 1)
-    turned, ba, bb, gx_local, factors = refs[:5]
-    gx_out, grad_out, *outs = refs[-steps[0] - 1 :] if direct else refs[-3:]
+    received, before = take_chunk(refs, steps[-1], len(steps) == 1)
+    turned, ba, bb, gx_local, factors = [refs.pop(0) for _ in range(5)]
+    gx_out, grad_out, *outs = refs
     seq = index()
     me = digit(seq, stride, steps[-1])
-    (gradient,) = entering(chunks, seq, stride * steps[-1], ba.shape[1])
+    gradient = entering(received, received, before, seq, stride * steps[-1], ba.shape[1], False)
     grad_x = gx_local[...]
     for k, (b, left) in enumerate(((ba, factors[1]), (bb, factors[3]))):
         grad = gradient(1 - k).astype(BF16)
@@ -334,7 +329,7 @@
 
 
 def share_kernel(index, n_head, grad_x, grads, x, w_in, ba, bb, maps_local, decay_local, factors, *outs):
-    decay_out, own_out, send_out = outs
+    decay_out, maps_out, own_out, send_out = outs
     heads = decay_local.shape[0]
     n = ba.shape[1]
     length, columns = x.shape
@@ -342,7 +337,6 @@
     row, col = iotas(length, length)
     group = head_groups(heads, columns)
     rows_out = w_in.shape[0] // n_head
-    half = n_head // 2 * rows_out
     for k, (b, earlier) in enumerate(((ba, row < col), (bb, row > col))):
         left, grad = factors[2 * k + 1], grads[k]
         write = nn(b[...], grad).astype(BF16).astype(F32) * left * xf
@@ -350,9 +344,7 @@
         part = slice(k * length, (k + 1) * length)
         decay_out[:, part] = decay_local[:, part] + nn(writes, earlier.astype(F32), precision=HIGH)[:heads]
         grad_b = maps_local[:, 2 * k * n : (2 * k + 1) * n] + nt((xf * left).astype(BF16), grad)
-        at = half + k * n
-        own_out[:, at : at + n] = grad_b
-        send_out[:, at : at + n] = grad_b.astype(BF16)
+        maps_out[:, k * n : (k + 1) * n] = grad_b
     for high in range(n_head // 2):
         part = slice(high * rows_out, (high + 1) * rows_out)
         for away in range(2):
@@ -366,13 +358,14 @@
 
 def state_share_kernel(index, steps, peers, *refs):
     refs = list(refs)
-    chunks = take_chunks(refs, steps[-1:], len(steps) == 1)
-    grads, gy, ca, cb, maps_local, decay_part, factors = [refs.pop(0) for _ in range(7)]
+    received, before = take_chunk(refs, steps[-1], len(steps) == 1)
+    decays, _ = take_chunk(refs, steps[-1], True)
+    grads, gy, ca, cb, maps_local, maps_b, decay_part, factors = [refs.pop(0) for _ in range(8)]
     *gd_outs, own_out, send_out = refs
     heads = decay_part.shape[0]
     n = ca.shape[1]
     length, columns = gy.shape
-    (state,) = entering(chunks, index(), peers, n)
+    state = entering(received, decays, before, index(), peers, n, True)
     gyf = gy[...].astype(F32)
     row, col = iotas(length, length)
     group = head_groups(heads, columns)
@@ -387,8 +380,9 @@
         gd = nn(reads, later.astype(F32), precision=HIGH)[:heads]
         gd_outs[k][...] = gd + decay_part[:, k * length : (k + 1) * length]
         grad_c = maps_local[:, (2 * k + 1) * n : (2 * k + 2) * n] + nt((gyf * grow).astype(BF16), low)
-        own_out[:, k * n : (k + 1) * n] = grad_c
-        send_out[:, k * n : (k + 1) * n] = grad_c.astype(BF16)
+        for at, value in ((2 * k, maps_b[:, k * n : (k + 1) * n]), (2 * k + 1, grad_c)):
+            own_out[:, at * n : (at + 1) * n] = value
+            send_out[:, at * n : (at + 1) * n] = value.astype(BF16)
 
 
 def pair_kernel(index, stride, rows_out, blocks, count, *refs):
@@ -397,11 +391,10 @@
     own, received = parts[0], parts[1]
     at = blocks * rows_out
     half = at // 2
-    maps = []
-    for mine, other in zip(parts[0::2], parts[1::2]):
-        maps.append(mine[:, at:] + other[:, at:].astype(F32))
-        at = 0
-    maps = jnp.concatenate(maps, axis=1)
+    if count == 4:
+        maps = parts[2][...] + parts[3][...].astype(F32)
+    else:
+        maps = own[:, at:] + received[:, at:].astype(F32)
     own_out[:, half:] = maps
     send_out[:, half:] = maps.astype(BF16)
     for high in range(blocks // 2):
@@ -419,7 +412,7 @@
     parts, gf_out, gw_out, map_outs = refs[:-6], refs[-6], refs[-5], refs[-4:]
     columns, n = gf_out.shape[1], map_outs[0].shape[1]
     gf_out[...] = (own[:, 0:columns] + other[:, 0:columns].astype(F32)).astype(BF16)
-    for k, out in enumerate((map_outs[0], map_outs[2], map_outs[1], map_outs[3])):
+    for k, out in enumerate(map_outs):
         at = columns + k * n
         out[...] = own[:, at : at + n] + other[:, at : at + n].astype(F32)
     total = 0.0
@@ -467,6 +460,7 @@
     square = shape((length, columns), BF16)
     whole = shape((2 * n + GAIN_ROWS, columns), BF16)
     half = shape((n + GAIN_ROWS, columns), BF16)
+    state_whole, state_half = shape((2 * n, columns), BF16), shape((n, columns), BF16)
     prefix = shape((2 * n + 8, columns), F32)
 
     steps = radices(peers)
@@ -481,7 +475,7 @@
     )
     *states, x, ba, bb, fs, wi = call(
         functools.partial(state_kernel, seq_index, only),
-        chunk_shapes + [square],
+        ([state_half] * (steps[0] - 1) if only else [state_whole]) + [square],
         b_ahead, b_behind, features, w_in, factors,
         micros=1.65,
         held=4,
@@ -498,25 +492,29 @@
         skip, x, gy, fs, *maps, da, db,
         micros=0.9,
     )
-    def merges(chunk):
-        stride, before = 1, None
+    def merges(chunk, decays):
+        stride, before, seen = 1, None, []
+        whole_shape, half_shape = (state_whole, state_half) if decays else (whole, half)
         for at, radix in enumerate(steps[:-1]):
-            received = [swap(chunk[0], "seq", j * stride) for j in range(1, radix)]
+            members = [chunk[0]] + [swap(chunk[0], "seq", j * stride) for j in range(1, radix)]
+            seen.append(members)
             next_last = at == len(steps) - 2
             following = steps[at + 1]
-            count = (following - 1) if next_last else 1
             before, *chunk = call(
-                functools.partial(step_kernel, seq_index, stride, radix, at == 0, next_last, following),
-                [prefix] + ([half] if next_last else [whole]) * count,
-                chunk[0], *received, *([] if at == 0 else [before]),
+                functools.partial(
+                    step_kernel, seq_index, stride, radix, at == 0, next_last, following, bool(decays)
+                ),
+                [prefix] + ([half_shape] * (following - 1) if next_last else [whole_shape]),
+                *members, *(decays[at] if decays else []), *([] if at == 0 else [before]),
                 micros=0.15,
             )
             stride *= radix
-        return far_first(chunk, stride) + ([] if only else [before])
+        return far_first(chunk, stride), [] if only else [before], seen
 
     stride = peers // steps[-1]
-    gradient_in = merges(gradients)
-    state_in = merges(states)
+    gradients, gradient_before, seen = merges(gradients, None)
+    states, state_before, _ = merges(states, seen) if not only else (far_first(states, stride), [], [])
+    gradient_in, state_in = gradients + gradient_before, states + state_before + gradients
     rows_out, rows_w = depth // n_head, depth // peers
     direct = len(steps) == 2 and rows_w % 16 == 0
     pieces = [shape((4, rows_w, columns), BF16)] * (steps[0] - 1) if direct else [shape((depth, columns), BF16)]
@@ -526,34 +524,33 @@
         *gradient_in, turned, ba, bb, gx_local, factors,
         micros=0.5,
     )
-    def head_shapes(blocks, maps):
-        wide = (length, blocks * rows_out + maps * n)
-        return [shape(wide, F32), shape(wide, BF16)]
-
-    decay_part, own, send = call(
+    def both(width):
+        return [shape((length, width), F32), shape((length, width), BF16)]
+
+    decay_part, maps_b, own, send = call(
         functools.partial(share_kernel, head_index, n_head),
-        [shape((heads, 2 * length), F32)] + head_shapes(n_head // 2, 2),
+        [shape((heads, 2 * length), F32), shape((length, 2 * n), F32)] + both(n_head // 2 * rows_out),
         grad_x, grads, x, wi, ba, bb, maps_local, decay_local, factors,
         micros=1.0,
     )
     shares = [own, swap(send, "head", 1)]
-    received = [swap(send, "seq", j) for j, send in enumerate(sends, start=1)] if direct else []
     gd_ahead, gd_behind, own, send = call(
         functools.partial(state_share_kernel, seq_index, steps, peers),
-        [shape((heads, length), F32)] * 2 + head_shapes(0, 2),
-        *state_in, grads, gy, ca, cb, maps_local, decay_part, factors,
+        [shape((heads, length), F32)] * 2 + both(4 * n),
+        *state_in, grads, gy, ca, cb, maps_local, maps_b, decay_part, factors,
         micros=1.4,
     )
     shares += [own, swap(send, "head", 1)]
     after = []
     if direct:
+        received = [swap(send, "seq", j) for j, send in enumerate(sends, start=1)]
         own_weight, *sends = call(
             functools.partial(fold_kernel, seq_index, steps),
             [shape((rows_w, columns), F32)] + [shape((rows_w, columns), BF16)] * 3,
             turned, grad_x, *received, own,
             micros=0.22,
         )
-        weight_parts = [own_weight] + far_first(sends, stride)
+        weight_parts = far_first(sends, stride) + [own_weight]
         after = [own_weight]
     else:
         weight_parts = [lax.all_to_all(sends[0].reshape(peers, rows_w, columns), "seq", 0, 0)]
@@ -561,7 +558,7 @@
     while mask < n_head:
         own, send = call(
             functools.partial(pair_kernel, head_index, mask, rows_out, blocks, len(shares)),
-            head_shapes(blocks // 2, 4),
+            both(blocks // 2 * rows_out + 4 * n),
             *shares, *after,
             micros=0.25,
         )

time: 39.3 us -> 38.9 us (0.990)
  waiting for transfers between devices: 10.7 us -> 10.2 us
    ppermute x15, waiting for transfers between devices: 10.7 us -> 10.2 us  [swap(): lax.ppermute(value, axis, [(i, i ^ mask) for i in range(lax.axis_size(axi...]
  transfers between devices with their start and end apart: 15 -> 15, of which waited for: 6 -> 5; matrix products, arithmetic and copies ran while one was open for 0% -> 0% of each run, Pallas kernels for 15% -> 15%
where the time goes in v6:
time: 38.9 us; the launch traced here: 38.7 us
  starting transfers between devices  19.7 us (51%)
  waiting for transfers between devices  10.2 us (26%)
  Pallas kernels  8.06 us (21%)
  between operations  0.76 us (2%)
    ppermute x15, starting transfers between devices, swap(): lax.ppermute(value, axis, [(i, i ^ mask) for i in range(lax.axis_size(axi...  19.7 us
    ppermute x15, waiting for transfers between devices, swap(): lax.ppermute(value, axis, [(i, i ^ mask) for i in range(lax.axis_size(axi...  10.2 us
    pallas_call x11, Pallas kernels, call(): pl.pallas_call(kernel, out_shape=outs, in_specs=specs, out_specs=[pl.Bloc...  8.06 us
  transfers between devices with their start and end apart: 15, of which 5 were waited for; matrix products, arithmetic and copies ran while one was open for 0% of the time, Pallas kernels for 15%

profile of v6, /device:TPU:0, one launch (start us, length us, event | category | flops | bytes accessed | tf_op | source)
XLA Modules:
  0.0 38.7 jit_solution(6523088707836665052)
XLA Ops:
  0.6 1.4 %shard_map.161 = (bf16[272,256]{1,0:T(8,128)(2,1)S(1)}, f32[4,128,256]{2,1,0:T(8,128)S(1)}, f32[4,128]{1,0:T(4,128)S(1)}, f32[4,128]{1,0:T(4,128)S(1)}, bf16[128...) custom-call(f32[4,128]{1,0:T(4,128)} %refs_0_.2, ...), custom_call_target="tpu_custom_call" | custom-call | flops 1552499968 | tf_op jit(solution)/shard_map/pallas_call | solution.py:432
  2.0 3.0 %collective-permute-start = (bf16[272,256]{1,0:T(8,128)(2,1)S(1)}, bf16[272,256]{1,0:T(8,128)(2,1)S(1)}, u32[]{:S(2)}, u32[]{:S(2)}) collective-permute-start(bf16[272,256]{1,0:T(8,128)(2,1)S(1)} %get-tuple-element.57.refs_0_.refs_2_), channel_id=1, source_target_pairs={{0,4},{4,0},{8,12},{12,8},{16,20},{20,16},{24,28},{28,24},{1,5},{5... | collective-permute-start | bytes 417800 | tf_op jit(solution)/shard_map/ppermute | solution.py:444
  5.0 1.7 %shard_map.163 = (bf16[256,256]{1,0:T(8,128)(2,1)S(1)}, bf16[128,256]{1,0:T(8,128)(2,1)S(1)}, bf16[128,128]{1,0:T(8,128)(2,1)S(1)}, bf16[128,128]{1,0:T(8,128)(2...) custom-call(bf16[128,128]{1,0:T(8,128)(2,1)} %refs_0_.3, bf16[128,128]{1,0:T(8,128)(2,1)} %refs_1_.3, ...), custom_call_target="tpu_custom_call" | custom-call | flops 1897500032 | tf_op jit(solution)/shard_map/pallas_call | solution.py:432
  6.8 2.3 %collective-permute-done.refs_1_.refs_3_ = bf16[272,256]{1,0:T(8,128)(2,1)S(1)} collective-permute-done((bf16[272,256]{1,0:T(8,128)(2,1)S(1)}, bf16[272,256]{1,0:T(8,128)(2,1)S(1)}, u32[]{:S(2)}, u32[]{:S(2)}) %collective-permute-start) | collective-permute-done | bytes 139296 | tf_op jit(solution)/shard_map/ppermute | solution.py:444
  9.1 0.1 shard_map.162
  9.2 3.6 %collective-permute-start.1 = (bf16[144,256]{1,0:T(8,128)(2,1)S(1)}, bf16[144,256]{1,0:T(8,128)(2,1)S(1)}, u32[]{:S(2)}, u32[]{:S(2)}) collective-permute-start(bf16[144,256]{1,0:T(8,128)(2,1)S(1)} %get-tuple-element.58), channel_id=1, source_target_pairs={{0,24},{4,28},{8,16},{12,20},{16,8},{20,12},{24,0},{28,4},{1,25},{... | collective-permute-start | bytes 221192 | tf_op jit(solution)/shard_map/ppermute | solution.py:444
  12.8 0.9 %collective-permute-start.3 = (bf16[144,256]{1,0:T(8,128)(2,1)S(1)}, bf16[144,256]{1,0:T(8,128)(2,1)S(1)}, u32[]{:S(2)}, u32[]{:S(2)}) collective-permute-start(bf16[144,256]{1,0:T(8,128)(2,1)S(1)} %get-tuple-element.60), channel_id=1, source_target_pairs={{0,8},{4,12},{8,0},{12,4},{16,24},{20,28},{24,16},{28,20},{1,9},{5... | collective-permute-start | bytes 221192 | tf_op jit(solution)/shard_map/ppermute | solution.py:444
  13.7 0.9 %shard_map.164 = (f32[128,256]{1,0:T(8,128)S(1)}, f32[128,512]{1,0:T(8,128)S(1)}, f32[4,256]{1,0:T(4,128)S(1)}, bf16[1024,128]{1,0:T(8,128)(2,1)S(1)}) custom-call(f32[1,4]{1,0:T(1,128)S(1)} %get-tuple-element.62.skip, bf16[128,256]{1,0:T(8,128)(2,1)S(1)} %get-tuple-element.64.x, bf16[128,256]{1,0:T(8,128)(2,1)S(1)} %get-tuple-element.65.gy.refs_8_, ...), custom_call_target="tpu_custom_call" | custom-call | flops 1035000000 | tf_op jit(solution)/shard_map/pallas_call | solution.py:432
  14.7 3.6 %collective-permute-start.6 = (bf16[128,256]{1,0:T(8,128)(2,1)S(1)}, bf16[128,256]{1,0:T(8,128)(2,1)S(1)}, u32[]{:S(2)}, u32[]{:S(2)}) collective-permute-start(bf16[128,256]{1,0:T(8,128)(2,1)S(1)} %get-tuple-element.83), channel_id=1, source_target_pairs={{0,24},{4,28},{8,16},{12,20},{16,8},{20,12},{24,0},{28,4},{1,25},{... | collective-permute-start | bytes 196616 | tf_op jit(solution)/shard_map/ppermute | solution.py:444
  18.3 0.9 %collective-permute-start.8 = (bf16[128,256]{1,0:T(8,128)(2,1)S(1)}, bf16[128,256]{1,0:T(8,128)(2,1)S(1)}, u32[]{:S(2)}, u32[]{:S(2)}) collective-permute-start(bf16[128,256]{1,0:T(8,128)(2,1)S(1)} %get-tuple-element.85), channel_id=1, source_target_pairs={{0,8},{4,12},{8,0},{12,4},{16,24},{20,28},{24,16},{28,20},{1,9},{5... | collective-permute-start | bytes 196616 | tf_op jit(solution)/shard_map/ppermute | solution.py:444
  19.2 2.2 %collective-permute-done.2.refs_1_.refs_5_ = bf16[144,256]{1,0:T(8,128)(2,1)S(1)} collective-permute-done((bf16[144,256]{1,0:T(8,128)(2,1)S(1)}, bf16[144,256]{1,0:T(8,128)(2,1)S(1)}, u32[]{:S(2)}, u32[]{:S(2)}) %collective-permute-start.2) | collective-permute-done | bytes 73760 | tf_op jit(solution)/shard_map/ppermute | solution.py:444
  21.4 0.5 %shard_map.165 = (bf16[128,256]{1,0:T(8,128)(2,1)S(1)}, bf16[2,128,256]{2,1,0:T(8,128)(2,1)S(1)}, bf16[4,128,256]{2,1,0:T(8,128)(2,1)S(1)}) custom-call(bf16[144,256]{1,0:T(8,128)(2,1)S(1)} %collective-permute-done.1.refs_0_.refs_4_, bf16[144,256]{1,0:T(8,128)(2,1)S(1)} %collective-permute-done.2.refs_1_.refs_5_, ...), custom_call_target="tpu_custom_call" | custom-call | flops 575000000 | tf_op jit(solution)/shard_map/pallas_call | solution.py:432
  21.9 1.3 %collective-permute-start.10 = (bf16[4,128,256]{2,1,0:T(8,128)(2,1)S(1)}, bf16[4,128,256]{2,1,0:T(8,128)(2,1)S(1)}, u32[]{:S(2)}, u32[]{:S(2)}) collective-permute-start(bf16[4,128,256]{2,1,0:T(8,128)(2,1)S(1)} %get-tuple-element.91), channel_id=1, source_target_pairs={{0,4},{4,0},{8,12},{12,8},{16,20},{20,16},{24,28},{28,24},{1,5},{5... | collective-permute-start | bytes 786440 | tf_op jit(solution)/shard_map/ppermute | solution.py:444
  23.2 1.0 %shard_map.166 = (f32[4,256]{1,0:T(4,128)S(1)}, f32[128,256]{1,0:T(8,128)S(1)}, f32[128,512]{1,0:T(8,128)S(1)}, bf16[128,512]{1,0:T(8,128)(2,1)S(1)}) custom-call(bf16[128,256]{1,0:T(8,128)(2,1)S(1)} %get-tuple-element.75.grad_x, bf16[2,128,256]{2,1,0:T(8,128)(2,1)S(1)} %get-tuple-element.76.grads.refs_7_, bf16[128,256]{1,0:T(8,128)(2,1)S(1)} %get-tuple-element.64.x, ...), custom_call_target="tpu_custom_call" | custom-call | flops 1150000000 | tf_op jit(solution)/shard_map/pallas_call | solution.py:432
  24.2 1.4 %shard_map.168 = (f32[4,128]{1,0:T(4,128)}, f32[4,128]{1,0:T(4,128)}, f32[128,512]{1,0:T(8,128)S(1)}, bf16[128,512]{1,0:T(8,128)(2,1)S(1)}) custom-call(bf16[128,256]{1,0:T(8,128)(2,1)S(1)} %collective-permute-done.6.refs_0_, bf16[128,256]{1,0:T(8,128)(2,1)S(1)} %collective-permute-done.7.refs_1_, bf16[128,256]{1,0:T(8,128)(2,1)S(1)} %collective-permute-done.8.refs_2_, ...), custom_call_target="tpu_custom_call" | custom-call | flops 1610000000 | tf_op jit(solution)/shard_map/pallas_call | solution.py:432
  25.6 0.5 %collective-permute-start.4 = (bf16[128,512]{1,0:T(8,128)(2,1)S(1)}, bf16[128,512]{1,0:T(8,128)(2,1)S(1)}, u32[]{:S(2)}, u32[]{:S(2)}) collective-permute-start(bf16[128,512]{1,0:T(8,128)(2,1)S(1)} %get-tuple-element.81), channel_id=1, source_target_pairs={{0,1},{1,0},{2,3},{3,2},{4,5},{5,4},{6,7},{7,6},{8,9},{9,8},{10,11... | collective-permute-start | bytes 393224 | tf_op jit(solution)/shard_map/ppermute | solution.py:444
  26.1 2.2 %collective-permute-done.10.refs_0_ = bf16[4,128,256]{2,1,0:T(8,128)(2,1)S(1)} collective-permute-done((bf16[4,128,256]{2,1,0:T(8,128)(2,1)S(1)}, bf16[4,128,256]{2,1,0:T(8,128)(2,1)S(1)}, u32[]{:S(2)}, u32[]{:S(2)}) %collective-permute-start.10) | collective-permute-done | bytes 262176 | tf_op jit(solution)/shard_map/ppermute | solution.py:444
  28.3 0.2 shard_map.169
  28.6 1.5 %collective-permute-start.11 = (bf16[128,768]{1,0:T(8,128)(2,1)S(1)}, bf16[128,768]{1,0:T(8,128)(2,1)S(1)}, u32[]{:S(2)}, u32[]{:S(2)}) collective-permute-start(bf16[128,768]{1,0:T(8,128)(2,1)S(1)} %get-tuple-element.94), channel_id=1, source_target_pairs={{0,2},{1,3},{2,0},{3,1},{4,6},{5,7},{6,4},{7,5},{8,10},{9,11},{10,... | collective-permute-start | bytes 589832 | tf_op jit(solution)/shard_map/ppermute | solution.py:444
  30.1 1.8 %collective-permute-start.12 = (bf16[128,256]{1,0:T(8,128)(2,1)S(1)}, bf16[128,256]{1,0:T(8,128)(2,1)S(1)}, u32[]{:S(2)}, u32[]{:S(2)}) collective-permute-start(bf16[128,256]{1,0:T(8,128)(2,1)S(1)} %get-tuple-element.95), channel_id=1, source_target_pairs={{0,24},{4,28},{8,16},{12,20},{16,8},{20,12},{24,0},{28,4},{1,25},{... | collective-permute-start | bytes 196616 | tf_op jit(solution)/shard_map/ppermute | solution.py:444
  31.9 2.6 %collective-permute-start.14 = (bf16[128,256]{1,0:T(8,128)(2,1)S(1)}, bf16[128,256]{1,0:T(8,128)(2,1)S(1)}, u32[]{:S(2)}, u32[]{:S(2)}) collective-permute-start(bf16[128,256]{1,0:T(8,128)(2,1)S(1)} %get-tuple-element.97), channel_id=1, source_target_pairs={{0,8},{4,12},{8,0},{12,4},{16,24},{20,28},{24,16},{28,20},{1,9},{5... | collective-permute-start | bytes 196616 | tf_op jit(solution)/shard_map/ppermute | solution.py:444
  34.5 2.2 %collective-permute-done.12.refs_0_ = bf16[128,256]{1,0:T(8,128)(2,1)S(1)} collective-permute-done((bf16[128,256]{1,0:T(8,128)(2,1)S(1)}, bf16[128,256]{1,0:T(8,128)(2,1)S(1)}, u32[]{:S(2)}, u32[]{:S(2)}) %collective-permute-start.12) | collective-permute-done | bytes 65568 | tf_op jit(solution)/shard_map/ppermute | solution.py:444
  36.7 1.2 %collective-permute-done.13.refs_1_ = bf16[128,256]{1,0:T(8,128)(2,1)S(1)} collective-permute-done((bf16[128,256]{1,0:T(8,128)(2,1)S(1)}, bf16[128,256]{1,0:T(8,128)(2,1)S(1)}, u32[]{:S(2)}, u32[]{:S(2)}) %collective-permute-start.13) | collective-permute-done | bytes 65568 | tf_op jit(solution)/shard_map/ppermute | solution.py:444
  37.9 0.8 %shard_map.171 = (bf16[128,256]{1,0:T(8,128)(2,1)}, f32[128,256]{1,0:T(8,128)}, f32[128,128]{1,0:T(8,128)}, f32[128,128]{1,0:T(8,128)}, f32[128,128]{1,0:T(8,128)}, /*index=5*/f32[128,128]{1,0:T(8,128)}) custom-call(f32[128,768]{1,0:T(8,128)S(1)} %get-tuple-element.93.own, bf16[128,768]{1,0:T(8,128)(2,1)S(1)} %collective-permute-done.11.other, ...), custom_call_target="tpu_custom_call" | custom-call | flops 920000000 | tf_op jit(solution)/shard_map/pallas_call | solution.py:432
  (17 shorter events, 0.3 us)
Async XLA Ops:
  2.0 7.1 %collective-permute-start = (bf16[272,256]{1,0:T(8,128)(2,1)S(1)}, bf16[272,256]{1,0:T(8,128)(2,1)S(1)}, u32[]{:S(2)}, u32[]{:S(2)}) collective-permute-start(bf16[272,256]{1,0:T(8,128)(2,1)S(1)} %get-tuple-element.57.refs_0_.refs_2_), channel_id=1, source_target_pairs={{0,4},{4,0},{8,12},{12,8},{16,20},{20,16},{24,28},{28,24},{1,5},{5... | collective-permute-start | bytes 417800 | tf_op jit(solution)/shard_map/ppermute | solution.py:444
  6.7 7.9 %collective-permute-start.5 = (bf16[256,256]{1,0:T(8,128)(2,1)S(1)}, bf16[256,256]{1,0:T(8,128)(2,1)S(1)}, u32[]{:S(2)}, u32[]{:S(2)}) collective-permute-start(bf16[256,256]{1,0:T(8,128)(2,1)S(1)} %get-tuple-element.82.refs_0_), channel_id=1, source_target_pairs={{0,4},{4,0},{8,12},{12,8},{16,20},{20,16},{24,28},{28,24},{1,5},{5... | collective-permute-start | bytes 393224 | tf_op jit(solution)/shard_map/ppermute | solution.py:444
  9.2 9.1 %collective-permute-start.1 = (bf16[144,256]{1,0:T(8,128)(2,1)S(1)}, bf16[144,256]{1,0:T(8,128)(2,1)S(1)}, u32[]{:S(2)}, u32[]{:S(2)}) collective-permute-start(bf16[144,256]{1,0:T(8,128)(2,1)S(1)} %get-tuple-element.58), channel_id=1, source_target_pairs={{0,24},{4,28},{8,16},{12,20},{16,8},{20,12},{24,0},{28,4},{1,25},{... | collective-permute-start | bytes 221192 | tf_op jit(solution)/shard_map/ppermute | solution.py:444
  12.8 8.6 %collective-permute-start.2 = (bf16[144,256]{1,0:T(8,128)(2,1)S(1)}, bf16[144,256]{1,0:T(8,128)(2,1)S(1)}, u32[]{:S(2)}, u32[]{:S(2)}) collective-permute-start(bf16[144,256]{1,0:T(8,128)(2,1)S(1)} %get-tuple-element.59), channel_id=1, source_target_pairs={{0,16},{4,20},{8,24},{12,28},{16,0},{20,4},{24,8},{28,12},{1,17},{... | collective-permute-start | bytes 221192 | tf_op jit(solution)/shard_map/ppermute | solution.py:444
  12.8 8.6 %collective-permute-start.3 = (bf16[144,256]{1,0:T(8,128)(2,1)S(1)}, bf16[144,256]{1,0:T(8,128)(2,1)S(1)}, u32[]{:S(2)}, u32[]{:S(2)}) collective-permute-start(bf16[144,256]{1,0:T(8,128)(2,1)S(1)} %get-tuple-element.60), channel_id=1, source_target_pairs={{0,8},{4,12},{8,0},{12,4},{16,24},{20,28},{24,16},{28,20},{1,9},{5... | collective-permute-start | bytes 221192 | tf_op jit(solution)/shard_map/ppermute | solution.py:444
  14.7 9.5 %collective-permute-start.6 = (bf16[128,256]{1,0:T(8,128)(2,1)S(1)}, bf16[128,256]{1,0:T(8,128)(2,1)S(1)}, u32[]{:S(2)}, u32[]{:S(2)}) collective-permute-start(bf16[128,256]{1,0:T(8,128)(2,1)S(1)} %get-tuple-element.83), channel_id=1, source_target_pairs={{0,24},{4,28},{8,16},{12,20},{16,8},{20,12},{24,0},{28,4},{1,25},{... | collective-permute-start | bytes 196616 | tf_op jit(solution)/shard_map/ppermute | solution.py:444
  18.3 5.9 %collective-permute-start.7 = (bf16[128,256]{1,0:T(8,128)(2,1)S(1)}, bf16[128,256]{1,0:T(8,128)(2,1)S(1)}, u32[]{:S(2)}, u32[]{:S(2)}) collective-permute-start(bf16[128,256]{1,0:T(8,128)(2,1)S(1)} %get-tuple-element.84), channel_id=1, source_target_pairs={{0,16},{4,20},{8,24},{12,28},{16,0},{20,4},{24,8},{28,12},{1,17},{... | collective-permute-start | bytes 196616 | tf_op jit(solution)/shard_map/ppermute | solution.py:444
  18.3 5.9 %collective-permute-start.8 = (bf16[128,256]{1,0:T(8,128)(2,1)S(1)}, bf16[128,256]{1,0:T(8,128)(2,1)S(1)}, u32[]{:S(2)}, u32[]{:S(2)}) collective-permute-start(bf16[128,256]{1,0:T(8,128)(2,1)S(1)} %get-tuple-element.85), channel_id=1, source_target_pairs={{0,8},{4,12},{8,0},{12,4},{16,24},{20,28},{24,16},{28,20},{1,9},{5... | collective-permute-start | bytes 196616 | tf_op jit(solution)/shard_map/ppermute | solution.py:444
  21.9 6.4 %collective-permute-start.10 = (bf16[4,128,256]{2,1,0:T(8,128)(2,1)S(1)}, bf16[4,128,256]{2,1,0:T(8,128)(2,1)S(1)}, u32[]{:S(2)}, u32[]{:S(2)}) collective-permute-start(bf16[4,128,256]{2,1,0:T(8,128)(2,1)S(1)} %get-tuple-element.91), channel_id=1, source_target_pairs={{0,4},{4,0},{8,12},{12,8},{16,20},{20,16},{24,28},{28,24},{1,5},{5... | collective-permute-start | bytes 786440 | tf_op jit(solution)/shard_map/ppermute | solution.py:444
  25.6 2.9 %collective-permute-start.9 = (bf16[128,512]{1,0:T(8,128)(2,1)S(1)}, bf16[128,512]{1,0:T(8,128)(2,1)S(1)}, u32[]{:S(2)}, u32[]{:S(2)}) collective-permute-start(bf16[128,512]{1,0:T(8,128)(2,1)S(1)} %get-tuple-element.90), channel_id=1, source_target_pairs={{0,1},{1,0},{2,3},{3,2},{4,5},{5,4},{6,7},{7,6},{8,9},{9,8},{10,11... | collective-permute-start | bytes 393224 | tf_op jit(solution)/shard_map/ppermute | solution.py:444
  25.6 2.9 %collective-permute-start.4 = (bf16[128,512]{1,0:T(8,128)(2,1)S(1)}, bf16[128,512]{1,0:T(8,128)(2,1)S(1)}, u32[]{:S(2)}, u32[]{:S(2)}) collective-permute-start(bf16[128,512]{1,0:T(8,128)(2,1)S(1)} %get-tuple-element.81), channel_id=1, source_target_pairs={{0,1},{1,0},{2,3},{3,2},{4,5},{5,4},{6,7},{7,6},{8,9},{9,8},{10,11... | collective-permute-start | bytes 393224 | tf_op jit(solution)/shard_map/ppermute | solution.py:444
  28.6 9.3 %collective-permute-start.11 = (bf16[128,768]{1,0:T(8,128)(2,1)S(1)}, bf16[128,768]{1,0:T(8,128)(2,1)S(1)}, u32[]{:S(2)}, u32[]{:S(2)}) collective-permute-start(bf16[128,768]{1,0:T(8,128)(2,1)S(1)} %get-tuple-element.94), channel_id=1, source_target_pairs={{0,2},{1,3},{2,0},{3,1},{4,6},{5,7},{6,4},{7,5},{8,10},{9,11},{10,... | collective-permute-start | bytes 589832 | tf_op jit(solution)/shard_map/ppermute | solution.py:444
  30.1 6.6 %collective-permute-start.12 = (bf16[128,256]{1,0:T(8,128)(2,1)S(1)}, bf16[128,256]{1,0:T(8,128)(2,1)S(1)}, u32[]{:S(2)}, u32[]{:S(2)}) collective-permute-start(bf16[128,256]{1,0:T(8,128)(2,1)S(1)} %get-tuple-element.95), channel_id=1, source_target_pairs={{0,24},{4,28},{8,16},{12,20},{16,8},{20,12},{24,0},{28,4},{1,25},{... | collective-permute-start | bytes 196616 | tf_op jit(solution)/shard_map/ppermute | solution.py:444
  31.9 6.0 %collective-permute-start.13 = (bf16[128,256]{1,0:T(8,128)(2,1)S(1)}, bf16[128,256]{1,0:T(8,128)(2,1)S(1)}, u32[]{:S(2)}, u32[]{:S(2)}) collective-permute-start(bf16[128,256]{1,0:T(8,128)(2,1)S(1)} %get-tuple-element.96), channel_id=1, source_target_pairs={{0,16},{4,20},{8,24},{12,28},{16,0},{20,4},{24,8},{28,12},{1,17},{... | collective-permute-start | bytes 196616 | tf_op jit(solution)/shard_map/ppermute | solution.py:444
  31.9 6.0 %collective-permute-start.14 = (bf16[128,256]{1,0:T(8,128)(2,1)S(1)}, bf16[128,256]{1,0:T(8,128)(2,1)S(1)}, u32[]{:S(2)}, u32[]{:S(2)}) collective-permute-start(bf16[128,256]{1,0:T(8,128)(2,1)S(1)} %get-tuple-element.97), channel_id=1, source_target_pairs={{0,8},{4,12},{8,0},{12,4},{16,24},{20,28},{24,16},{28,20},{1,9},{5... | collective-permute-start | bytes 196616 | tf_op jit(solution)/shard_map/ppermute | solution.py:444

commit v7 on v6

--- a/solution.py
+++ b/solution.py
@@ -51,19 +51,13 @@
     return sum(nt(masks, part) for part in split3(values))
 
 
-def decay_factors(d_ahead, d_behind, width):
+def decay_factors(d_ahead, d_behind, width, rest):
     length = d_ahead.shape[1]
     row, col = iotas(length, length)
-    upto = (col <= row).astype(F32)
-    since = (col >= row).astype(F32)
-    ahead = masked_sums(
-        jnp.concatenate([upto, 1.0 - upto], axis=0), spread_rows(d_ahead, width)
-    )
-    behind = masked_sums(
-        jnp.concatenate([since, 1.0 - since], axis=0), spread_rows(d_behind, width)
-    )
-    ahead, behind = jnp.exp(ahead), jnp.exp(behind)
-    return ahead[:length], ahead[length:], behind[:length], behind[length:]
+    masks = (col > row, col < row) if rest else (col <= row, col >= row)
+    return [
+        jnp.exp(masked_sums(mask.astype(F32), spread_rows(d, width))) for mask, d in zip(masks, (d_ahead, d_behind))
+    ]
 
 
 def radices(peers):
@@ -147,11 +141,10 @@
     da, db, gy, ca, cb, _ = held
     for copy in copies[:2]:
         copy.wait()
-    factors = decay_factors(da[...], db[...], width)
-    *sends, factors_out = outs
-    for k in range(4):
-        factors_out[k] = factors[k]
-    grow_a, _, grow_b, _ = factors
+    grow_a, grow_b = decay_factors(da[...], db[...], width, False)
+    *sends, grow_out = outs
+    grow_out[0] = grow_a
+    grow_out[1] = grow_b
     for copy in copies[2:]:
         copy.wait()
     gyf = gy[...].astype(F32)
@@ -160,19 +153,22 @@
     write_chunk(sends, me, last, up, down, (grow_a[gyf.shape[0] - 1 :], grow_b[0:1]))
 
 
-def state_kernel(me, last, *refs):
+def state_kernel(me, last, width, *refs):
     *refs, sems = refs
-    sources, factors, outs, held = refs[:4], refs[4], refs[5:-4], refs[-4:]
+    sources, da, db, outs, held = refs[:4], refs[4], refs[5], refs[6:-4], refs[-4:]
     copies = start_copies(sources, held, sems)
     ba, bb, features, w_in = held
+    *sends, x_out, left_out = outs
+    left_a, left_b = decay_factors(da[...], db[...], width, True)
+    left_out[0] = left_a
+    left_out[1] = left_b
     for copy in copies:
         copy.wait()
-    *sends, x_out = outs
     x = nn(features[...], w_in[...]).astype(BF16)
     x_out[...] = x
     xf = x.astype(F32)
-    up = nn(ba[...].T, (xf * factors[1]).astype(BF16))
-    down = nn(bb[...].T, (xf * factors[3]).astype(BF16))
+    up = nn(ba[...].T, (xf * left_a).astype(BF16))
+    down = nn(bb[...].T, (xf * left_b).astype(BF16))
     write_chunk(sends, me, last, up, down, ())
 
 
@@ -290,16 +286,16 @@
 def carry_kernel(index, steps, stride, direct, *refs):
     refs = list(refs)
     received, before = take_chunk(refs, steps[-1], len(steps) == 1)
-    turned, ba, bb, gx_local, factors = [refs.pop(0) for _ in range(5)]
+    turned, ba, bb, gx_local, left = [refs.pop(0) for _ in range(5)]
     gx_out, grad_out, *outs = refs
     seq = index()
     me = digit(seq, stride, steps[-1])
     gradient = entering(received, received, before, seq, stride * steps[-1], ba.shape[1], False)
     grad_x = gx_local[...]
-    for k, (b, left) in enumerate(((ba, factors[1]), (bb, factors[3]))):
+    for k, b in enumerate((ba, bb)):
         grad = gradient(1 - k).astype(BF16)
         grad_out[k] = grad
-        grad_x = grad_x + nn(b[...], grad).astype(BF16).astype(F32) * left
+        grad_x = grad_x + nn(b[...], grad).astype(BF16).astype(F32) * left[k]
     grad_x = grad_x.astype(BF16)
     gx_out[...] = grad_x
     if not direct:
@@ -328,7 +324,7 @@
     return (lax.div(cols, columns // heads) == rows).astype(BF16)
 
 
-def share_kernel(index, n_head, grad_x, grads, x, w_in, ba, bb, maps_local, decay_local, factors, *outs):
+def share_kernel(index, n_head, grad_x, grads, x, w_in, ba, bb, maps_local, decay_local, lefts, *outs):
     decay_out, maps_out, own_out, send_out = outs
     heads = decay_local.shape[0]
     n = ba.shape[1]
@@ -338,7 +334,7 @@
     group = head_groups(heads, columns)
     rows_out = w_in.shape[0] // n_head
     for k, (b, earlier) in enumerate(((ba, row < col), (bb, row > col))):
-        left, grad = factors[2 * k + 1], grads[k]
+        left, grad = lefts[k], grads[k]
         write = nn(b[...], grad).astype(BF16).astype(F32) * left * xf
         writes = nt(group, write.astype(BF16))
         part = slice(k * length, (k + 1) * length)
@@ -360,29 +356,36 @@
     refs = list(refs)
     received, before = take_chunk(refs, steps[-1], len(steps) == 1)
     decays, _ = take_chunk(refs, steps[-1], True)
-    grads, gy, ca, cb, maps_local, maps_b, decay_part, factors = [refs.pop(0) for _ in range(8)]
-    *gd_outs, own_out, send_out = refs
+    gy, maps_local, maps_b, grows = [refs.pop(0) for _ in range(4)]
+    states_out, own_out, send_out = refs
+    n = maps_b.shape[1] // 2
+    state = entering(received, decays, before, index(), peers, n, True)
+    gyf = gy[...].astype(F32)
+    for k in range(2):
+        low = state(k).astype(BF16)
+        states_out[k] = low
+        grad_c = maps_local[:, (2 * k + 1) * n : (2 * k + 2) * n] + nt((gyf * grows[k]).astype(BF16), low)
+        for at, value in ((2 * k, maps_b[:, k * n : (k + 1) * n]), (2 * k + 1, grad_c)):
+            own_out[:, at * n : (at + 1) * n] = value
+            send_out[:, at * n : (at + 1) * n] = value.astype(BF16)
+
+
+def decay_kernel(states, grads, gy, ca, cb, decay_part, grows, *refs):
+    gd_outs = refs[-2:]
     heads = decay_part.shape[0]
-    n = ca.shape[1]
     length, columns = gy.shape
-    state = entering(received, decays, before, index(), peers, n, True)
     gyf = gy[...].astype(F32)
     row, col = iotas(length, length)
     group = head_groups(heads, columns)
     frame = lax.broadcasted_iota(jnp.int32, (length, 1), 0)
     for k, (c, at_end, later) in enumerate(((ca, length - 1, row >= col), (cb, 0, row <= col))):
-        grow, entered = factors[2 * k], state(k)
-        low = entered.astype(BF16)
+        grow, low = grows[k], states[k]
         gain = grow[at_end : at_end + 1]
-        through = gain * jnp.sum(entered * grads[k].astype(F32), axis=0, keepdims=True)
+        through = gain * jnp.sum(low.astype(F32) * grads[k].astype(F32), axis=0, keepdims=True)
         read = gyf * (grow * nn(c[...], low)) + jnp.where(frame == at_end, through, 0.0)
         reads = nt(group, read.astype(BF16))
         gd = nn(reads, later.astype(F32), precision=HIGH)[:heads]
         gd_outs[k][...] = gd + decay_part[:, k * length : (k + 1) * length]
-        grad_c = maps_local[:, (2 * k + 1) * n : (2 * k + 2) * n] + nt((gyf * grow).astype(BF16), low)
-        for at, value in ((2 * k, maps_b[:, k * n : (k + 1) * n]), (2 * k + 1, grad_c)):
-            own_out[:, at * n : (at + 1) * n] = value
-            send_out[:, at * n : (at + 1) * n] = value.astype(BF16)
 
 
 def pair_kernel(index, stride, rows_out, blocks, count, *refs):
@@ -466,17 +469,18 @@
     steps = radices(peers)
     only = len(steps) == 1
     chunk_shapes = [half] * (steps[0] - 1) if only else [whole]
-    *gradients, factors, da, db, gy, ca, cb, skip = call(
+    pair = shape((2, length, columns), F32)
+    *gradients, grow, da, db, gy, ca, cb, skip = call(
         functools.partial(gradient_kernel, seq_index, only, columns // heads),
-        chunk_shapes + [shape((4, length, columns), F32)],
+        chunk_shapes + [pair],
         decay_ahead, decay_behind, grad_y, c_ahead, c_behind, skip_gain.reshape(1, heads),
         micros=1.35,
         held=6,
     )
-    *states, x, ba, bb, fs, wi = call(
-        functools.partial(state_kernel, seq_index, only),
-        ([state_half] * (steps[0] - 1) if only else [state_whole]) + [square],
-        b_ahead, b_behind, features, w_in, factors,
+    *states, x, left, ba, bb, fs, wi = call(
+        functools.partial(state_kernel, seq_index, only, columns // heads),
+        ([state_half] * (steps[0] - 1) if only else [state_whole]) + [square, pair],
+        b_ahead, b_behind, features, w_in, da, db,
         micros=1.65,
         held=4,
     )
@@ -521,7 +525,7 @@
     grad_x, grads, *sends = call(
         functools.partial(carry_kernel, seq_index, steps, stride, direct),
         [square, shape((2, n, columns), BF16)] + pieces,
-        *gradient_in, turned, ba, bb, gx_local, factors,
+        *gradient_in, turned, ba, bb, gx_local, left,
         micros=0.5,
     )
     def both(width):
@@ -530,40 +534,44 @@
     decay_part, maps_b, own, send = call(
         functools.partial(share_kernel, head_index, n_head),
         [shape((heads, 2 * length), F32), shape((length, 2 * n), F32)] + both(n_head // 2 * rows_out),
-        grad_x, grads, x, wi, ba, bb, maps_local, decay_local, factors,
+        grad_x, grads, x, wi, ba, bb, maps_local, decay_local, left,
         micros=1.0,
     )
     shares = [own, swap(send, "head", 1)]
-    gd_ahead, gd_behind, own, send = call(
+    entered, own, send = call(
         functools.partial(state_share_kernel, seq_index, steps, peers),
-        [shape((heads, length), F32)] * 2 + both(4 * n),
-        *state_in, grads, gy, ca, cb, maps_local, maps_b, decay_part, factors,
-        micros=1.4,
+        [shape((2, n, columns), BF16)] + both(4 * n),
+        *state_in, gy, maps_local, maps_b, grow,
+        micros=0.7,
     )
     shares += [own, swap(send, "head", 1)]
-    after = []
+    mask, blocks = 2, n_head // 2
+    while mask < n_head:
+        own, send = call(
+            functools.partial(pair_kernel, head_index, mask, rows_out, blocks, len(shares)),
+            both(blocks // 2 * rows_out + 4 * n),
+            *shares,
+            micros=0.0,
+        )
+        shares = [own, swap(send, "head", mask)]
+        mask, blocks = mask * 2, blocks // 2
     if direct:
         received = [swap(send, "seq", j) for j, send in enumerate(sends, start=1)]
         own_weight, *sends = call(
             functools.partial(fold_kernel, seq_index, steps),
             [shape((rows_w, columns), F32)] + [shape((rows_w, columns), BF16)] * 3,
-            turned, grad_x, *received, own,
+            turned, grad_x, *received, shares[0],
             micros=0.22,
         )
         weight_parts = far_first(sends, stride) + [own_weight]
-        after = [own_weight]
     else:
         weight_parts = [lax.all_to_all(sends[0].reshape(peers, rows_w, columns), "seq", 0, 0)]
-    mask, blocks = 2, n_head // 2
-    while mask < n_head:
-        own, send = call(
-            functools.partial(pair_kernel, head_index, mask, rows_out, blocks, len(shares)),
-            both(blocks // 2 * rows_out + 4 * n),
-            *shares, *after,
-            micros=0.25,
-        )
-        shares = [own, swap(send, "head", mask)]
-        mask, blocks = mask * 2, blocks // 2
+    gd_ahead, gd_behind = call(
+        decay_kernel,
+        [shape((heads, length), F32)] * 2,
+        entered, grads, gy, ca, cb, decay_part, grow, weight_parts[-1],
+        micros=1.0,
+    )
     grad_features, grad_w_in, *grad_maps = call(
         functools.partial(last_kernel, 1.0 / math.sqrt(length * peers)),
         [shape((length, rows_out), BF16), shape((rows_w, columns), F32)] + [shape((length, n), F32)] * 4,

time: 38.9 us -> 37.7 us (0.969)
  waiting for transfers between devices: 10.2 us -> 8.49 us
  starting transfers between devices: 19.7 us -> 20.1 us
    ppermute x15, waiting for transfers between devices: 10.2 us -> 8.49 us  [swap(): lax.ppermute(value, axis, [(i, i ^ mask) for i in range(lax.axis_size(axi...]
    pallas_call x11 -> x12, Pallas kernels: 8.06 us -> 8.19 us  [call(): pl.pallas_call(kernel, out_shape=outs, in_specs=specs, out_specs=[pl.Bloc...]
  transfers between devices with their start and end apart: 15 -> 15, of which waited for: 5 -> 7; matrix products, arithmetic and copies ran while one was open for 0% -> 0% of each run, Pallas kernels for 15% -> 16%
where the time goes in v7:
time: 37.7 us; the launch traced here: 37.5 us
  starting transfers between devices  20.1 us (53%)
  waiting for transfers between devices  8.49 us (23%)
  Pallas kernels  8.19 us (22%)
  between operations  0.75 us (2%)
    ppermute x15, starting transfers between devices, swap(): lax.ppermute(value, axis, [(i, i ^ mask) for i in range(lax.axis_size(axi...  20.1 us
    ppermute x15, waiting for transfers between devices, swap(): lax.ppermute(value, axis, [(i, i ^ mask) for i in range(lax.axis_size(axi...  8.49 us
    pallas_call x12, Pallas kernels, call(): pl.pallas_call(kernel, out_shape=outs, in_specs=specs, out_specs=[pl.Bloc...  8.19 us
  transfers between devices with their start and end apart: 15, of which 7 were waited for; matrix products, arithmetic and copies ran while one was open for 0% of the time, Pallas kernels for 16%

profile of v7, /device:TPU:0, one launch (start us, length us, event | category | flops | bytes accessed | tf_op | source)
XLA Modules:
  0.0 37.5 jit_solution(17102279126227023179)
XLA Ops:
  0.6 1.3 %shard_map.161 = (bf16[272,256]{1,0:T(8,128)(2,1)S(1)}, f32[2,128,256]{2,1,0:T(8,128)S(1)}, f32[4,128]{1,0:T(4,128)S(1)}, f32[4,128]{1,0:T(4,128)S(1)}, bf16[128...) custom-call(f32[4,128]{1,0:T(4,128)} %refs_0_.2, ...), custom_call_target="tpu_custom_call" | custom-call | flops 1552499968 | tf_op jit(solution)/shard_map/pallas_call | solution.py:435
  1.9 3.0 %collective-permute-start = (bf16[272,256]{1,0:T(8,128)(2,1)S(1)}, bf16[272,256]{1,0:T(8,128)(2,1)S(1)}, u32[]{:S(2)}, u32[]{:S(2)}) collective-permute-start(bf16[272,256]{1,0:T(8,128)(2,1)S(1)} %get-tuple-element.59.refs_0_.refs_2_), channel_id=1, source_target_pairs={{0,4},{4,0},{8,12},{12,8},{16,20},{20,16},{24,28},{28,24},{1,5},{5... | collective-permute-start | bytes 417800 | tf_op jit(solution)/shard_map/ppermute | solution.py:447
  4.9 1.7 %shard_map.163 = (bf16[256,256]{1,0:T(8,128)(2,1)S(1)}, bf16[128,256]{1,0:T(8,128)(2,1)S(1)}, f32[2,128,256]{2,1,0:T(8,128)S(1)}, bf16[128,128]{1,0:T(8,128)(2,1...) custom-call(bf16[128,128]{1,0:T(8,128)(2,1)} %refs_0_.3, ...), custom_call_target="tpu_custom_call" | custom-call | flops 1897500032 | tf_op jit(solution)/shard_map/pallas_call | solution.py:435
  6.7 2.3 %collective-permute-done.refs_1_.refs_3_ = bf16[272,256]{1,0:T(8,128)(2,1)S(1)} collective-permute-done((bf16[272,256]{1,0:T(8,128)(2,1)S(1)}, bf16[272,256]{1,0:T(8,128)(2,1)S(1)}, u32[]{:S(2)}, u32[]{:S(2)}) %collective-permute-start) | collective-permute-done | bytes 139296 | tf_op jit(solution)/shard_map/ppermute | solution.py:447
  9.1 3.6 %collective-permute-start.1 = (bf16[144,256]{1,0:T(8,128)(2,1)S(1)}, bf16[144,256]{1,0:T(8,128)(2,1)S(1)}, u32[]{:S(2)}, u32[]{:S(2)}) collective-permute-start(bf16[144,256]{1,0:T(8,128)(2,1)S(1)} %get-tuple-element.60), channel_id=1, source_target_pairs={{0,24},{4,28},{8,16},{12,20},{16,8},{20,12},{24,0},{28,4},{1,25},{... | collective-permute-start | bytes 221192 | tf_op jit(solution)/shard_map/ppermute | solution.py:447
  12.7 0.9 %collective-permute-start.3 = (bf16[144,256]{1,0:T(8,128)(2,1)S(1)}, bf16[144,256]{1,0:T(8,128)(2,1)S(1)}, u32[]{:S(2)}, u32[]{:S(2)}) collective-permute-start(bf16[144,256]{1,0:T(8,128)(2,1)S(1)} %get-tuple-element.62), channel_id=1, source_target_pairs={{0,8},{4,12},{8,0},{12,4},{16,24},{20,28},{24,16},{28,20},{1,9},{5... | collective-permute-start | bytes 221192 | tf_op jit(solution)/shard_map/ppermute | solution.py:447
  13.6 0.9 %shard_map.164 = (f32[128,256]{1,0:T(8,128)S(1)}, f32[128,512]{1,0:T(8,128)S(1)}, f32[4,256]{1,0:T(4,128)S(1)}, bf16[1024,128]{1,0:T(8,128)(2,1)S(1)}) custom-call(f32[1,4]{1,0:T(1,128)S(1)} %get-tuple-element.64.skip, bf16[128,256]{1,0:T(8,128)(2,1)S(1)} %get-tuple-element.67.x, bf16[128,256]{1,0:T(8,128)(2,1)S(1)} %get-tuple-element.68.gy.refs_7_, ...), custom_call_target="tpu_custom_call" | custom-call | flops 1035000000 | tf_op jit(solution)/shard_map/pallas_call | solution.py:435
  14.6 3.6 %collective-permute-start.6 = (bf16[128,256]{1,0:T(8,128)(2,1)S(1)}, bf16[128,256]{1,0:T(8,128)(2,1)S(1)}, u32[]{:S(2)}, u32[]{:S(2)}) collective-permute-start(bf16[128,256]{1,0:T(8,128)(2,1)S(1)} %get-tuple-element.85), channel_id=1, source_target_pairs={{0,24},{4,28},{8,16},{12,20},{16,8},{20,12},{24,0},{28,4},{1,25},{... | collective-permute-start | bytes 196616 | tf_op jit(solution)/shard_map/ppermute | solution.py:447
  18.2 0.9 %collective-permute-start.8 = (bf16[128,256]{1,0:T(8,128)(2,1)S(1)}, bf16[128,256]{1,0:T(8,128)(2,1)S(1)}, u32[]{:S(2)}, u32[]{:S(2)}) collective-permute-start(bf16[128,256]{1,0:T(8,128)(2,1)S(1)} %get-tuple-element.87), channel_id=1, source_target_pairs={{0,8},{4,12},{8,0},{12,4},{16,24},{20,28},{24,16},{28,20},{1,9},{5... | collective-permute-start | bytes 196616 | tf_op jit(solution)/shard_map/ppermute | solution.py:447
  19.1 2.2 %collective-permute-done.2.refs_1_.refs_5_ = bf16[144,256]{1,0:T(8,128)(2,1)S(1)} collective-permute-done((bf16[144,256]{1,0:T(8,128)(2,1)S(1)}, bf16[144,256]{1,0:T(8,128)(2,1)S(1)}, u32[]{:S(2)}, u32[]{:S(2)}) %collective-permute-start.2) | collective-permute-done | bytes 73760 | tf_op jit(solution)/shard_map/ppermute | solution.py:447
  21.3 0.5 %shard_map.165 = (bf16[128,256]{1,0:T(8,128)(2,1)S(1)}, bf16[2,128,256]{2,1,0:T(8,128)(2,1)S(1)}, bf16[4,128,256]{2,1,0:T(8,128)(2,1)S(1)}) custom-call(bf16[144,256]{1,0:T(8,128)(2,1)S(1)} %collective-permute-done.1.refs_0_.refs_4_, bf16[144,256]{1,0:T(8,128)(2,1)S(1)} %collective-permute-done.2.refs_1_.refs_5_, ...), custom_call_target="tpu_custom_call" | custom-call | flops 575000000 | tf_op jit(solution)/shard_map/pallas_call | solution.py:435
  21.7 1.3 %collective-permute-start.11 = (bf16[4,128,256]{2,1,0:T(8,128)(2,1)S(1)}, bf16[4,128,256]{2,1,0:T(8,128)(2,1)S(1)}, u32[]{:S(2)}, u32[]{:S(2)}) collective-permute-start(bf16[4,128,256]{2,1,0:T(8,128)(2,1)S(1)} %get-tuple-element.95), channel_id=1, source_target_pairs={{0,4},{4,0},{8,12},{12,8},{16,20},{20,16},{24,28},{28,24},{1,5},{5... | collective-permute-start | bytes 786440 | tf_op jit(solution)/shard_map/ppermute | solution.py:447
  23.1 1.0 %shard_map.166 = (f32[4,256]{1,0:T(4,128)S(1)}, f32[128,256]{1,0:T(8,128)S(1)}, f32[128,512]{1,0:T(8,128)S(1)}, bf16[128,512]{1,0:T(8,128)(2,1)S(1)}) custom-call(bf16[128,256]{1,0:T(8,128)(2,1)S(1)} %get-tuple-element.77.grad_x, bf16[2,128,256]{2,1,0:T(8,128)(2,1)S(1)} %get-tuple-element.78.grads, bf16[128,256]{1,0:T(8,128)(2,1)S(1)} %get-tuple-element.67.x, ...), custom_call_target="tpu_custom_call" | custom-call | flops 1150000000 | tf_op jit(solution)/shard_map/pallas_call | solution.py:435
  24.1 0.3 shard_map.168
  24.4 0.5 %collective-permute-start.4 = (bf16[128,512]{1,0:T(8,128)(2,1)S(1)}, bf16[128,512]{1,0:T(8,128)(2,1)S(1)}, u32[]{:S(2)}, u32[]{:S(2)}) collective-permute-start(bf16[128,512]{1,0:T(8,128)(2,1)S(1)} %get-tuple-element.83), channel_id=1, source_target_pairs={{0,1},{1,0},{2,3},{3,2},{4,5},{5,4},{6,7},{7,6},{8,9},{9,8},{10,11... | collective-permute-start | bytes 393224 | tf_op jit(solution)/shard_map/ppermute | solution.py:447
  24.9 0.8 %collective-permute-done.9.refs_3_ = bf16[128,512]{1,0:T(8,128)(2,1)S(1)} collective-permute-done((bf16[128,512]{1,0:T(8,128)(2,1)S(1)}, bf16[128,512]{1,0:T(8,128)(2,1)S(1)}, u32[]{:S(2)}, u32[]{:S(2)}) %collective-permute-start.9) | collective-permute-done | bytes 131104 | tf_op jit(solution)/shard_map/ppermute | solution.py:447
  26.0 1.7 %collective-permute-start.10 = (bf16[128,768]{1,0:T(8,128)(2,1)S(1)}, bf16[128,768]{1,0:T(8,128)(2,1)S(1)}, u32[]{:S(2)}, u32[]{:S(2)}) collective-permute-start(bf16[128,768]{1,0:T(8,128)(2,1)S(1)} %get-tuple-element.94), channel_id=1, source_target_pairs={{0,2},{1,3},{2,0},{3,1},{4,6},{5,7},{6,4},{7,5},{8,10},{9,11},{10,... | collective-permute-start | bytes 589832 | tf_op jit(solution)/shard_map/ppermute | solution.py:447
  27.8 0.4 %collective-permute-done.11.refs_0_ = bf16[4,128,256]{2,1,0:T(8,128)(2,1)S(1)} collective-permute-done((bf16[4,128,256]{2,1,0:T(8,128)(2,1)S(1)}, bf16[4,128,256]{2,1,0:T(8,128)(2,1)S(1)}, u32[]{:S(2)}, u32[]{:S(2)}) %collective-permute-start.11) | collective-permute-done | bytes 262176 | tf_op jit(solution)/shard_map/ppermute | solution.py:447
  28.4 2.0 %collective-permute-start.12 = (bf16[128,256]{1,0:T(8,128)(2,1)S(1)}, bf16[128,256]{1,0:T(8,128)(2,1)S(1)}, u32[]{:S(2)}, u32[]{:S(2)}) collective-permute-start(bf16[128,256]{1,0:T(8,128)(2,1)S(1)} %get-tuple-element.96), channel_id=1, source_target_pairs={{0,24},{4,28},{8,16},{12,20},{16,8},{20,12},{24,0},{28,4},{1,25},{... | collective-permute-start | bytes 196616 | tf_op jit(solution)/shard_map/ppermute | solution.py:447
  30.4 2.4 %collective-permute-start.14 = (bf16[128,256]{1,0:T(8,128)(2,1)S(1)}, bf16[128,256]{1,0:T(8,128)(2,1)S(1)}, u32[]{:S(2)}, u32[]{:S(2)}) collective-permute-start(bf16[128,256]{1,0:T(8,128)(2,1)S(1)} %get-tuple-element.98), channel_id=1, source_target_pairs={{0,8},{4,12},{8,0},{12,4},{16,24},{20,28},{24,16},{28,20},{1,9},{5... | collective-permute-start | bytes 196616 | tf_op jit(solution)/shard_map/ppermute | solution.py:447
  32.9 1.3 %shard_map.172 = (f32[4,128]{1,0:T(4,128)}, f32[4,128]{1,0:T(4,128)}) custom-call(bf16[2,128,256]{2,1,0:T(8,128)(2,1)S(1)} %get-tuple-element.106.states, bf16[2,128,256]{2,1,0:T(8,128)(2,1)S(1)} %get-tuple-element.78.grads, bf16[128,256]{1,0:T(8,128)(2,1)S(1)} %get-tuple-element.68.gy.refs_7_, bf16[128,128]{1,0:T(8,128)(2,1)S(1)} %get-tuple-element.71.ca, ...), custom_call_target="tpu_custom_call" | custom-call | flops 1150000000 | tf_op jit(solution)/shard_map/pallas_call | solution.py:435
  34.2 0.5 %collective-permute-done.12.refs_0_ = bf16[128,256]{1,0:T(8,128)(2,1)S(1)} collective-permute-done((bf16[128,256]{1,0:T(8,128)(2,1)S(1)}, bf16[128,256]{1,0:T(8,128)(2,1)S(1)}, u32[]{:S(2)}, u32[]{:S(2)}) %collective-permute-start.12) | collective-permute-done | bytes 65568 | tf_op jit(solution)/shard_map/ppermute | solution.py:447
  34.7 2.0 %collective-permute-done.13.refs_1_ = bf16[128,256]{1,0:T(8,128)(2,1)S(1)} collective-permute-done((bf16[128,256]{1,0:T(8,128)(2,1)S(1)}, bf16[128,256]{1,0:T(8,128)(2,1)S(1)}, u32[]{:S(2)}, u32[]{:S(2)}) %collective-permute-start.13) | collective-permute-done | bytes 65568 | tf_op jit(solution)/shard_map/ppermute | solution.py:447
  36.7 0.8 %shard_map.171 = (bf16[128,256]{1,0:T(8,128)(2,1)}, f32[128,256]{1,0:T(8,128)}, f32[128,128]{1,0:T(8,128)}, f32[128,128]{1,0:T(8,128)}, f32[128,128]{1,0:T(8,128)}, /*index=5*/f32[128,128]{1,0:T(8,128)}) custom-call(f32[128,768]{1,0:T(8,128)S(1)} %get-tuple-element.93.refs_1_.own, bf16[128,768]{1,0:T(8,128)(2,1)S(1)} %collective-permute-done.10.other, ...), custom_call_target="tpu_custom_call" | custom-call | flops 920000000 | tf_op jit(solution)/shard_map/pallas_call | solution.py:435
  (18 shorter events, 0.9 us)
Async XLA Ops:
  1.9 7.1 %collective-permute-start = (bf16[272,256]{1,0:T(8,128)(2,1)S(1)}, bf16[272,256]{1,0:T(8,128)(2,1)S(1)}, u32[]{:S(2)}, u32[]{:S(2)}) collective-permute-start(bf16[272,256]{1,0:T(8,128)(2,1)S(1)} %get-tuple-element.59.refs_0_.refs_2_), channel_id=1, source_target_pairs={{0,4},{4,0},{8,12},{12,8},{16,20},{20,16},{24,28},{28,24},{1,5},{5... | collective-permute-start | bytes 417800 | tf_op jit(solution)/shard_map/ppermute | solution.py:447
  6.6 7.9 %collective-permute-start.5 = (bf16[256,256]{1,0:T(8,128)(2,1)S(1)}, bf16[256,256]{1,0:T(8,128)(2,1)S(1)}, u32[]{:S(2)}, u32[]{:S(2)}) collective-permute-start(bf16[256,256]{1,0:T(8,128)(2,1)S(1)} %get-tuple-element.84.refs_0_), channel_id=1, source_target_pairs={{0,4},{4,0},{8,12},{12,8},{16,20},{20,16},{24,28},{28,24},{1,5},{5... | collective-permute-start | bytes 393224 | tf_op jit(solution)/shard_map/ppermute | solution.py:447
  9.1 9.0 %collective-permute-start.1 = (bf16[144,256]{1,0:T(8,128)(2,1)S(1)}, bf16[144,256]{1,0:T(8,128)(2,1)S(1)}, u32[]{:S(2)}, u32[]{:S(2)}) collective-permute-start(bf16[144,256]{1,0:T(8,128)(2,1)S(1)} %get-tuple-element.60), channel_id=1, source_target_pairs={{0,24},{4,28},{8,16},{12,20},{16,8},{20,12},{24,0},{28,4},{1,25},{... | collective-permute-start | bytes 221192 | tf_op jit(solution)/shard_map/ppermute | solution.py:447
  12.7 8.6 %collective-permute-start.2 = (bf16[144,256]{1,0:T(8,128)(2,1)S(1)}, bf16[144,256]{1,0:T(8,128)(2,1)S(1)}, u32[]{:S(2)}, u32[]{:S(2)}) collective-permute-start(bf16[144,256]{1,0:T(8,128)(2,1)S(1)} %get-tuple-element.61), channel_id=1, source_target_pairs={{0,16},{4,20},{8,24},{12,28},{16,0},{20,4},{24,8},{28,12},{1,17},{... | collective-permute-start | bytes 221192 | tf_op jit(solution)/shard_map/ppermute | solution.py:447
  12.7 8.6 %collective-permute-start.3 = (bf16[144,256]{1,0:T(8,128)(2,1)S(1)}, bf16[144,256]{1,0:T(8,128)(2,1)S(1)}, u32[]{:S(2)}, u32[]{:S(2)}) collective-permute-start(bf16[144,256]{1,0:T(8,128)(2,1)S(1)} %get-tuple-element.62), channel_id=1, source_target_pairs={{0,8},{4,12},{8,0},{12,4},{16,24},{20,28},{24,16},{28,20},{1,9},{5... | collective-permute-start | bytes 221192 | tf_op jit(solution)/shard_map/ppermute | solution.py:447
  14.6 9.4 %collective-permute-start.6 = (bf16[128,256]{1,0:T(8,128)(2,1)S(1)}, bf16[128,256]{1,0:T(8,128)(2,1)S(1)}, u32[]{:S(2)}, u32[]{:S(2)}) collective-permute-start(bf16[128,256]{1,0:T(8,128)(2,1)S(1)} %get-tuple-element.85), channel_id=1, source_target_pairs={{0,24},{4,28},{8,16},{12,20},{16,8},{20,12},{24,0},{28,4},{1,25},{... | collective-permute-start | bytes 196616 | tf_op jit(solution)/shard_map/ppermute | solution.py:447
  18.2 5.9 %collective-permute-start.7 = (bf16[128,256]{1,0:T(8,128)(2,1)S(1)}, bf16[128,256]{1,0:T(8,128)(2,1)S(1)}, u32[]{:S(2)}, u32[]{:S(2)}) collective-permute-start(bf16[128,256]{1,0:T(8,128)(2,1)S(1)} %get-tuple-element.86), channel_id=1, source_target_pairs={{0,16},{4,20},{8,24},{12,28},{16,0},{20,4},{24,8},{28,12},{1,17},{... | collective-permute-start | bytes 196616 | tf_op jit(solution)/shard_map/ppermute | solution.py:447
  18.2 5.9 %collective-permute-start.8 = (bf16[128,256]{1,0:T(8,128)(2,1)S(1)}, bf16[128,256]{1,0:T(8,128)(2,1)S(1)}, u32[]{:S(2)}, u32[]{:S(2)}) collective-permute-start(bf16[128,256]{1,0:T(8,128)(2,1)S(1)} %get-tuple-element.87), channel_id=1, source_target_pairs={{0,8},{4,12},{8,0},{12,4},{16,24},{20,28},{24,16},{28,20},{1,9},{5... | collective-permute-start | bytes 196616 | tf_op jit(solution)/shard_map/ppermute | solution.py:447
  21.7 6.4 %collective-permute-start.11 = (bf16[4,128,256]{2,1,0:T(8,128)(2,1)S(1)}, bf16[4,128,256]{2,1,0:T(8,128)(2,1)S(1)}, u32[]{:S(2)}, u32[]{:S(2)}) collective-permute-start(bf16[4,128,256]{2,1,0:T(8,128)(2,1)S(1)} %get-tuple-element.95), channel_id=1, source_target_pairs={{0,4},{4,0},{8,12},{12,8},{16,20},{20,16},{24,28},{28,24},{1,5},{5... | collective-permute-start | bytes 786440 | tf_op jit(solution)/shard_map/ppermute | solution.py:447
  24.4 1.4 %collective-permute-start.9 = (bf16[128,512]{1,0:T(8,128)(2,1)S(1)}, bf16[128,512]{1,0:T(8,128)(2,1)S(1)}, u32[]{:S(2)}, u32[]{:S(2)}) collective-permute-start(bf16[128,512]{1,0:T(8,128)(2,1)S(1)} %get-tuple-element.92), channel_id=1, source_target_pairs={{0,1},{1,0},{2,3},{3,2},{4,5},{5,4},{6,7},{7,6},{8,9},{9,8},{10,11... | collective-permute-start | bytes 393224 | tf_op jit(solution)/shard_map/ppermute | solution.py:447
  24.4 1.5 %collective-permute-start.4 = (bf16[128,512]{1,0:T(8,128)(2,1)S(1)}, bf16[128,512]{1,0:T(8,128)(2,1)S(1)}, u32[]{:S(2)}, u32[]{:S(2)}) collective-permute-start(bf16[128,512]{1,0:T(8,128)(2,1)S(1)} %get-tuple-element.83), channel_id=1, source_target_pairs={{0,1},{1,0},{2,3},{3,2},{4,5},{5,4},{6,7},{7,6},{8,9},{9,8},{10,11... | collective-permute-start | bytes 393224 | tf_op jit(solution)/shard_map/ppermute | solution.py:447
  26.0 10.7 %collective-permute-start.10 = (bf16[128,768]{1,0:T(8,128)(2,1)S(1)}, bf16[128,768]{1,0:T(8,128)(2,1)S(1)}, u32[]{:S(2)}, u32[]{:S(2)}) collective-permute-start(bf16[128,768]{1,0:T(8,128)(2,1)S(1)} %get-tuple-element.94), channel_id=1, source_target_pairs={{0,2},{1,3},{2,0},{3,1},{4,6},{5,7},{6,4},{7,5},{8,10},{9,11},{10,... | collective-permute-start | bytes 589832 | tf_op jit(solution)/shard_map/ppermute | solution.py:447
  28.4 6.3 %collective-permute-start.12 = (bf16[128,256]{1,0:T(8,128)(2,1)S(1)}, bf16[128,256]{1,0:T(8,128)(2,1)S(1)}, u32[]{:S(2)}, u32[]{:S(2)}) collective-permute-start(bf16[128,256]{1,0:T(8,128)(2,1)S(1)} %get-tuple-element.96), channel_id=1, source_target_pairs={{0,24},{4,28},{8,16},{12,20},{16,8},{20,12},{24,0},{28,4},{1,25},{... | collective-permute-start | bytes 196616 | tf_op jit(solution)/shard_map/ppermute | solution.py:447
  30.4 6.3 %collective-permute-start.13 = (bf16[128,256]{1,0:T(8,128)(2,1)S(1)}, bf16[128,256]{1,0:T(8,128)(2,1)S(1)}, u32[]{:S(2)}, u32[]{:S(2)}) collective-permute-start(bf16[128,256]{1,0:T(8,128)(2,1)S(1)} %get-tuple-element.97), channel_id=1, source_target_pairs={{0,16},{4,20},{8,24},{12,28},{16,0},{20,4},{24,8},{28,12},{1,17},{... | collective-permute-start | bytes 196616 | tf_op jit(solution)/shard_map/ppermute | solution.py:447
  30.4 6.3 %collective-permute-start.14 = (bf16[128,256]{1,0:T(8,128)(2,1)S(1)}, bf16[128,256]{1,0:T(8,128)(2,1)S(1)}, u32[]{:S(2)}, u32[]{:S(2)}) collective-permute-start(bf16[128,256]{1,0:T(8,128)(2,1)S(1)} %get-tuple-element.98), channel_id=1, source_target_pairs={{0,8},{4,12},{8,0},{12,4},{16,24},{20,28},{24,16},{28,20},{1,9},{5... | collective-permute-start | bytes 196616 | tf_op jit(solution)/shard_map/ppermute | solution.py:447

commit v8 on v7

--- a/solution.py
+++ b/solution.py
@@ -13,6 +13,7 @@
 HIGH = lax.Precision.HIGHEST
 GAIN_ROWS = 16
 FLOPS_PER_MICRO = 1.15e9
+STATES_FAR = False
 VMEM_LIMIT = 48 * 1024 * 1024
 
 
@@ -155,10 +156,11 @@
 
 def state_kernel(me, last, width, *refs):
     *refs, sems = refs
-    sources, da, db, outs, held = refs[:4], refs[4], refs[5], refs[6:-4], refs[-4:]
+    sources, rest, held = refs[:4], refs[4:-4], refs[-4:]
     copies = start_copies(sources, held, sems)
     ba, bb, features, w_in = held
-    *sends, x_out, left_out = outs
+    skip, gy, ca, cb, da, db, *outs = rest
+    *sends, x_out, left_out, gx_out, maps_out, decay_out, turned_out = outs
     left_a, left_b = decay_factors(da[...], db[...], width, True)
     left_out[0] = left_a
     left_out[1] = left_b
@@ -170,6 +172,7 @@
     up = nn(ba[...].T, (xf * left_a).astype(BF16))
     down = nn(bb[...].T, (xf * left_b).astype(BF16))
     write_chunk(sends, me, last, up, down, ())
+    in_block(skip, x, gy, features, ba, ca, bb, cb, da, db, gx_out, maps_out, decay_out, turned_out)
 
 
 def step_kernel(index, stride, radix, first, next_last, next_radix, states, *refs):
@@ -210,9 +213,7 @@
     write_chunk(outs, lambda: digit(seq, stride * radix, next_radix), next_last, *totals, new)
 
 
-def local_kernel(
-    skip, x, gy, features, ba, ca, bb, cb, da, db, gx_out, maps_out, decay_out, turned_out
-):
+def in_block(skip, x, gy, features, ba, ca, bb, cb, da, db, gx_out, maps_out, decay_out, turned_out):
     heads, length = da.shape
     width = x.shape[1] // heads
     n = ba.shape[1]
@@ -278,14 +279,14 @@
     return enter
 
 
-def take_chunk(refs, radix, first):
-    received = [refs.pop(0) for _ in range(radix - 1)][::-1]
-    return received, None if first else refs.pop(0)
+def take_chunk(refs, radix, first, far_first):
+    received = [refs.pop(0) for _ in range(radix - 1)]
+    return received[::-1] if far_first else received, None if first else refs.pop(0)
 
 
 def carry_kernel(index, steps, stride, direct, *refs):
     refs = list(refs)
-    received, before = take_chunk(refs, steps[-1], len(steps) == 1)
+    received, before = take_chunk(refs, steps[-1], len(steps) == 1, True)
     turned, ba, bb, gx_local, left = [refs.pop(0) for _ in range(5)]
     gx_out, grad_out, *outs = refs
     seq = index()
@@ -354,8 +355,8 @@
 
 def state_share_kernel(index, steps, peers, *refs):
     refs = list(refs)
-    received, before = take_chunk(refs, steps[-1], len(steps) == 1)
-    decays, _ = take_chunk(refs, steps[-1], True)
+    received, before = take_chunk(refs, steps[-1], len(steps) == 1, STATES_FAR)
+    decays, _ = take_chunk(refs, steps[-1], True, True)
     gy, maps_local, maps_b, grows = [refs.pop(0) for _ in range(4)]
     states_out, own_out, send_out = refs
     n = maps_b.shape[1] // 2
@@ -447,9 +448,9 @@
     return lax.ppermute(value, axis, [(i, i ^ mask) for i in range(lax.axis_size(axis))])
 
 
-def far_first(sends, stride):
-    jobs = list(enumerate(sends, start=1))
-    return [swap(send, "seq", j * stride) for j, send in reversed(jobs)]
+def exchange(sends, stride, far_first):
+    arrived = [swap(send, "seq", j * stride) for j, send in enumerate(sends, start=1)]
+    return arrived[::-1] if far_first else arrived
 
 
 def local(features, w_in, b_ahead, c_ahead, b_behind, c_behind, decay_ahead, decay_behind, skip_gain, grad_y):
@@ -477,25 +478,21 @@
         micros=1.35,
         held=6,
     )
-    *states, x, left, ba, bb, fs, wi = call(
+    *states, x, left, gx_local, maps_local, decay_local, turned, ba, bb, _, wi = call(
         functools.partial(state_kernel, seq_index, only, columns // heads),
-        ([state_half] * (steps[0] - 1) if only else [state_whole]) + [square, pair],
-        b_ahead, b_behind, features, w_in, da, db,
-        micros=1.65,
-        held=4,
-    )
-    maps = (ba, ca, bb, cb)
-    gx_local, maps_local, decay_local, turned = call(
-        local_kernel,
-        [
+        ([state_half] * (steps[0] - 1) if only else [state_whole])
+        + [square, pair]
+        + [
             shape((length, columns), F32),
             shape((length, 4 * n), F32),
             shape((heads, 2 * length), F32),
             shape((depth, length), BF16),
         ],
-        skip, x, gy, fs, *maps, da, db,
-        micros=0.9,
-    )
+        b_ahead, b_behind, features, w_in, skip, gy, ca, cb, da, db,
+        micros=2.5,
+        held=4,
+    )
+
     def merges(chunk, decays):
         stride, before, seen = 1, None, []
         whole_shape, half_shape = (state_whole, state_half) if decays else (whole, half)
@@ -513,11 +510,11 @@
                 micros=0.15,
             )
             stride *= radix
-        return far_first(chunk, stride), [] if only else [before], seen
+        return exchange(chunk, stride, not decays or STATES_FAR), [] if only else [before], seen
 
     stride = peers // steps[-1]
     gradients, gradient_before, seen = merges(gradients, None)
-    states, state_before, _ = merges(states, seen) if not only else (far_first(states, stride), [], [])
+    states, state_before, _ = merges(states, seen) if not only else (exchange(states, stride, STATES_FAR), [], [])
     gradient_in, state_in = gradients + gradient_before, states + state_before + gradients
     rows_out, rows_w = depth // n_head, depth // peers
     direct = len(steps) == 2 and rows_w % 16 == 0
@@ -542,7 +539,7 @@
         functools.partial(state_share_kernel, seq_index, steps, peers),
         [shape((2, n, columns), BF16)] + both(4 * n),
         *state_in, gy, maps_local, maps_b, grow,
-        micros=0.7,
+        micros=0.2,
     )
     shares += [own, swap(send, "head", 1)]
     mask, blocks = 2, n_head // 2
@@ -563,7 +560,7 @@
             turned, grad_x, *received, shares[0],
             micros=0.22,
         )
-        weight_parts = far_first(sends, stride) + [own_weight]
+        weight_parts = exchange(sends, stride, True) + [own_weight]
     else:
         weight_parts = [lax.all_to_all(sends[0].reshape(peers, rows_w, columns), "seq", 0, 0)]
     gd_ahead, gd_behind = call(

time: 37.7 us -> 37.1 us (0.984)
  waiting for transfers between devices: 8.49 us -> 6.14 us
  starting transfers between devices: 20.1 us -> 21.8 us
    ppermute x15, waiting for transfers between devices: 8.49 us -> 6.14 us  [swap(): lax.ppermute(value, axis, [(i, i ^ mask) for i in range(lax.axis_size(axi...]
    ppermute x15, starting transfers between devices: 20.1 us -> 21.8 us  [swap(): lax.ppermute(value, axis, [(i, i ^ mask) for i in range(lax.axis_size(axi...]
    pallas_call x12 -> x11, Pallas kernels: 8.19 us -> 8.21 us  [call(): pl.pallas_call(kernel, out_shape=outs, in_specs=specs, out_specs=[pl.Bloc...]
  transfers between devices with their start and end apart: 15 -> 15, of which waited for: 7 -> 5; matrix products, arithmetic and copies ran while one was open for 0% -> 0% of each run, Pallas kernels for 16% -> 17%
where the time goes in v8:
time: 37.1 us; the launch traced here: 36.9 us
  starting transfers between devices  21.8 us (59%)
  Pallas kernels  8.21 us (22%)
  waiting for transfers between devices  6.14 us (17%)
  between operations  0.74 us (2%)
    ppermute x15, starting transfers between devices, swap(): lax.ppermute(value, axis, [(i, i ^ mask) for i in range(lax.axis_size(axi...  21.8 us
    pallas_call x11, Pallas kernels, call(): pl.pallas_call(kernel, out_shape=outs, in_specs=specs, out_specs=[pl.Bloc...  8.21 us
    ppermute x15, waiting for transfers between devices, swap(): lax.ppermute(value, axis, [(i, i ^ mask) for i in range(lax.axis_size(axi...  6.14 us
  transfers between devices with their start and end apart: 15, of which 5 were waited for; matrix products, arithmetic and copies ran while one was open for 0% of the time, Pallas kernels for 17%

profile of v8, /device:TPU:0, one launch (start us, length us, event | category | flops | bytes accessed | tf_op | source)
XLA Modules:
  0.0 36.9 jit_solution(11545734827625715979)
XLA Ops:
  0.6 1.3 %shard_map.161 = (bf16[272,256]{1,0:T(8,128)(2,1)S(1)}, f32[2,128,256]{2,1,0:T(8,128)S(1)}, f32[4,128]{1,0:T(4,128)S(1)}, f32[4,128]{1,0:T(4,128)S(1)}, bf16[128...) custom-call(f32[4,128]{1,0:T(4,128)} %refs_0_.2, ...), custom_call_target="tpu_custom_call" | custom-call | flops 1552499968 | tf_op jit(solution)/shard_map/pallas_call | solution.py:436
  1.9 3.0 %collective-permute-start = (bf16[272,256]{1,0:T(8,128)(2,1)S(1)}, bf16[272,256]{1,0:T(8,128)(2,1)S(1)}, u32[]{:S(2)}, u32[]{:S(2)}) collective-permute-start(bf16[272,256]{1,0:T(8,128)(2,1)S(1)} %get-tuple-element.58.refs_0_.refs_2_), channel_id=1, source_target_pairs={{0,4},{4,0},{8,12},{12,8},{16,20},{20,16},{24,28},{28,24},{1,5},{5... | collective-permute-start | bytes 417800 | tf_op jit(solution)/shard_map/ppermute | solution.py:448
  4.9 2.6 %shard_map.163 = (bf16[256,256]{1,0:T(8,128)(2,1)S(1)}, bf16[128,256]{1,0:T(8,128)(2,1)S(1)}, f32[2,128,256]{2,1,0:T(8,128)S(1)}, f32[128,256]{1,0:T(8,128)S(1)}...) custom-call(bf16[128,128]{1,0:T(8,128)(2,1)} %refs_0_.3, ...), custom_call_target="tpu_custom_call" | custom-call | flops 2875000064 | tf_op jit(solution)/shard_map/pallas_call | solution.py:436
  7.6 1.0 %collective-permute-done.refs_1_.refs_3_ = bf16[272,256]{1,0:T(8,128)(2,1)S(1)} collective-permute-done((bf16[272,256]{1,0:T(8,128)(2,1)S(1)}, bf16[272,256]{1,0:T(8,128)(2,1)S(1)}, u32[]{:S(2)}, u32[]{:S(2)}) %collective-permute-start) | collective-permute-done | bytes 139296 | tf_op jit(solution)/shard_map/ppermute | solution.py:448
  8.6 0.1 shard_map.162
  8.7 3.9 %collective-permute-start.1 = (bf16[144,256]{1,0:T(8,128)(2,1)S(1)}, bf16[144,256]{1,0:T(8,128)(2,1)S(1)}, u32[]{:S(2)}, u32[]{:S(2)}) collective-permute-start(bf16[144,256]{1,0:T(8,128)(2,1)S(1)} %get-tuple-element.59), channel_id=1, source_target_pairs={{0,24},{4,28},{8,16},{12,20},{16,8},{20,12},{24,0},{28,4},{1,25},{... | collective-permute-start | bytes 221192 | tf_op jit(solution)/shard_map/ppermute | solution.py:448
  12.6 0.6 %collective-permute-start.3 = (bf16[144,256]{1,0:T(8,128)(2,1)S(1)}, bf16[144,256]{1,0:T(8,128)(2,1)S(1)}, u32[]{:S(2)}, u32[]{:S(2)}) collective-permute-start(bf16[144,256]{1,0:T(8,128)(2,1)S(1)} %get-tuple-element.61), channel_id=1, source_target_pairs={{0,8},{4,12},{8,0},{12,4},{16,24},{20,28},{24,16},{28,20},{1,9},{5... | collective-permute-start | bytes 221192 | tf_op jit(solution)/shard_map/ppermute | solution.py:448
  13.4 1.5 %collective-permute-start.6 = (bf16[128,256]{1,0:T(8,128)(2,1)S(1)}, bf16[128,256]{1,0:T(8,128)(2,1)S(1)}, u32[]{:S(2)}, u32[]{:S(2)}) collective-permute-start(bf16[128,256]{1,0:T(8,128)(2,1)S(1)} %get-tuple-element.83), channel_id=1, source_target_pairs={{0,8},{4,12},{8,0},{12,4},{16,24},{20,28},{24,16},{28,20},{1,9},{5... | collective-permute-start | bytes 196616 | tf_op jit(solution)/shard_map/ppermute | solution.py:448
  14.8 2.9 %collective-permute-start.7 = (bf16[128,256]{1,0:T(8,128)(2,1)S(1)}, bf16[128,256]{1,0:T(8,128)(2,1)S(1)}, u32[]{:S(2)}, u32[]{:S(2)}) collective-permute-start(bf16[128,256]{1,0:T(8,128)(2,1)S(1)} %get-tuple-element.84), channel_id=1, source_target_pairs={{0,16},{4,20},{8,24},{12,28},{16,0},{20,4},{24,8},{28,12},{1,17},{... | collective-permute-start | bytes 196616 | tf_op jit(solution)/shard_map/ppermute | solution.py:448
  17.7 2.0 %collective-permute-start.8 = (bf16[128,256]{1,0:T(8,128)(2,1)S(1)}, bf16[128,256]{1,0:T(8,128)(2,1)S(1)}, u32[]{:S(2)}, u32[]{:S(2)}) collective-permute-start(bf16[128,256]{1,0:T(8,128)(2,1)S(1)} %get-tuple-element.85), channel_id=1, source_target_pairs={{0,24},{4,28},{8,16},{12,20},{16,8},{20,12},{24,0},{28,4},{1,25},{... | collective-permute-start | bytes 196616 | tf_op jit(solution)/shard_map/ppermute | solution.py:448
  19.7 0.5 %shard_map.164 = (bf16[128,256]{1,0:T(8,128)(2,1)S(1)}, bf16[2,128,256]{2,1,0:T(8,128)(2,1)S(1)}, bf16[4,128,256]{2,1,0:T(8,128)(2,1)S(1)}) custom-call(bf16[144,256]{1,0:T(8,128)(2,1)S(1)} %collective-permute-done.1.refs_0_.refs_4_, bf16[144,256]{1,0:T(8,128)(2,1)S(1)} %collective-permute-done.2.refs_1_.refs_5_, ...), custom_call_target="tpu_custom_call" | custom-call | flops 575000000 | tf_op jit(solution)/shard_map/pallas_call | solution.py:436
  20.2 1.7 %collective-permute-start.11 = (bf16[4,128,256]{2,1,0:T(8,128)(2,1)S(1)}, bf16[4,128,256]{2,1,0:T(8,128)(2,1)S(1)}, u32[]{:S(2)}, u32[]{:S(2)}) collective-permute-start(bf16[4,128,256]{2,1,0:T(8,128)(2,1)S(1)} %get-tuple-element.93), channel_id=1, source_target_pairs={{0,4},{4,0},{8,12},{12,8},{16,20},{20,16},{24,28},{28,24},{1,5},{5... | collective-permute-start | bytes 786440 | tf_op jit(solution)/shard_map/ppermute | solution.py:448
  21.9 1.0 %shard_map.165 = (f32[4,256]{1,0:T(4,128)S(1)}, f32[128,256]{1,0:T(8,128)S(1)}, f32[128,512]{1,0:T(8,128)S(1)}, bf16[128,512]{1,0:T(8,128)(2,1)S(1)}) custom-call(bf16[128,256]{1,0:T(8,128)(2,1)S(1)} %get-tuple-element.74.grad_x, bf16[2,128,256]{2,1,0:T(8,128)(2,1)S(1)} %get-tuple-element.75.grads, bf16[128,256]{1,0:T(8,128)(2,1)S(1)} %get-tuple-element.76.x, ...), custom_call_target="tpu_custom_call" | custom-call | flops 1150000000 | tf_op jit(solution)/shard_map/pallas_call | solution.py:436
  23.0 0.9 %collective-permute-done.8.refs_2_ = bf16[128,256]{1,0:T(8,128)(2,1)S(1)} collective-permute-done((bf16[128,256]{1,0:T(8,128)(2,1)S(1)}, bf16[128,256]{1,0:T(8,128)(2,1)S(1)}, u32[]{:S(2)}, u32[]{:S(2)}) %collective-permute-start.8) | collective-permute-done | bytes 65568 | tf_op jit(solution)/shard_map/ppermute | solution.py:448
  23.9 0.3 shard_map.167
  24.3 1.3 %collective-permute-done.9.refs_3_ = bf16[128,512]{1,0:T(8,128)(2,1)S(1)} collective-permute-done((bf16[128,512]{1,0:T(8,128)(2,1)S(1)}, bf16[128,512]{1,0:T(8,128)(2,1)S(1)}, u32[]{:S(2)}, u32[]{:S(2)}) %collective-permute-start.9) | collective-permute-done | bytes 131104 | tf_op jit(solution)/shard_map/ppermute | solution.py:448
  25.7 1.6 %collective-permute-start.10 = (bf16[128,768]{1,0:T(8,128)(2,1)S(1)}, bf16[128,768]{1,0:T(8,128)(2,1)S(1)}, u32[]{:S(2)}, u32[]{:S(2)}) collective-permute-start(bf16[128,768]{1,0:T(8,128)(2,1)S(1)} %get-tuple-element.92), channel_id=1, source_target_pairs={{0,2},{1,3},{2,0},{3,1},{4,6},{5,7},{6,4},{7,5},{8,10},{9,11},{10,... | collective-permute-start | bytes 589832 | tf_op jit(solution)/shard_map/ppermute | solution.py:448
  27.3 0.2 shard_map.169
  27.5 2.5 %collective-permute-start.12 = (bf16[128,256]{1,0:T(8,128)(2,1)S(1)}, bf16[128,256]{1,0:T(8,128)(2,1)S(1)}, u32[]{:S(2)}, u32[]{:S(2)}) collective-permute-start(bf16[128,256]{1,0:T(8,128)(2,1)S(1)} %get-tuple-element.94), channel_id=1, source_target_pairs={{0,24},{4,28},{8,16},{12,20},{16,8},{20,12},{24,0},{28,4},{1,25},{... | collective-permute-start | bytes 196616 | tf_op jit(solution)/shard_map/ppermute | solution.py:448
  30.0 1.9 %collective-permute-start.14 = (bf16[128,256]{1,0:T(8,128)(2,1)S(1)}, bf16[128,256]{1,0:T(8,128)(2,1)S(1)}, u32[]{:S(2)}, u32[]{:S(2)}) collective-permute-start(bf16[128,256]{1,0:T(8,128)(2,1)S(1)} %get-tuple-element.96), channel_id=1, source_target_pairs={{0,8},{4,12},{8,0},{12,4},{16,24},{20,28},{24,16},{28,20},{1,9},{5... | collective-permute-start | bytes 196616 | tf_op jit(solution)/shard_map/ppermute | solution.py:448
  31.9 1.3 %shard_map.171 = (f32[4,128]{1,0:T(4,128)}, f32[4,128]{1,0:T(4,128)}) custom-call(bf16[2,128,256]{2,1,0:T(8,128)(2,1)S(1)} %get-tuple-element.104.states, bf16[2,128,256]{2,1,0:T(8,128)(2,1)S(1)} %get-tuple-element.75.grads, bf16[128,256]{1,0:T(8,128)(2,1)S(1)} %get-tuple-element.64.refs_5_.refs_7_.gy, bf16[128,128]{1,0:T(8,128)(2,1)S(1)} %get-tuple-element.65.refs_6_.ca, ...), custom_call_target="tpu_custom_call" | custom-call | flops 1150000000 | tf_op jit(solution)/shard_map/pallas_call | solution.py:436
  33.3 0.8 %collective-permute-done.12.refs_0_ = bf16[128,256]{1,0:T(8,128)(2,1)S(1)} collective-permute-done((bf16[128,256]{1,0:T(8,128)(2,1)S(1)}, bf16[128,256]{1,0:T(8,128)(2,1)S(1)}, u32[]{:S(2)}, u32[]{:S(2)}) %collective-permute-start.12) | collective-permute-done | bytes 65568 | tf_op jit(solution)/shard_map/ppermute | solution.py:448
  34.0 2.1 %collective-permute-done.13.refs_1_ = bf16[128,256]{1,0:T(8,128)(2,1)S(1)} collective-permute-done((bf16[128,256]{1,0:T(8,128)(2,1)S(1)}, bf16[128,256]{1,0:T(8,128)(2,1)S(1)}, u32[]{:S(2)}, u32[]{:S(2)}) %collective-permute-start.13) | collective-permute-done | bytes 65568 | tf_op jit(solution)/shard_map/ppermute | solution.py:448
  36.1 0.8 %shard_map.170 = (bf16[128,256]{1,0:T(8,128)(2,1)}, f32[128,256]{1,0:T(8,128)}, f32[128,128]{1,0:T(8,128)}, f32[128,128]{1,0:T(8,128)}, f32[128,128]{1,0:T(8,128)}, /*index=5*/f32[128,128]{1,0:T(8,128)}) custom-call(f32[128,768]{1,0:T(8,128)S(1)} %get-tuple-element.91.refs_1_.own, bf16[128,768]{1,0:T(8,128)(2,1)S(1)} %collective-permute-done.10.other, ...), custom_call_target="tpu_custom_call" | custom-call | flops 920000000 | tf_op jit(solution)/shard_map/pallas_call | solution.py:436
  (17 shorter events, 0.5 us)
Async XLA Ops:
  1.9 6.7 %collective-permute-start = (bf16[272,256]{1,0:T(8,128)(2,1)S(1)}, bf16[272,256]{1,0:T(8,128)(2,1)S(1)}, u32[]{:S(2)}, u32[]{:S(2)}) collective-permute-start(bf16[272,256]{1,0:T(8,128)(2,1)S(1)} %get-tuple-element.58.refs_0_.refs_2_), channel_id=1, source_target_pairs={{0,4},{4,0},{8,12},{12,8},{16,20},{20,16},{24,28},{28,24},{1,5},{5... | collective-permute-start | bytes 417800 | tf_op jit(solution)/shard_map/ppermute | solution.py:448
  7.5 5.7 %collective-permute-start.5 = (bf16[256,256]{1,0:T(8,128)(2,1)S(1)}, bf16[256,256]{1,0:T(8,128)(2,1)S(1)}, u32[]{:S(2)}, u32[]{:S(2)}) collective-permute-start(bf16[256,256]{1,0:T(8,128)(2,1)S(1)} %get-tuple-element.82.refs_0_), channel_id=1, source_target_pairs={{0,4},{4,0},{8,12},{12,8},{16,20},{20,16},{24,28},{28,24},{1,5},{5... | collective-permute-start | bytes 393224 | tf_op jit(solution)/shard_map/ppermute | solution.py:448
  8.7 9.0 %collective-permute-start.1 = (bf16[144,256]{1,0:T(8,128)(2,1)S(1)}, bf16[144,256]{1,0:T(8,128)(2,1)S(1)}, u32[]{:S(2)}, u32[]{:S(2)}) collective-permute-start(bf16[144,256]{1,0:T(8,128)(2,1)S(1)} %get-tuple-element.59), channel_id=1, source_target_pairs={{0,24},{4,28},{8,16},{12,20},{16,8},{20,12},{24,0},{28,4},{1,25},{... | collective-permute-start | bytes 221192 | tf_op jit(solution)/shard_map/ppermute | solution.py:448
  12.6 7.1 %collective-permute-start.2 = (bf16[144,256]{1,0:T(8,128)(2,1)S(1)}, bf16[144,256]{1,0:T(8,128)(2,1)S(1)}, u32[]{:S(2)}, u32[]{:S(2)}) collective-permute-start(bf16[144,256]{1,0:T(8,128)(2,1)S(1)} %get-tuple-element.60), channel_id=1, source_target_pairs={{0,16},{4,20},{8,24},{12,28},{16,0},{20,4},{24,8},{28,12},{1,17},{... | collective-permute-start | bytes 221192 | tf_op jit(solution)/shard_map/ppermute | solution.py:448
  12.6 7.1 %collective-permute-start.3 = (bf16[144,256]{1,0:T(8,128)(2,1)S(1)}, bf16[144,256]{1,0:T(8,128)(2,1)S(1)}, u32[]{:S(2)}, u32[]{:S(2)}) collective-permute-start(bf16[144,256]{1,0:T(8,128)(2,1)S(1)} %get-tuple-element.61), channel_id=1, source_target_pairs={{0,8},{4,12},{8,0},{12,4},{16,24},{20,28},{24,16},{28,20},{1,9},{5... | collective-permute-start | bytes 221192 | tf_op jit(solution)/shard_map/ppermute | solution.py:448
  13.4 9.6 %collective-permute-start.6 = (bf16[128,256]{1,0:T(8,128)(2,1)S(1)}, bf16[128,256]{1,0:T(8,128)(2,1)S(1)}, u32[]{:S(2)}, u32[]{:S(2)}) collective-permute-start(bf16[128,256]{1,0:T(8,128)(2,1)S(1)} %get-tuple-element.83), channel_id=1, source_target_pairs={{0,8},{4,12},{8,0},{12,4},{16,24},{20,28},{24,16},{28,20},{1,9},{5... | collective-permute-start | bytes 196616 | tf_op jit(solution)/shard_map/ppermute | solution.py:448
  14.8 8.2 %collective-permute-start.7 = (bf16[128,256]{1,0:T(8,128)(2,1)S(1)}, bf16[128,256]{1,0:T(8,128)(2,1)S(1)}, u32[]{:S(2)}, u32[]{:S(2)}) collective-permute-start(bf16[128,256]{1,0:T(8,128)(2,1)S(1)} %get-tuple-element.84), channel_id=1, source_target_pairs={{0,16},{4,20},{8,24},{12,28},{16,0},{20,4},{24,8},{28,12},{1,17},{... | collective-permute-start | bytes 196616 | tf_op jit(solution)/shard_map/ppermute | solution.py:448
  17.7 6.2 %collective-permute-start.8 = (bf16[128,256]{1,0:T(8,128)(2,1)S(1)}, bf16[128,256]{1,0:T(8,128)(2,1)S(1)}, u32[]{:S(2)}, u32[]{:S(2)}) collective-permute-start(bf16[128,256]{1,0:T(8,128)(2,1)S(1)} %get-tuple-element.85), channel_id=1, source_target_pairs={{0,24},{4,28},{8,16},{12,20},{16,8},{20,12},{24,0},{28,4},{1,25},{... | collective-permute-start | bytes 196616 | tf_op jit(solution)/shard_map/ppermute | solution.py:448
  20.2 7.0 %collective-permute-start.11 = (bf16[4,128,256]{2,1,0:T(8,128)(2,1)S(1)}, bf16[4,128,256]{2,1,0:T(8,128)(2,1)S(1)}, u32[]{:S(2)}, u32[]{:S(2)}) collective-permute-start(bf16[4,128,256]{2,1,0:T(8,128)(2,1)S(1)} %get-tuple-element.93), channel_id=1, source_target_pairs={{0,4},{4,0},{8,12},{12,8},{16,20},{20,16},{24,28},{28,24},{1,5},{5... | collective-permute-start | bytes 786440 | tf_op jit(solution)/shard_map/ppermute | solution.py:448
  22.9 1.4 %collective-permute-start.4 = (bf16[128,512]{1,0:T(8,128)(2,1)S(1)}, bf16[128,512]{1,0:T(8,128)(2,1)S(1)}, u32[]{:S(2)}, u32[]{:S(2)}) collective-permute-start(bf16[128,512]{1,0:T(8,128)(2,1)S(1)} %get-tuple-element.81), channel_id=1, source_target_pairs={{0,1},{1,0},{2,3},{3,2},{4,5},{5,4},{6,7},{7,6},{8,9},{9,8},{10,11... | collective-permute-start | bytes 393224 | tf_op jit(solution)/shard_map/ppermute | solution.py:448
  24.2 1.4 %collective-permute-start.9 = (bf16[128,512]{1,0:T(8,128)(2,1)S(1)}, bf16[128,512]{1,0:T(8,128)(2,1)S(1)}, u32[]{:S(2)}, u32[]{:S(2)}) collective-permute-start(bf16[128,512]{1,0:T(8,128)(2,1)S(1)} %get-tuple-element.90), channel_id=1, source_target_pairs={{0,1},{1,0},{2,3},{3,2},{4,5},{5,4},{6,7},{7,6},{8,9},{9,8},{10,11... | collective-permute-start | bytes 393224 | tf_op jit(solution)/shard_map/ppermute | solution.py:448
  25.7 7.6 %collective-permute-start.10 = (bf16[128,768]{1,0:T(8,128)(2,1)S(1)}, bf16[128,768]{1,0:T(8,128)(2,1)S(1)}, u32[]{:S(2)}, u32[]{:S(2)}) collective-permute-start(bf16[128,768]{1,0:T(8,128)(2,1)S(1)} %get-tuple-element.92), channel_id=1, source_target_pairs={{0,2},{1,3},{2,0},{3,1},{4,6},{5,7},{6,4},{7,5},{8,10},{9,11},{10,... | collective-permute-start | bytes 589832 | tf_op jit(solution)/shard_map/ppermute | solution.py:448
  27.5 6.6 %collective-permute-start.12 = (bf16[128,256]{1,0:T(8,128)(2,1)S(1)}, bf16[128,256]{1,0:T(8,128)(2,1)S(1)}, u32[]{:S(2)}, u32[]{:S(2)}) collective-permute-start(bf16[128,256]{1,0:T(8,128)(2,1)S(1)} %get-tuple-element.94), channel_id=1, source_target_pairs={{0,24},{4,28},{8,16},{12,20},{16,8},{20,12},{24,0},{28,4},{1,25},{... | collective-permute-start | bytes 196616 | tf_op jit(solution)/shard_map/ppermute | solution.py:448
  30.0 6.1 %collective-permute-start.13 = (bf16[128,256]{1,0:T(8,128)(2,1)S(1)}, bf16[128,256]{1,0:T(8,128)(2,1)S(1)}, u32[]{:S(2)}, u32[]{:S(2)}) collective-permute-start(bf16[128,256]{1,0:T(8,128)(2,1)S(1)} %get-tuple-element.95), channel_id=1, source_target_pairs={{0,16},{4,20},{8,24},{12,28},{16,0},{20,4},{24,8},{28,12},{1,17},{... | collective-permute-start | bytes 196616 | tf_op jit(solution)/shard_map/ppermute | solution.py:448
  30.0 6.1 %collective-permute-start.14 = (bf16[128,256]{1,0:T(8,128)(2,1)S(1)}, bf16[128,256]{1,0:T(8,128)(2,1)S(1)}, u32[]{:S(2)}, u32[]{:S(2)}) collective-permute-start(bf16[128,256]{1,0:T(8,128)(2,1)S(1)} %get-tuple-element.96), channel_id=1, source_target_pairs={{0,8},{4,12},{8,0},{12,4},{16,24},{20,28},{24,16},{28,20},{1,9},{5... | collective-permute-start | bytes 196616 | tf_op jit(solution)/shard_map/ppermute | solution.py:448
